TPU v7x, 32 devices: a whole 2x2x4 slice. The times are simulated.
32 devices in a mesh: groups: 2 (over y), seq: 16 (over z, x, core).
Axes of the slice: x: 2, y: 2, z: 4, core: 2. Of those that a mesh axis runs over, the one named last changes fastest.
Arguments:
- hidden_in: bfloat16 [2, 2048, 2048], P('groups', 'seq'), parts along dimension 0, may hold values from -6 to 6
- qkv: bfloat16 [2, 16, 2048, 384], P('groups', None, 'seq'), parts along dimension 0, may hold values from -6 to 6
- modulation: float32 [2, 4, 2048], P('groups'), parts along dimension 0, may hold values from -3 to 3
- route_weight: float32 [2, 2048, 2], P('groups', 'seq'), parts along dimension 0, may hold values from 0.2 to 1
- expert_ids: int32 [2, 2048, 2], P('groups', 'seq'), parts along dimension 0, may hold values from 0 to 15, as said below
- slots: int32 [2, 2048, 2], P('groups', 'seq'), parts along dimension 0, may hold values from 0 to 8, as said below
- w_in: bfloat16 [2048, 131072], P(None, 'seq'), may hold values from -0.125 to 0.125
- w_out: bfloat16 [131072, 2048], P('seq'), may hold values from -0.0625 to 0.0625
Outputs:
- block_out: bfloat16 [2, 2048, 2048], P('groups', 'seq'), parts along dimension 0
There are 2 independent parts, one for each index of `groups`. A program takes and returns all parts, laid end to end along the dimension named above; an argument that names none is the same for every part. Nothing has to cross between parts.
Inputs may be any that keep to these rules, and one draw needn't show every extreme that they name: `expert_ids`: the two experts of a token differ. Within the rows of one device, the kept choices of each expert hold distinct slots 0, 1, ... upward, assigned in the device's priority order with all first choices before second choices; 8 marks a dropped choice.
All inputs are finite; a program needn't handle non-finite values.
Results may differ from a plain program's by a relative error of at most 0.0047.
Values may be sent and summed in bfloat16 or wider, within the bound.
No kernel may reach another device: no remote copies, remote signals or barrier semaphores. Data moves between devices by JAX's collectives and lax.ppermute only.
A program may use at most 192 MiB of HBM per device.

v0:
```python
import math

import jax
import jax.numpy as jnp
from jax import lax
from jax.sharding import PartitionSpec as P

EXPERTS = 16
CAP = 8
FRAMES = 16


def attend(queries, key_rows, values):
    length, width = queries.shape
    block_rows = math.gcd(length, 512)
    stacked = queries.reshape(length // block_rows, block_rows, width)

    def scores_for(query_block):
        scores = jnp.dot(query_block, key_rows.T, preferred_element_type=jnp.float32) * width ** (
            -0.5
        )
        scores = scores - jnp.max(scores, axis=-1, keepdims=True)
        exponent = jnp.exp(scores)
        weights = (exponent / jnp.sum(exponent, axis=-1, keepdims=True)).astype(jnp.bfloat16)
        return jnp.dot(weights, values, preferred_element_type=jnp.float32).astype(jnp.bfloat16)

    return lax.map(scores_for, stacked).reshape(length, width)


def normalize(resid):
    center = jnp.mean(resid, axis=-1, keepdims=True)
    shifted = resid - center
    spread = jnp.mean(shifted * shifted, axis=-1, keepdims=True)
    return shifted * lax.rsqrt(spread + 1e-06)


def body(hidden_in, qkv, modulation, route_weight, expert_ids, slots, w_in, w_out):
    seq_count, head_count, row_count, triple = qkv.shape
    head_width = triple // 3
    width = head_count * head_width
    devices_seq = lax.axis_size("seq")
    frame_parts = devices_seq // (seq_count * head_count)
    local_frames = FRAMES // frame_parts
    places = row_count // FRAMES
    arranged = qkv.reshape(seq_count, head_count, places, frame_parts, local_frames, triple)
    arranged = arranged.transpose(0, 1, 3, 2, 4, 5).reshape(
        devices_seq, places, local_frames, triple
    )
    owned = lax.all_to_all(arranged, "seq", split_axis=0, concat_axis=1, tiled=True)[0]
    by_frame = owned.transpose(1, 0, 2)
    attended = lax.map(
        lambda one_frame: attend(
            one_frame[:, :head_width],
            one_frame[:, head_width : 2 * head_width],
            one_frame[:, 2 * head_width :],
        ),
        by_frame,
    )
    outgoing = attended.transpose(1, 0, 2).reshape(devices_seq, places, local_frames, head_width)
    returned = lax.all_to_all(outgoing, "seq", split_axis=0, concat_axis=0, tiled=True)
    mixed = returned.reshape(seq_count, head_count, frame_parts, places, local_frames, head_width)
    mixed = mixed.transpose(0, 3, 2, 4, 1, 5).reshape(seq_count, row_count, width)
    resid = hidden_in.astype(jnp.float32) + modulation[:, 0][:, None, :] * mixed.astype(jnp.float32)
    normed = (
        normalize(resid) * (1.0 + modulation[:, 2][:, None, :]) + modulation[:, 1][:, None, :]
    ).astype(jnp.bfloat16)
    token_rows = normed.reshape(seq_count * row_count, width)
    choice_count = expert_ids.shape[-1]
    chosen = expert_ids.reshape(-1, choice_count)
    slot_assignment = slots.reshape(-1, choice_count)
    weight = route_weight.reshape(-1, choice_count)
    code = jnp.where(slot_assignment < CAP, chosen * CAP + slot_assignment, -1)
    column = jnp.arange(EXPERTS * CAP, dtype=jnp.int32)
    hits = code[:, :, None] == column
    selected_expert = jnp.sum(hits, axis=1).astype(jnp.bfloat16)
    expert_blending = jnp.sum(jnp.where(hits, weight[:, :, None], 0.0), axis=1)
    gathered = jnp.einsum(
        "tk,td->kd", selected_expert, token_rows, preferred_element_type=jnp.float32
    ).astype(jnp.bfloat16)
    shards = devices_seq // EXPERTS
    spread_rows = jnp.broadcast_to(
        gathered.reshape(EXPERTS, 1, CAP, width), (EXPERTS, shards, CAP, width)
    ).reshape(devices_seq, CAP, width)
    arrived = lax.all_to_all(spread_rows, "seq", split_axis=0, concat_axis=0, tiled=True)
    flat = arrived.reshape(-1, width)
    inner = jax.nn.gelu(
        jnp.dot(flat, w_in, preferred_element_type=jnp.float32), approximate=True
    ).astype(jnp.bfloat16)
    computed = (
        jnp.dot(inner, w_out, preferred_element_type=jnp.float32)
        .astype(jnp.bfloat16)
        .reshape(arrived.shape)
    )
    brought = lax.all_to_all(computed, "seq", split_axis=0, concat_axis=0, tiled=True)
    combined_outputs = jnp.sum(
        brought.astype(jnp.float32).reshape(EXPERTS, shards, CAP, width), axis=1
    ).reshape(EXPERTS * CAP, width)
    expert_mixture_layer = jnp.dot(
        expert_blending,
        combined_outputs,
        precision=lax.Precision.HIGHEST,
        preferred_element_type=jnp.float32,
    )
    final = resid + modulation[:, 3][:, None, :] * expert_mixture_layer.reshape(
        seq_count, row_count, width
    )
    return final.astype(jnp.bfloat16)


def solution(mesh):
    in_specs = (
        P("groups", "seq", None),
        P("groups", None, "seq", None),
        P("groups", None, None),
        P("groups", "seq", None),
        P("groups", "seq", None),
        P("groups", "seq", None),
        P(None, "seq"),
        P("seq", None),
    )
    out_specs = P("groups", "seq", None)
    return jax.shard_map(body, mesh=mesh, in_specs=in_specs, out_specs=out_specs, check_vma=False)
```

profile of v0, /device:TPU:0, one launch (start us, length us, event | category | flops | bytes accessed | tf_op | source)
XLA Modules:
  0.0 140.4 jit_solution(15151597030639884631)
XLA Ops:
  0.0 3.0 %copy.24 = bf16[16,8,16,384]{3,1,2,0:T(8,128)(2,1)} copy(bf16[16,8,16,384]{3,2,1,0:T(8,128)(2,1)} %bitcast.59) | data formatting | bytes 3145728 | tf_op jit(solution)/shard_map/reshape;transpose;reshape | solution.py:46
  3.0 7.4 %all-to-all-start = ((bf16[16,8,16,384]{3,1,2,0:T(8,128)(2,1)}), bf16[16,8,16,384]{3,1,2,0:T(8,128)(2,1)S(1)}, u32[]{:S(2)}, u32[]{:S(2)}) async-start(bf16[16,8,16,384]{3,1,2,0:T(8,128)(2,1)} %copy.24), calls=%async_computation | async-start | bytes 3145728 | tf_op jit(solution)/shard_map/all_to_all | solution.py:49
  10.3 32.0 %all-to-all-done = bf16[16,8,16,384]{3,1,2,0:T(8,128)(2,1)S(1)} async-done(((bf16[16,8,16,384]{3,1,2,0:T(8,128)(2,1)}), bf16[16,8,16,384]{3,1,2,0:T(8,128)(2,1)S(1)}, u32[]{:S(2)}, u32[]{:S(2)}) %all-to-all-start) | async-done | bytes 1572896 | tf_op jit(solution)/shard_map/all_to_all | solution.py:49
  42.3 0.3 copy.25
  42.6 0.4 copy.26
  43.0 7.5 %while.10 = (s32[]{:T(128)}, bf16[16,128,128]{2,1,0:T(8,128)(2,1)S(1)}, bf16[16,128,384]{2,1,0:T(8,128)(2,1)S(1)}, s32[]{:T(128)}) while((s32[]{:T(128)}, bf16[16,128,128]{2,1,0:T(8,128)(2,1)S(1)}, bf16[16,128,384]{2,1,0:T(8,128)(2,1)S(1)}, s32[]{:T(128)}) %tuple.28), condition=%wide.region_3.0_spmd, body=%wide.region_0.3_spmd.sunk | while | flops 8519426 | bytes 526909 | solution.py:51
  43.3 0.2 fusion.58
  44.2 0.2 fusion.58
  44.7 0.2 fusion.58
  45.6 0.2 fusion.58
  46.1 0.2 fusion.58
  46.6 0.2 fusion.58
  50.6 1.1 copy.27
  51.7 9.1 %all-to-all-start.1 = ((bf16[16,8,16,128]{3,2,1,0:T(8,128)(2,1)}), bf16[16,8,16,128]{3,2,1,0:T(8,128)(2,1)S(1)}, u32[]{:S(2)}, u32[]{:S(2)}) async-start(bf16[16,8,16,128]{3,2,1,0:T(8,128)(2,1)} %bitcast.7), calls=%async_computation.1 | async-start | bytes 1048576 | tf_op jit(solution)/shard_map/all_to_all | solution.py:60
  61.0 14.3 %all-to-all-done.1 = bf16[16,8,16,128]{3,2,1,0:T(8,128)(2,1)S(1)} async-done(((bf16[16,8,16,128]{3,2,1,0:T(8,128)(2,1)}), bf16[16,8,16,128]{3,2,1,0:T(8,128)(2,1)S(1)}, u32[]{:S(2)}, u32[]{:S(2)}) %all-to-all-start.1) | async-done | bytes 524320 | tf_op jit(solution)/shard_map/all_to_all | solution.py:60
  75.4 0.6 copy.28
  76.2 0.2 fusion.45
  76.4 0.3 multiply_reduce_fusion
  76.7 0.5 fusion.19
  77.2 18.4 %all_to_all.24 = bf16[16,8,2048]{2,1,0:T(8,128)(2,1)S(1)} all-to-all(bf16[16,8,2048]{2,1,0:T(8,128)(2,1)S(1)} %fusion.19), channel_id=1, replica_groups=mesh['groups'=2,'seq'=16] {'seq'}, dimensions={0} | all-to-all | bytes 1048576 | tf_op jit(solution)/shard_map/all_to_all | solution.py:84
  95.6 24.8 %fusion.20 = bf16[16,8,2048]{2,1,0:T(8,128)(2,1)} fusion(bf16[8192,2048]{1,0:T(8,128)(2,1)} %param.17, bf16[2048,8192]{1,0:T(8,128)(2,1)} %param.16, bf16[16,8,2048]{2,1,0:T(8,128)(2,1)S(1)} %all_to_all.24), kind=kOutput, calls=%fused_computation.29 | convolution fusion | flops 8599633920 | bytes 68157440 | tf_op jit(solution)/shard_map/dot_general | solution.py:90
  120.4 4.1 %all-to-all-start.3 = ((bf16[16,8,2048]{2,1,0:T(8,128)(2,1)}), bf16[16,8,2048]{2,1,0:T(8,128)(2,1)S(1)}, u32[]{:S(2)}, u32[]{:S(2)}) async-start(bf16[16,8,2048]{2,1,0:T(8,128)(2,1)} %fusion.20), calls=%async_computation.3 | async-start | bytes 1048576 | tf_op jit(solution)/shard_map/all_to_all | solution.py:94
  124.7 14.3 %all-to-all-done.3 = bf16[16,8,2048]{2,1,0:T(8,128)(2,1)S(1)} async-done(((bf16[16,8,2048]{2,1,0:T(8,128)(2,1)}), bf16[16,8,2048]{2,1,0:T(8,128)(2,1)S(1)}, u32[]{:S(2)}, u32[]{:S(2)}) %all-to-all-start.3) | async-done | bytes 524320 | tf_op jit(solution)/shard_map/all_to_all | solution.py:94
  139.0 1.5 %fusion.18 = bf16[1,128,2048]{2,1,0:T(8,128)(2,1)} fusion(f32[128,128]{1,0:T(8,128)S(1)} %select_reduce_fusion, bf16[16,8,2048]{2,1,0:T(8,128)(2,1)S(1)} %all-to-all-done.3, f32[2048]{0:T(1024)S(1)} %bitcast.65, f32[1,128,2048]{2,1,0:T(8,128)S(1)} %reshape.137, f32[2048]{0:T(1024)S(1)} %bitcast.64, bf16[1,128,2048]{2,1,0:T(8,128)(2,1)S(1)} %copy-done), kind=kOutput, calls=%fused_computation.25 | convolution fusion | flops 404226048 | bytes 2703360 | tf_op jit(solution)/shard_map/dot_general | solution.py:98
  (77 shorter events, 6.4 us)
Async XLA Ops:
  3.0 39.3 %all-to-all-start = ((bf16[16,8,16,384]{3,1,2,0:T(8,128)(2,1)}), bf16[16,8,16,384]{3,1,2,0:T(8,128)(2,1)S(1)}, u32[]{:S(2)}, u32[]{:S(2)}) async-start(bf16[16,8,16,384]{3,1,2,0:T(8,128)(2,1)} %copy.24), calls=%async_computation | async-start | bytes 3145728 | tf_op jit(solution)/shard_map/all_to_all | solution.py:49
  42.6 18.2 %copy-start.3 = (s32[1,128,2]{1,2,0:T(2,128)S(1)}, s32[1,128,2]{1,2,0:T(2,128)}, u32[]{:S(2)}) copy-start(s32[1,128,2]{1,2,0:T(2,128)} %param.15) | copy-start | bytes 3076
  42.6 18.2 %copy-start.4 = (s32[1,128,2]{1,2,0:T(2,128)S(1)}, s32[1,128,2]{1,2,0:T(2,128)}, u32[]{:S(2)}) copy-start(s32[1,128,2]{1,2,0:T(2,128)} %param.14) | copy-start | bytes 3076
  42.6 18.3 %copy-start.1 = (f32[1,4,2048]{2,1,0:T(4,128)S(1)}, f32[1,4,2048]{2,1,0:T(4,128)}, u32[]{:S(2)}) copy-start(f32[1,4,2048]{2,1,0:T(4,128)} %param.12) | copy-start | bytes 98308
  50.6 25.6 %copy-start = (bf16[1,128,2048]{2,1,0:T(8,128)(2,1)S(1)}, bf16[1,128,2048]{2,1,0:T(8,128)(2,1)}, u32[]{:S(2)}) copy-start(bf16[1,128,2048]{2,1,0:T(8,128)(2,1)} %param.10) | copy-start | bytes 1572868
  51.7 23.6 %all-to-all-start.1 = ((bf16[16,8,16,128]{3,2,1,0:T(8,128)(2,1)}), bf16[16,8,16,128]{3,2,1,0:T(8,128)(2,1)S(1)}, u32[]{:S(2)}, u32[]{:S(2)}) async-start(bf16[16,8,16,128]{3,2,1,0:T(8,128)(2,1)} %bitcast.7), calls=%async_computation.1 | async-start | bytes 1048576 | tf_op jit(solution)/shard_map/all_to_all | solution.py:60
  95.6 28.9 %copy-start.2 = (f32[1,128,2]{1,2,0:T(2,128)S(1)}, f32[1,128,2]{1,2,0:T(2,128)}, u32[]{:S(2)}) copy-start(f32[1,128,2]{1,2,0:T(2,128)} %param.13) | copy-start | bytes 3076
  120.4 18.6 %all-to-all-start.3 = ((bf16[16,8,2048]{2,1,0:T(8,128)(2,1)}), bf16[16,8,2048]{2,1,0:T(8,128)(2,1)S(1)}, u32[]{:S(2)}, u32[]{:S(2)}) async-start(bf16[16,8,2048]{2,1,0:T(8,128)(2,1)} %fusion.20), calls=%async_computation.3 | async-start | bytes 1048576 | tf_op jit(solution)/shard_map/all_to_all | solution.py:94
where the time goes:
time: 141 us; the launch traced here: 140 us
  waiting for transfers between devices  60.6 us (43%)
  matrix products  32.8 us (23%)
  starting transfers between devices  20.5 us (15%)
  blocking collectives  18.4 us (13%)
  local copies, waits for them, and re-layouts  5.83 us (4%)
  other arithmetic  1.64 us (1%)
    all_to_all x1, waiting for transfers between devices, body(): lax.all_to_all(arranged, 'seq', split_axis=0, concat_axis=1, tiled=True)[0]  32 us
    dot_general x1, matrix products, body(): jnp.dot(inner, w_out, preferred_element_type=jnp.float32)  24.8 us
    all_to_all x1, blocking collectives, body(): lax.all_to_all(spread_rows, 'seq', split_axis=0, concat_axis=0, tiled=True)  18.4 us
    all_to_all x1, waiting for transfers between devices, body(): lax.all_to_all(computed, 'seq', split_axis=0, concat_axis=0, tiled=True)  14.3 us
    all_to_all x1, waiting for transfers between devices, body(): lax.all_to_all(outgoing, 'seq', split_axis=0, concat_axis=0, tiled=True)  14.3 us
    all_to_all x1, starting transfers between devices, body(): lax.all_to_all(outgoing, 'seq', split_axis=0, concat_axis=0, tiled=True)  9.11 us
    all_to_all x1, starting transfers between devices, body(): lax.all_to_all(arranged, 'seq', split_axis=0, concat_axis=1, tiled=True)[0]  7.36 us
    all_to_all x1, starting transfers between devices, body(): lax.all_to_all(computed, 'seq', split_axis=0, concat_axis=0, tiled=True)  4.08 us
  transfers between devices with their start and end apart: 3, of which 3 were waited for; matrix products, arithmetic and copies ran while one was open for 0% of the time, Pallas kernels for 0%

commit v1 on v0

v1 whole, which is shorter than its diff:
```python
import functools

import jax
import jax.numpy as jnp
import numpy as np
from jax import lax
from jax.experimental import pallas as pl
from jax.experimental.pallas import tpu as pltpu
from jax.sharding import PartitionSpec as P

EXPERTS = 16
CAP = 8
FRAMES = 16
MIB = 2**20

VMEM = pl.BlockSpec(memory_space=pltpu.VMEM)
ANY = pl.BlockSpec(memory_space=pl.ANY)


def frame_order(chunk, places, local_frames):
    index = np.arange(chunk).reshape(-1, places, local_frames).transpose(2, 0, 1).reshape(chunk)
    return (index[:, None] == np.arange(chunk)[None, :]).astype(np.float32)


def attention_kernel(local_frames, chunk, order_ref, back_ref, rows_ref, out_ref, framed, attended):
    total, triple = rows_ref.shape
    width = triple // 3
    length = total // local_frames
    piece = chunk // local_frames
    order = order_ref[...]
    back = back_ref[...]
    for c in range(total // chunk):
        rows = jnp.dot(order, rows_ref[c * chunk : (c + 1) * chunk], preferred_element_type=jnp.float32)
        framed[:, c * piece : (c + 1) * piece, :] = rows.astype(jnp.bfloat16).reshape(
            local_frames, piece, triple
        )
    block = min(length, 256)
    for f in range(local_frames):
        keys = framed[f, :, width : 2 * width]
        values = framed[f, :, 2 * width :]
        for b in range(length // block):
            queries = framed[f, b * block : (b + 1) * block, :width]
            scores = lax.dot_general(
                queries, keys, (((1,), (1,)), ((), ())), preferred_element_type=jnp.float32
            ) * width ** (-0.5)
            exponent = jnp.exp(scores - jnp.max(scores, axis=-1, keepdims=True))
            weights = (exponent / jnp.sum(exponent, axis=-1, keepdims=True)).astype(jnp.bfloat16)
            attended[f, b * block : (b + 1) * block, :] = jnp.dot(
                weights, values, preferred_element_type=jnp.float32
            ).astype(jnp.bfloat16)
    for c in range(total // chunk):
        rows = attended[:, c * piece : (c + 1) * piece, :].reshape(chunk, width)
        out_ref[c * chunk : (c + 1) * chunk, :] = jnp.dot(
            back, rows, preferred_element_type=jnp.float32
        ).astype(jnp.bfloat16)


def attention(rows, places, local_frames):
    total, triple = rows.shape
    width = triple // 3
    chunk = min(total, 256)
    order = frame_order(chunk, places, local_frames)
    return pl.pallas_call(
        functools.partial(attention_kernel, local_frames, chunk),
        out_shape=jax.ShapeDtypeStruct((total, width), jnp.bfloat16),
        in_specs=[VMEM] * 3,
        out_specs=VMEM,
        scratch_shapes=[
            pltpu.VMEM((local_frames, total // local_frames, triple), jnp.bfloat16),
            pltpu.VMEM((local_frames, total // local_frames, width), jnp.bfloat16),
        ],
        compiler_params=pltpu.CompilerParams(vmem_limit_bytes=24 * MIB),
    )(jnp.asarray(order, jnp.bfloat16), jnp.asarray(order.T, jnp.bfloat16), rows)


def residual(hidden_ref, mixed_ref, modulation_ref):
    heads, _, width = mixed_ref.shape
    parts = []
    for h in range(heads):
        columns = slice(h * width, (h + 1) * width)
        parts.append(
            hidden_ref[:, columns].astype(jnp.float32)
            + modulation_ref[0:1, columns] * mixed_ref[h].astype(jnp.float32)
        )
    return jnp.concatenate(parts, axis=1)


def slot_code(ids_ref, slots_ref):
    return jnp.where(slots_ref[...] < CAP, ids_ref[...] * CAP + slots_ref[...], -1)


def dispatch_kernel(hidden_ref, mixed_ref, modulation_ref, ids_ref, slots_ref, out_ref):
    resid = residual(hidden_ref, mixed_ref, modulation_ref)
    shifted = resid - jnp.mean(resid, axis=-1, keepdims=True)
    spread = jnp.mean(shifted * shifted, axis=-1, keepdims=True)
    normed = (
        shifted * lax.rsqrt(spread + 1e-06) * (1.0 + modulation_ref[2:3, :]) + modulation_ref[1:2, :]
    ).astype(jnp.bfloat16)
    code = slot_code(ids_ref, slots_ref)
    row = lax.broadcasted_iota(jnp.int32, (EXPERTS * CAP, code.shape[1]), 0)
    chosen = jnp.zeros(row.shape, jnp.float32)
    for i in range(code.shape[0]):
        chosen = chosen + jnp.where(code[i : i + 1, :] == row, 1.0, 0.0)
    out_ref[...] = jnp.dot(
        chosen.astype(jnp.bfloat16), normed, preferred_element_type=jnp.float32
    ).astype(jnp.bfloat16)


def dispatch(hidden, mixed, modulation, ids, slots):
    return pl.pallas_call(
        dispatch_kernel,
        out_shape=jax.ShapeDtypeStruct((EXPERTS * CAP, hidden.shape[1]), jnp.bfloat16),
        in_specs=[VMEM] * 5,
        out_specs=VMEM,
        compiler_params=pltpu.CompilerParams(vmem_limit_bytes=24 * MIB),
    )(hidden, mixed, modulation, ids, slots)


def expert_kernel(blocks, depth, rows_ref, first_ref, second_hbm, out_ref, total, held, arrived):
    step_width = first_ref.shape[1] // blocks

    def fetch(block, place):
        return pltpu.make_async_copy(
            second_hbm.at[pl.ds(pl.multiple_of(block * step_width, step_width), step_width)],
            held.at[place],
            arrived.at[place],
        )

    for place in range(min(depth, blocks)):
        fetch(place, place).start()
    total[...] = jnp.zeros_like(total)

    def step(block, _):
        place = lax.rem(block, depth)
        columns = pl.ds(pl.multiple_of(block * step_width, step_width), step_width)
        inner = jnp.dot(rows_ref[...], first_ref[:, columns], preferred_element_type=jnp.float32)
        inner = jax.nn.gelu(inner, approximate=True).astype(jnp.bfloat16)
        fetch(block, place).wait()
        total[...] += jnp.dot(inner, held[place], preferred_element_type=jnp.float32)

        @pl.when(block + depth < blocks)
        def _():
            fetch(block + depth, place).start()

        return 0

    lax.fori_loop(0, blocks, step, 0)
    out_ref[...] = total[...].astype(jnp.bfloat16)


def expert(rows, first, second):
    count, width = rows.shape
    hidden = first.shape[1]
    step_width = min(hidden, 1024)
    blocks = hidden // step_width
    depth = min(blocks, 3)
    return pl.pallas_call(
        functools.partial(expert_kernel, blocks, depth),
        out_shape=jax.ShapeDtypeStruct((count, width), jnp.bfloat16),
        in_specs=[VMEM, VMEM, ANY],
        out_specs=VMEM,
        scratch_shapes=[
            pltpu.VMEM((count, width), jnp.float32),
            pltpu.VMEM((depth, step_width, width), jnp.bfloat16),
            pltpu.SemaphoreType.DMA((depth,)),
        ],
        compiler_params=pltpu.CompilerParams(vmem_limit_bytes=26 * MIB),
        cost_estimate=pl.CostEstimate(
            flops=4 * count * width * hidden, bytes_accessed=2 * width * hidden, transcendentals=count * hidden
        ),
    )(rows, pltpu.with_memory_space_constraint(first, pltpu.VMEM), second)


def combine_kernel(shards, hidden_ref, mixed_ref, modulation_ref, ids_ref, slots_ref, gate_ref, back_ref, out_ref):
    resid = residual(hidden_ref, mixed_ref, modulation_ref)
    code = slot_code(ids_ref, slots_ref)
    count = code.shape[1]
    row = lax.broadcasted_iota(jnp.int32, (EXPERTS * CAP * shards, count), 0)
    slot = row // (CAP * shards) * CAP + row % CAP
    blending = jnp.zeros(row.shape, jnp.float32)
    for i in range(code.shape[0]):
        blending = blending + jnp.where(code[i : i + 1, :] == slot, gate_ref[i : i + 1, :], 0.0)
    blending = blending.T
    parts = []
    for _ in range(3):
        part = blending.astype(jnp.bfloat16)
        parts.append(part)
        blending = blending - part.astype(jnp.float32)
    mixture = jnp.dot(jnp.concatenate(parts, axis=0), back_ref[...], preferred_element_type=jnp.float32)
    mixture = mixture[:count] + (mixture[count : 2 * count] + mixture[2 * count :])
    out_ref[...] = (resid + modulation_ref[3:4, :] * mixture).astype(jnp.bfloat16)


def combine(shards, hidden, mixed, modulation, ids, slots, gate, back):
    return pl.pallas_call(
        functools.partial(combine_kernel, shards),
        out_shape=jax.ShapeDtypeStruct(hidden.shape, jnp.bfloat16),
        in_specs=[VMEM] * 7,
        out_specs=VMEM,
        compiler_params=pltpu.CompilerParams(vmem_limit_bytes=24 * MIB),
    )(hidden, mixed, modulation, ids, slots, gate, back)


def body(hidden_in, qkv, modulation, route_weight, expert_ids, slots, w_in, w_out):
    seq_count, head_count, row_count, triple = qkv.shape
    assert seq_count == 1
    head_width = triple // 3
    width = head_count * head_width
    devices = lax.axis_size("seq")
    frame_parts = devices // head_count
    local_frames = FRAMES // frame_parts
    places = row_count // FRAMES
    shards = devices // EXPERTS
    outgoing = qkv.reshape(head_count, places, frame_parts, local_frames, triple)
    outgoing = outgoing.transpose(0, 2, 1, 3, 4).reshape(devices, places * local_frames, triple)
    owned = lax.all_to_all(outgoing, "seq", split_axis=0, concat_axis=0, tiled=True)
    attended = attention(owned.reshape(-1, triple), places, local_frames)
    returned = lax.all_to_all(
        attended.reshape(devices, places * local_frames, head_width), "seq", split_axis=0, concat_axis=0, tiled=True
    )
    mixed = returned.reshape(head_count, frame_parts, places, local_frames, head_width)
    mixed = mixed.transpose(0, 2, 1, 3, 4).reshape(head_count, row_count, head_width)
    hidden = hidden_in[0]
    scales = modulation[0]
    ids = expert_ids[0].T
    slot_rows = slots[0].T
    gate = route_weight[0].T
    gathered = dispatch(hidden, mixed, scales, ids, slot_rows)
    spread_rows = jnp.broadcast_to(
        gathered.reshape(EXPERTS, 1, CAP, width), (EXPERTS, shards, CAP, width)
    ).reshape(devices, CAP, width)
    arrived = lax.all_to_all(spread_rows, "seq", split_axis=0, concat_axis=0, tiled=True)
    computed = expert(arrived.reshape(devices * CAP, width), w_in, w_out)
    brought = lax.all_to_all(
        computed.reshape(devices, CAP, width), "seq", split_axis=0, concat_axis=0, tiled=True
    )
    final = combine(shards, hidden, mixed, scales, ids, slot_rows, gate, brought.reshape(devices * CAP, width))
    return final[None]


def solution(mesh):
    in_specs = (
        P("groups", "seq", None),
        P("groups", None, "seq", None),
        P("groups", None, None),
        P("groups", "seq", None),
        P("groups", "seq", None),
        P("groups", "seq", None),
        P(None, "seq"),
        P("seq", None),
    )
    out_specs = P("groups", "seq", None)
    return jax.shard_map(body, mesh=mesh, in_specs=in_specs, out_specs=out_specs, check_vma=False)
```

time: 141 us -> 139 us (0.986)
  blocking collectives: 18.4 us -> 99.8 us
  waiting for transfers between devices: 60.6 us -> 0 us
  matrix products: 32.8 us -> 0 us
  Pallas kernels: 0 us -> 24.1 us
  starting transfers between devices: 20.5 us -> 0 us
  local copies, waits for them, and re-layouts: 5.83 us -> 14.6 us
  other arithmetic: 1.64 us -> 0 us
    all_to_all x0 -> x3, blocking collectives: none -> 81.3 us  [the longest x1 43.4 us: body(): lax.all_to_all(outgoing, 'seq', split_axis=0, concat_axis=0, tiled=True)]
    all_to_all x3 -> x0, waiting for transfers between devices: 60.6 us -> none  [the longest x1 32 us: body(): lax.all_to_all(arranged, 'seq', split_axis=0, concat_axis=1, tiled=True)[0]]
    dot_general x35 -> x0, matrix products: 32.8 us -> none  [the longest x1 24.8 us: body(): jnp.dot(inner, w_out, preferred_element_type=jnp.float32)]
    pallas_call x0 -> x4, Pallas kernels: none -> 24.1 us  [the longest x1 16 us: expert(): pl.pallas_call(functools.partial(expert_kernel, blocks, depth), out_shape...]
    all_to_all x3 -> x0, starting transfers between devices: 20.5 us -> none  [the longest x1 9.11 us: body(): lax.all_to_all(outgoing, 'seq', split_axis=0, concat_axis=0, tiled=True)]
    unnamed x10 -> x22, local copies, waits for them, and re-layouts: 0.03 us -> 14.6 us
    another operation x1 -> x0, local copies, waits for them, and re-layouts: 2.95 us -> none  [body(): arranged.transpose(0, 1, 3, 2, 4, 5)]
    reduce_sum x20 -> x0, other arithmetic: 1.49 us -> none  [the longest x16 0.74 us: scores_for(): jnp.sum(exponent, axis=-1, keepdims=True)]
  transfers between devices with their start and end apart: 3 -> 0, of which waited for: 3 -> 0; matrix products, arithmetic and copies ran while one was open for 0% -> 0% of each run, Pallas kernels for 0% -> 0%
where the time goes in v1:
time: 139 us
  blocking collectives  99.8 us (72%)
  Pallas kernels  24.1 us (17%)
  local copies, waits for them, and re-layouts  14.6 us (11%)
    all_to_all x1, blocking collectives, body(): lax.all_to_all(outgoing, 'seq', split_axis=0, concat_axis=0, tiled=True)  43.4 us
    all_to_all x1, blocking collectives, body(): lax.all_to_all(attended.reshape(devices, places * local_frames, head_widt...  19.3 us
    all_to_all x1, blocking collectives, body(): lax.all_to_all(computed.reshape(devices, CAP, width), 'seq', split_axis=0...  18.6 us
    all_to_all x1, blocking collectives, body(): lax.all_to_all(spread_rows, 'seq', split_axis=0, concat_axis=0, tiled=True)  18.5 us
    pallas_call x1, Pallas kernels, expert(): pl.pallas_call(functools.partial(expert_kernel, blocks, depth), out_shape...  16 us
    unnamed x22, local copies, waits for them, and re-layouts  14.6 us
    pallas_call x1, Pallas kernels, attention(): pl.pallas_call(functools.partial(attention_kernel, local_frames, chunk),...  6 us

profile of v1, /device:TPU:0, one launch (start us, length us, event | category | flops | bytes accessed | tf_op | source)
XLA Modules:
  0.0 138.5 jit_solution(8376528801869875769)
XLA Ops:
  0.0 43.4 %all_to_all.20 = bf16[16,128,384]{2,1,0:T(8,128)(2,1)S(1)} all-to-all(bf16[16,128,384]{2,1,0:T(8,128)(2,1)} %bitcast.34), channel_id=1, replica_groups=mesh['groups'=2,'seq'=16] {'seq'}, dimensions={0} | all-to-all | bytes 3145728 | tf_op jit(solution)/shard_map/all_to_all | solution.py:216
  43.4 0.0 copy-start.3
  43.4 0.9 copy-done.3
  44.3 6.0 %shard_map.100 = bf16[2048,128]{1,0:T(8,128)(2,1)S(1)} custom-call(bf16[256,256]{1,0:T(8,128)(2,1)S(1)} %copy-done.3, bf16[256,256]{1,0:T(8,128)(2,1)S(1)} %copy-done.3, bf16[2048,384]{1,0:T(8,128)(2,1)S(1)} %bitcast.19), custom_call_target="tpu_custom_call" | custom-call | tf_op jit(solution)/shard_map/pallas_call | solution.py:63
  50.4 19.3 %all_to_all.21.mixed_ref = bf16[16,128,128]{2,1,0:T(8,128)(2,1)S(1)} all-to-all(bf16[16,128,128]{2,1,0:T(8,128)(2,1)S(1)} %bitcast.24), channel_id=1, replica_groups=mesh['groups'=2,'seq'=16] {'seq'}, dimensions={0} | all-to-all | bytes 1048576 | tf_op jit(solution)/shard_map/all_to_all | solution.py:218
  69.7 0.0 copy-start.1
  69.7 1.0 copy-done.1
  70.7 0.0 copy-start.4
  70.7 0.8 copy-done.4
  71.5 0.0 copy-start.6
  71.5 0.7 copy-done.6
  72.1 0.7 copy-done.8
  72.8 0.7 shard_map.101
  73.5 18.5 %all_to_all.22 = bf16[16,8,2048]{2,1,0:T(8,128)(2,1)} all-to-all(bf16[16,8,2048]{2,1,0:T(8,128)(2,1)S(1)} %bitcast.23), channel_id=1, replica_groups=mesh['groups'=2,'seq'=16] {'seq'}, dimensions={0} | all-to-all | bytes 1048576 | tf_op jit(solution)/shard_map/all_to_all | solution.py:232
  92.0 10.5 %copy-done = bf16[2048,8192]{1,0:T(8,128)(2,1)S(1)} copy-done((bf16[2048,8192]{1,0:T(8,128)(2,1)S(1)}, bf16[2048,8192]{1,0:T(8,128)(2,1)}, u32[]{:S(2)}) %copy-start) | copy-done | bytes 33554456
  102.5 0.0 copy-start.10
  102.5 16.0 %shard_map.102 = bf16[128,2048]{1,0:T(8,128)(2,1)} custom-call(bf16[128,2048]{1,0:T(8,128)(2,1)} %bitcast.32, bf16[2048,8192]{1,0:T(8,128)(2,1)S(1)} %copy-done, bf16[8192,2048]{1,0:T(8,128)(2,1)} %second_hbm.1), custom_call_target="tpu_custom_call" | custom-call | flops 8589934592 | bytes 33554432 | tf_op jit(solution)/shard_map/pallas_call | solution.py:157
  118.5 18.6 %all_to_all.23 = bf16[16,8,2048]{2,1,0:T(8,128)(2,1)S(1)} all-to-all(bf16[16,8,2048]{2,1,0:T(8,128)(2,1)} %bitcast.33), channel_id=1, replica_groups=mesh['groups'=2,'seq'=16] {'seq'}, dimensions={0} | all-to-all | bytes 1048576 | tf_op jit(solution)/shard_map/all_to_all | solution.py:234
  137.1 0.0 copy-done.2
  137.1 0.0 copy-done.5
  137.1 0.0 copy-done.7
  137.1 0.0 copy-done.9
  137.1 0.0 copy-done.10
  137.1 1.4 %shard_map.103 = bf16[128,2048]{1,0:T(8,128)(2,1)} custom-call(bf16[128,2048]{1,0:T(8,128)(2,1)S(1)} %bitcast.21, bf16[16,128,128]{2,1,0:T(8,128)(2,1)S(1)} %all_to_all.21.mixed_ref, f32[4,2048]{1,0:T(4,128)S(1)} %bitcast.26, s32[2,128]{1,0:T(2,128)S(1)} %bitcast.28, s32[2,128]{1,0:T(2,128)S(1)} %bitcast.30, f32[2,128]{1,0:T(2,128)S(1)} %bitcast.31, ...), custom_call_target="tpu_custom_call" | custom-call | tf_op jit(solution)/shard_map/pallas_call | solution.py:195
  (6 shorter events, 0.0 us)
Async XLA Ops:
  43.4 0.9 copy-start.3
  69.7 1.0 copy-start.1
  70.7 0.8 copy-start.4
  71.5 0.7 copy-start.6
  72.1 0.7 copy-start.8
  92.0 10.5 %copy-start = (bf16[2048,8192]{1,0:T(8,128)(2,1)S(1)}, bf16[2048,8192]{1,0:T(8,128)(2,1)}, u32[]{:S(2)}) copy-start(bf16[2048,8192]{1,0:T(8,128)(2,1)} %first_ref.1) | copy-start | bytes 100663296
  102.5 34.6 %copy-start.2 = (bf16[1,128,2048]{2,1,0:T(8,128)(2,1)S(1)}, bf16[1,128,2048]{2,1,0:T(8,128)(2,1)}, u32[]{:S(2)}) copy-start(bf16[1,128,2048]{2,1,0:T(8,128)(2,1)} %param.10) | copy-start | bytes 1572868
  102.5 34.6 %copy-start.5 = (f32[1,4,2048]{2,1,0:T(4,128)S(1)}, f32[1,4,2048]{2,1,0:T(4,128)}, u32[]{:S(2)}) copy-start(f32[1,4,2048]{2,1,0:T(4,128)} %param.12) | copy-start | bytes 98308
  102.5 34.6 %copy-start.7 = (s32[1,128,2]{1,2,0:T(2,128)S(1)}, s32[1,128,2]{1,2,0:T(2,128)}, u32[]{:S(2)}) copy-start(s32[1,128,2]{1,2,0:T(2,128)} %param.14) | copy-start | bytes 3076
  102.5 34.6 %copy-start.9 = (s32[1,128,2]{1,2,0:T(2,128)S(1)}, s32[1,128,2]{1,2,0:T(2,128)}, u32[]{:S(2)}) copy-start(s32[1,128,2]{1,2,0:T(2,128)} %param.15) | copy-start | bytes 3076
  102.5 34.6 %copy-start.10 = (f32[1,128,2]{1,2,0:T(2,128)S(1)}, f32[1,128,2]{1,2,0:T(2,128)}, u32[]{:S(2)}) copy-start(f32[1,128,2]{1,2,0:T(2,128)} %param.13) | copy-start | bytes 3076

commit v2 on v0

v2 whole, which is shorter than its diff:
```python
import functools

import jax
import jax.numpy as jnp
from jax import lax
from jax.experimental import pallas as pl
from jax.experimental.pallas import tpu as pltpu
from jax.sharding import PartitionSpec as P

EXPERTS = 16
CAP = 8
FRAMES = 16
MIB = 2**20

VMEM = pl.BlockSpec(memory_space=pltpu.VMEM)
HBM = pl.BlockSpec(memory_space=pltpu.HBM)


def held(array):
    return pltpu.with_memory_space_constraint(array, pltpu.VMEM)


def frame_order(rows, transposed=False):
    places = rows // FRAMES
    out = lax.broadcasted_iota(jnp.int32, (rows, rows), 1 if transposed else 0)
    old = lax.broadcasted_iota(jnp.int32, (rows, rows), 0 if transposed else 1)
    return jnp.where(old == out % places * FRAMES + out // places, 1.0, 0.0).astype(jnp.bfloat16)


def prepare_kernel(
    shards, qkv_hbm, hidden_hbm, scales_hbm, ids_hbm, slots_hbm, gate_hbm,
    send_out, hidden_out, scales_out, chosen_out, blending_out, back_out,
    qkv, ids, slots, gate, done, qkv_done,
):
    heads = qkv.shape[0]
    copies = [
        pltpu.make_async_copy(source, target, done.at[i])
        for i, (source, target) in enumerate(
            ((ids_hbm, ids), (slots_hbm, slots), (gate_hbm, gate), (hidden_hbm, hidden_out), (scales_hbm, scales_out))
        )
    ]
    blocks = [pltpu.make_async_copy(qkv_hbm.at[h], qkv.at[h], qkv_done.at[h]) for h in range(heads)]
    for copy in blocks + copies:
        copy.start()
    order = frame_order(qkv.shape[1])
    back_out[...] = frame_order(qkv.shape[1], True)
    for h in range(heads):
        blocks[h].wait()
        send_out[h] = jnp.dot(order, qkv[h], preferred_element_type=jnp.float32).astype(jnp.bfloat16)
    for copy in copies:
        copy.wait()
    code = jnp.where(slots[...] < CAP, ids[...] * CAP + slots[...], -1)
    choices, count = code.shape
    row = lax.broadcasted_iota(jnp.int32, (EXPERTS * CAP, count), 0)
    chosen = jnp.zeros(row.shape, jnp.float32)
    for i in range(choices):
        chosen = chosen + jnp.where(code[i : i + 1, :] == row, 1.0, 0.0)
    chosen_out[...] = chosen.astype(jnp.bfloat16)
    row = lax.broadcasted_iota(jnp.int32, (EXPERTS * CAP * shards, count), 0)
    slot = row // (CAP * shards) * CAP + row % CAP
    blending = jnp.zeros(row.shape, jnp.float32)
    for i in range(choices):
        blending = blending + jnp.where(code[i : i + 1, :] == slot, gate[i : i + 1, :], 0.0)
    blending = blending.T
    for i in range(3):
        part = blending.astype(jnp.bfloat16)
        blending_out[i * count : (i + 1) * count, :] = part
        blending = blending - part.astype(jnp.float32)


def prepare(shards, qkv, hidden, scales, ids, slots, gate):
    count = ids.shape[1]
    slot_count = EXPERTS * CAP
    return pl.pallas_call(
        functools.partial(prepare_kernel, shards),
        out_shape=[
            jax.ShapeDtypeStruct(qkv.shape, qkv.dtype),
            pltpu.VMEM(hidden.shape, hidden.dtype),
            pltpu.VMEM(scales.shape, scales.dtype),
            pltpu.VMEM((slot_count, count), jnp.bfloat16),
            pltpu.VMEM((3 * count, slot_count * shards), jnp.bfloat16),
            pltpu.VMEM((count, count), jnp.bfloat16),
        ],
        in_specs=[HBM] * 6,
        out_specs=[VMEM] * 6,
        scratch_shapes=[
            pltpu.VMEM(qkv.shape, qkv.dtype),
            pltpu.VMEM(ids.shape, ids.dtype),
            pltpu.VMEM(slots.shape, slots.dtype),
            pltpu.VMEM(gate.shape, gate.dtype),
            pltpu.SemaphoreType.DMA((5,)),
            pltpu.SemaphoreType.DMA((qkv.shape[0],)),
        ],
        compiler_params=pltpu.CompilerParams(vmem_limit_bytes=24 * MIB),
    )(qkv, hidden, scales, ids, slots, gate)


def attention_kernel(places, rows_ref, out_ref):
    sources, rows, triple = rows_ref.shape
    width = triple // 3
    length = sources * places
    block = min(length, 256)
    pair = []
    for f in range(rows // places):
        frame = rows_ref[:, f * places : (f + 1) * places, :].astype(jnp.float32)
        frame = frame.reshape(length, triple).astype(jnp.bfloat16)
        keys = frame[:, width : 2 * width]
        values = frame[:, 2 * width :]
        attended = []
        for b in range(length // block):
            queries = frame[b * block : (b + 1) * block, :width]
            scores = lax.dot_general(
                queries, keys, (((1,), (1,)), ((), ())), preferred_element_type=jnp.float32
            ) * width ** (-0.5)
            exponent = jnp.exp(scores - jnp.max(scores, axis=-1, keepdims=True))
            weights = (exponent / jnp.sum(exponent, axis=-1, keepdims=True)).astype(jnp.bfloat16)
            attended.append(jnp.dot(weights, values, preferred_element_type=jnp.float32))
        pair.append(jnp.concatenate(attended, axis=0).reshape(sources, places, width))
        if len(pair) == 2:
            out_ref[:, (f - 1) * places : (f + 1) * places, :] = jnp.concatenate(pair, axis=1).astype(jnp.bfloat16)
            pair = []


def attention(rows, places):
    sources, count, triple = rows.shape
    return pl.pallas_call(
        functools.partial(attention_kernel, places),
        out_shape=jax.ShapeDtypeStruct((sources, count, triple // 3), jnp.bfloat16),
        in_specs=[VMEM],
        out_specs=VMEM,
        compiler_params=pltpu.CompilerParams(vmem_limit_bytes=32 * MIB),
    )(rows)


def residual(hidden_ref, mixed_ref, scales_ref, back_ref):
    heads = mixed_ref.shape[0]
    mixed = jnp.concatenate([mixed_ref[h] for h in range(heads)], axis=1)
    mixed = jnp.dot(back_ref[...], mixed, preferred_element_type=jnp.float32)
    return hidden_ref[...].astype(jnp.float32) + scales_ref[0:1, :] * mixed


def dispatch_kernel(hidden_ref, mixed_ref, scales_ref, back_ref, chosen_ref, out_ref):
    resid = residual(hidden_ref, mixed_ref, scales_ref, back_ref)
    shifted = resid - jnp.mean(resid, axis=-1, keepdims=True)
    spread = jnp.mean(shifted * shifted, axis=-1, keepdims=True)
    normed = (
        shifted * lax.rsqrt(spread + 1e-06) * (1.0 + scales_ref[2:3, :]) + scales_ref[1:2, :]
    ).astype(jnp.bfloat16)
    out_ref[...] = jnp.dot(chosen_ref[...], normed, preferred_element_type=jnp.float32).astype(jnp.bfloat16)


def dispatch(hidden, mixed, scales, back, chosen):
    return pl.pallas_call(
        dispatch_kernel,
        out_shape=jax.ShapeDtypeStruct((EXPERTS * CAP, hidden.shape[1]), jnp.bfloat16),
        in_specs=[VMEM] * 5,
        out_specs=VMEM,
        compiler_params=pltpu.CompilerParams(vmem_limit_bytes=24 * MIB),
    )(held(hidden), mixed, held(scales), held(back), held(chosen))


def expert_kernel(block, rows_ref, first_hbm, second_hbm, out_ref, total, first, second, first_done, second_done):
    blocks = first_hbm.shape[1] // block
    depth = first.shape[0]

    def fetch_first(step):
        place = lax.rem(step, depth)
        start = pl.multiple_of(step * block, block)
        return pltpu.make_async_copy(first_hbm.at[:, pl.ds(start, block)], first.at[place], first_done.at[place])

    def fetch_second(step):
        place = lax.rem(step, depth)
        start = pl.multiple_of(step * block, block)
        return pltpu.make_async_copy(second_hbm.at[pl.ds(start, block)], second.at[place], second_done.at[place])

    for step in range(min(depth, blocks)):
        fetch_first(step).start()
        fetch_second(step).start()
    total[...] = jnp.zeros_like(total)

    def work(step, _):
        place = lax.rem(step, depth)
        fetch_first(step).wait()
        inner = jnp.dot(rows_ref[...], first[place], preferred_element_type=jnp.float32)
        inner = jax.nn.gelu(inner, approximate=True).astype(jnp.bfloat16)

        @pl.when(step + depth < blocks)
        def _():
            fetch_first(step + depth).start()

        fetch_second(step).wait()
        total[...] += jnp.dot(inner, second[place], preferred_element_type=jnp.float32)

        @pl.when(step + depth < blocks)
        def _():
            fetch_second(step + depth).start()

        return 0

    lax.fori_loop(0, blocks, work, 0)
    out_ref[...] = total[...].astype(jnp.bfloat16)


def expert(rows, first, second):
    count, width = rows.shape
    hidden = first.shape[1]
    block = min(hidden, 1024)
    depth = min(hidden // block, 3)
    return pl.pallas_call(
        functools.partial(expert_kernel, block),
        out_shape=jax.ShapeDtypeStruct((count, width), jnp.bfloat16),
        in_specs=[VMEM, HBM, HBM],
        out_specs=VMEM,
        scratch_shapes=[
            pltpu.VMEM((count, width), jnp.float32),
            pltpu.VMEM((depth, width, block), jnp.bfloat16),
            pltpu.VMEM((depth, block, width), jnp.bfloat16),
            pltpu.SemaphoreType.DMA((depth,)),
            pltpu.SemaphoreType.DMA((depth,)),
        ],
        compiler_params=pltpu.CompilerParams(vmem_limit_bytes=44 * MIB),
        cost_estimate=pl.CostEstimate(
            flops=4 * count * width * hidden, bytes_accessed=4 * width * hidden, transcendentals=count * hidden
        ),
    )(rows, first, second)


def combine_kernel(hidden_ref, mixed_ref, scales_ref, back_ref, blending_ref, brought_ref, out_ref):
    resid = residual(hidden_ref, mixed_ref, scales_ref, back_ref)
    count = resid.shape[0]
    mixture = jnp.dot(blending_ref[...], brought_ref[...], preferred_element_type=jnp.float32)
    mixture = mixture[:count] + (mixture[count : 2 * count] + mixture[2 * count :])
    out_ref[...] = (resid + scales_ref[3:4, :] * mixture).astype(jnp.bfloat16)


def combine(hidden, mixed, scales, back, blending, brought):
    return pl.pallas_call(
        combine_kernel,
        out_shape=jax.ShapeDtypeStruct(hidden.shape, jnp.bfloat16),
        in_specs=[VMEM] * 6,
        out_specs=VMEM,
        compiler_params=pltpu.CompilerParams(vmem_limit_bytes=24 * MIB),
    )(held(hidden), mixed, held(scales), held(back), held(blending), brought)


def exchange(array):
    return lax.all_to_all(array, "seq", split_axis=0, concat_axis=0, tiled=True)


def body(hidden_in, qkv, modulation, route_weight, expert_ids, slots, w_in, w_out):
    seq_count, head_count, row_count, triple = qkv.shape
    assert seq_count == 1
    head_width = triple // 3
    width = head_count * head_width
    devices = lax.axis_size("seq")
    frame_parts = devices // head_count
    places = row_count // FRAMES
    shards = devices // EXPERTS
    send, hidden, scales, chosen, blending, back = prepare(
        shards, qkv[0], hidden_in[0], modulation[0], expert_ids[0].T, slots[0].T, route_weight[0].T
    )
    owned = exchange(send.reshape(devices, row_count // frame_parts, triple))
    returned = exchange(attention(owned, places))
    mixed = returned.reshape(head_count, row_count, head_width)
    gathered = dispatch(hidden, mixed, scales, back, chosen)
    spread_rows = jnp.broadcast_to(
        gathered.reshape(EXPERTS, 1, CAP, width), (EXPERTS, shards, CAP, width)
    ).reshape(devices, CAP, width)
    arrived = exchange(spread_rows)
    computed = expert(arrived.reshape(devices * CAP, width), w_in, w_out)
    brought = exchange(computed.reshape(devices, CAP, width))
    final = combine(hidden, mixed, scales, back, blending, brought.reshape(devices * CAP, width))
    return final[None]


def solution(mesh):
    in_specs = (
        P("groups", "seq", None),
        P("groups", None, "seq", None),
        P("groups", None, None),
        P("groups", "seq", None),
        P("groups", "seq", None),
        P("groups", "seq", None),
        P(None, "seq"),
        P("seq", None),
    )
    out_specs = P("groups", "seq", None)
    return jax.shard_map(body, mesh=mesh, in_specs=in_specs, out_specs=out_specs, check_vma=False)
```

time: 141 us -> 139 us (0.986)
  blocking collectives: 18.4 us -> 99.3 us
  waiting for transfers between devices: 60.6 us -> 0 us
  Pallas kernels: 0 us -> 34.1 us
  matrix products: 32.8 us -> 0 us
  starting transfers between devices: 20.5 us -> 0 us
  other arithmetic: 1.64 us -> 0 us
    all_to_all x1 -> x4, blocking collectives: 18.4 us -> 99.3 us  [exchange(): return lax.all_to_all(array, 'seq', split_axis=0, concat_axis=0, tiled=True)]
    all_to_all x3 -> x0, waiting for transfers between devices: 60.6 us -> none  [the longest x1 32 us: body(): lax.all_to_all(arranged, 'seq', split_axis=0, concat_axis=1, tiled=True)[0]]
    pallas_call x0 -> x5, Pallas kernels: none -> 34.1 us  [the longest x1 21.3 us: expert(): pl.pallas_call(functools.partial(expert_kernel, block), out_shape=jax.Sha...]
    dot_general x35 -> x0, matrix products: 32.8 us -> none  [the longest x1 24.8 us: body(): jnp.dot(inner, w_out, preferred_element_type=jnp.float32)]
    all_to_all x3 -> x0, starting transfers between devices: 20.5 us -> none  [the longest x1 9.11 us: body(): lax.all_to_all(outgoing, 'seq', split_axis=0, concat_axis=0, tiled=True)]
    unnamed x10 -> x12, local copies, waits for them, and re-layouts: 0.03 us -> 5.24 us
    another operation x1 -> x0, local copies, waits for them, and re-layouts: 2.95 us -> none  [body(): arranged.transpose(0, 1, 3, 2, 4, 5)]
    reduce_sum x20 -> x0, other arithmetic: 1.49 us -> none  [the longest x16 0.74 us: scores_for(): jnp.sum(exponent, axis=-1, keepdims=True)]
  transfers between devices with their start and end apart: 3 -> 0, of which waited for: 3 -> 0; matrix products, arithmetic and copies ran while one was open for 0% -> 0% of each run, Pallas kernels for 0% -> 0%
where the time goes in v2:
time: 139 us
  blocking collectives  99.3 us (71%)
  Pallas kernels  34.1 us (25%)
  local copies, waits for them, and re-layouts  5.24 us (4%)
    all_to_all x4, blocking collectives, exchange(): return lax.all_to_all(array, 'seq', split_axis=0, concat_axis=0, tiled=True)  99.3 us
    pallas_call x1, Pallas kernels, expert(): pl.pallas_call(functools.partial(expert_kernel, block), out_shape=jax.Sha...  21.3 us
    unnamed x12, local copies, waits for them, and re-layouts  5.24 us
    pallas_call x1, Pallas kernels, attention(): pl.pallas_call(functools.partial(attention_kernel, places), out_shape=jax...  5.23 us
    pallas_call x1, Pallas kernels, prepare(): pl.pallas_call(functools.partial(prepare_kernel, shards), out_shape=[jax....  5.2 us

profile of v2, /device:TPU:0, one launch (start us, length us, event | category | flops | bytes accessed | tf_op | source)
XLA Modules:
  0.0 138.7 jit_solution(8422858408628508868)
XLA Ops:
  0.0 0.0 copy-start
  0.0 1.4 %copy-done = bf16[1,16,128,384]{3,2,1,0:T(8,128)(2,1)S(1)} copy-done((bf16[1,16,128,384]{3,2,1,0:T(8,128)(2,1)S(1)}, bf16[1,16,128,384]{3,2,1,0:T(8,128)(2,1)}, u32[]{:S(2)}) %copy-start) | copy-done | bytes 1572888
  1.4 0.0 copy-start.1
  1.4 1.0 copy-done.1
  2.5 0.0 copy-start.2
  2.5 0.8 copy-done.2
  3.2 0.0 copy-start.3
  3.2 0.7 copy-done.3
  3.9 0.0 copy-start.4
  3.9 0.7 copy-done.4
  4.6 0.0 copy-start.5
  4.6 0.7 copy-done.5
  5.2 5.2 %shard_map.82 = (bf16[16,128,384]{2,1,0:T(8,128)(2,1)S(1)}, bf16[128,2048]{1,0:T(8,128)(2,1)S(1)}, f32[4,2048]{1,0:T(4,128)S(1)}, bf16[128,128]{1,0:T(8,128)(2,1...) custom-call(bf16[16,128,384]{2,1,0:T(8,128)(2,1)S(1)} %bitcast.21, bf16[128,2048]{1,0:T(8,128)(2,1)S(1)} %bitcast.22, ...), custom_call_target="tpu_custom_call" | custom-call | tf_op jit(solution)/shard_map/pallas_call | solution.py:74
  10.5 43.2 %all_to_all.20.rows_ref = bf16[16,128,384]{2,1,0:T(8,128)(2,1)S(1)} all-to-all(bf16[16,128,384]{2,1,0:T(8,128)(2,1)S(1)} %get-tuple-element.12), channel_id=1, replica_groups=mesh['groups'=2,'seq'=16] {'seq'}, dimensions={0} | all-to-all | bytes 3145728 | tf_op jit(solution)/shard_map/all_to_all | solution.py:247
  53.7 5.2 %shard_map.83 = bf16[16,128,128]{2,1,0:T(8,128)(2,1)S(1)} custom-call(bf16[16,128,384]{2,1,0:T(8,128)(2,1)S(1)} %all_to_all.20.rows_ref), custom_call_target="tpu_custom_call" | custom-call | tf_op jit(solution)/shard_map/pallas_call | solution.py:126
  58.9 19.3 %all_to_all.21.mixed_ref = bf16[16,128,128]{2,1,0:T(8,128)(2,1)S(1)} all-to-all(bf16[16,128,128]{2,1,0:T(8,128)(2,1)S(1)} %shard_map.83), channel_id=1, replica_groups=mesh['groups'=2,'seq'=16] {'seq'}, dimensions={0} | all-to-all | bytes 1048576 | tf_op jit(solution)/shard_map/all_to_all | solution.py:247
  78.2 0.8 shard_map.84
  79.1 18.4 %all_to_all.22 = bf16[16,8,2048]{2,1,0:T(8,128)(2,1)S(1)} all-to-all(bf16[16,8,2048]{2,1,0:T(8,128)(2,1)S(1)} %bitcast.20), channel_id=1, replica_groups=mesh['groups'=2,'seq'=16] {'seq'}, dimensions={0} | all-to-all | bytes 1048576 | tf_op jit(solution)/shard_map/all_to_all | solution.py:247
  97.5 21.3 %shard_map.85 = bf16[128,2048]{1,0:T(8,128)(2,1)S(1)} custom-call(bf16[128,2048]{1,0:T(8,128)(2,1)S(1)} %bitcast.17, bf16[2048,8192]{1,0:T(8,128)(2,1)} %first_hbm.1, bf16[8192,2048]{1,0:T(8,128)(2,1)} %second_hbm.1), custom_call_target="tpu_custom_call" | custom-call | flops 8589934592 | bytes 67108864 | tf_op jit(solution)/shard_map/pallas_call | solution.py:209
  118.8 18.4 %all_to_all.23 = bf16[16,8,2048]{2,1,0:T(8,128)(2,1)S(1)} all-to-all(bf16[16,8,2048]{2,1,0:T(8,128)(2,1)S(1)} %bitcast.18), channel_id=1, replica_groups=mesh['groups'=2,'seq'=16] {'seq'}, dimensions={0} | all-to-all | bytes 1048576 | tf_op jit(solution)/shard_map/all_to_all | solution.py:247
  137.2 1.5 %shard_map.86 = bf16[128,2048]{1,0:T(8,128)(2,1)} custom-call(bf16[128,2048]{1,0:T(8,128)(2,1)S(1)} %get-tuple-element.11.hidden_ref, bf16[16,128,128]{2,1,0:T(8,128)(2,1)S(1)} %all_to_all.21.mixed_ref, f32[4,2048]{1,0:T(4,128)S(1)} %get-tuple-element.13.scales_ref, bf16[128,128]{1,0:T(8,128)(2,1)S(1)} %get-tuple-element.14.back_ref, ...), custom_call_target="tpu_custom_call" | custom-call | tf_op jit(solution)/shard_map/pallas_call | solution.py:237
Async XLA Ops:
  0.0 1.4 %copy-start = (bf16[1,16,128,384]{3,2,1,0:T(8,128)(2,1)S(1)}, bf16[1,16,128,384]{3,2,1,0:T(8,128)(2,1)}, u32[]{:S(2)}) copy-start(bf16[1,16,128,384]{3,2,1,0:T(8,128)(2,1)} %param.9) | copy-start | bytes 4718596
  1.4 1.0 copy-start.1
  2.5 0.8 copy-start.2
  3.2 0.7 copy-start.3
  3.9 0.7 copy-start.4
  4.6 0.7 copy-start.5

commit v3 on v0

v3 whole, which is shorter than its diff:
```python
import functools
import math

import jax
import jax.numpy as jnp
from jax import lax
from jax.experimental import pallas as pl
from jax.experimental.pallas import tpu as pltpu
from jax.sharding import PartitionSpec as P

EXPERTS = 16
CAP = 8
FRAMES = 16
LAYER = 4
CODE_ROWS = 8
MIB = 2**20

VMEM = pl.BlockSpec(memory_space=pltpu.VMEM)
SMEM = pl.BlockSpec(memory_space=pltpu.SMEM)
HBM = pl.BlockSpec(memory_space=pltpu.HBM)


def held(array):
    return pltpu.with_memory_space_constraint(array, pltpu.VMEM)


def far(array):
    return pltpu.with_memory_space_constraint(array, pltpu.HBM)


def exchange(array):
    return lax.all_to_all(array, "seq", split_axis=0, concat_axis=0, tiled=True)


def slot_code(chosen, slot_assignment):
    return jnp.where(slot_assignment < CAP, chosen * CAP + slot_assignment, -1)


def one_hot(code, values=None, me=0):
    choices, count = code.shape
    row = lax.broadcasted_iota(jnp.int32, (EXPERTS * CAP, count), 0) ^ me * CAP
    hits = jnp.zeros(row.shape, jnp.float32)
    for i in range(choices):
        hits = hits + jnp.where(code[i : i + 1, :] == row, 1.0 if values is None else values[i : i + 1, :], 0.0)
    return hits


def frame_order(rows, transposed):
    each = rows // FRAMES
    out = lax.broadcasted_iota(jnp.int32, (rows, rows), 1 if transposed else 0)
    old = lax.broadcasted_iota(jnp.int32, (rows, rows), 0 if transposed else 1)
    return jnp.where(old == out % each * FRAMES + out // each, 1.0, 0.0).astype(jnp.bfloat16)


def prepare_kernel(
    me_ref, hidden_hbm, scales_hbm, ids_ref, slots_ref, gate_ref,
    scales_out, stay_out, core_out, chip_out, blending_out, hidden, done,
):
    copies = [
        pltpu.make_async_copy(hidden_hbm, hidden, done.at[0]),
        pltpu.make_async_copy(scales_hbm, scales_out, done.at[1]),
    ]
    for copy in copies:
        copy.start()
    code = slot_code(ids_ref[...], slots_ref[...])
    count = code.shape[1]
    blending = one_hot(code, gate_ref[...]).T
    for i in range(3):
        part = blending.astype(jnp.bfloat16)
        blending_out[i * count : (i + 1) * count, :] = part
        blending = blending - part.astype(jnp.float32)
    chosen = one_hot(code, me=me_ref[0]).astype(jnp.bfloat16)
    for copy in copies:
        copy.wait()
    layers, packed, lanes = stay_out.shape
    rows = jnp.dot(chosen, hidden[...], preferred_element_type=jnp.float32)
    for h in range(0, packed // CAP, 2):
        pair = [
            rows[:, (h + i) * lanes : (h + i + 1) * lanes].reshape(layers, LAYER, CAP, lanes) for i in range(2)
        ]
        pair = jnp.concatenate(pair, axis=2).astype(jnp.bfloat16)
        part = slice(h * CAP, (h + 2) * CAP)
        stay_out[:, part, :] = pair[:, 0]
        core_out[0, :, part, :] = pair[:, 1]
        chip_out[:, part, :] = pair[:, 2]
        core_out[1, :, part, :] = pair[:, 3]


def prepare(me, hidden, scales, ids, slots, gate, lanes):
    count, width = hidden.shape
    slot_count = EXPERTS * CAP
    layers = EXPERTS // LAYER
    block = (CAP * width // lanes, lanes)
    return pl.pallas_call(
        prepare_kernel,
        out_shape=[
            pltpu.VMEM(scales.shape, scales.dtype),
            jax.ShapeDtypeStruct((layers,) + block, hidden.dtype),
            jax.ShapeDtypeStruct((2, layers) + block, hidden.dtype),
            jax.ShapeDtypeStruct((layers,) + block, hidden.dtype),
            pltpu.VMEM((3 * count, slot_count), jnp.bfloat16),
        ],
        in_specs=[SMEM, HBM, HBM, VMEM, VMEM, VMEM],
        out_specs=[VMEM] * 5,
        scratch_shapes=[pltpu.VMEM(hidden.shape, hidden.dtype), pltpu.SemaphoreType.DMA((2,))],
        compiler_params=pltpu.CompilerParams(vmem_limit_bytes=16 * MIB),
        cost_estimate=pl.CostEstimate(flops=2 * slot_count * count * width, bytes_accessed=4 * MIB, transcendentals=0),
    )(me, far(hidden), far(scales), ids, slots, gate)


def regroup_kernel(*refs):
    sources, outs = refs[:LAYER], refs[LAYER:]
    for r, source in enumerate(sources):
        for i, out in enumerate(outs):
            out[r] = source[i + 1]


def regroup(*sources):
    layers, *block = sources[0].shape
    return pl.pallas_call(
        regroup_kernel,
        out_shape=[jax.ShapeDtypeStruct((LAYER, *block), sources[0].dtype)] * (layers - 1),
        in_specs=[VMEM] * LAYER,
        out_specs=[VMEM] * (layers - 1),
        compiler_params=pltpu.CompilerParams(vmem_limit_bytes=8 * MIB),
    )(*sources)


def assemble_kernel(me_ref, stay_ref, core_ref, chip_ref, both_ref, *refs):
    *layer_refs, out_ref = refs
    here = [stay_ref[0], core_ref[0, 0], chip_ref[0], both_ref[0]]
    for r in range(LAYER):
        out_ref[me_ref[0] ^ r] = here[r]
        for i, layer_ref in enumerate(layer_refs):
            out_ref[me_ref[0] ^ (LAYER * (i + 1) + r)] = layer_ref[r]


def assemble(me, stay, core, chip, both, layers):
    count = LAYER * (len(layers) + 1)
    return pl.pallas_call(
        assemble_kernel,
        out_shape=jax.ShapeDtypeStruct((count,) + stay.shape[1:], stay.dtype),
        in_specs=[SMEM] + [VMEM] * (4 + len(layers)),
        out_specs=VMEM,
        compiler_params=pltpu.CompilerParams(vmem_limit_bytes=8 * MIB),
    )(me, stay, core, chip, both, *layers)


def pack_kernel(qkv_hbm, ids_hbm, slots_hbm, send_ref, ids, slots, done):
    heads, count, triple = qkv_hbm.shape
    width = triple // 3
    copies = [
        pltpu.make_async_copy(ids_hbm, ids, done.at[0]),
        pltpu.make_async_copy(slots_hbm, slots, done.at[1]),
    ]
    copies += [
        pltpu.make_async_copy(
            qkv_hbm.at[:, :, pl.ds(i * width, width)], send_ref.at[:, pl.ds(i * count, count), :], done.at[2 + i]
        )
        for i in range(3)
    ]
    for copy in copies:
        copy.start()
    for copy in copies[:2]:
        copy.wait()
    own = slot_code(ids[...], slots[...]).astype(jnp.float32)
    own = jnp.concatenate([own, jnp.zeros((CODE_ROWS - own.shape[0], own.shape[1]), jnp.float32)])
    for h in range(heads):
        send_ref[h, 3 * count :, :] = own.astype(jnp.bfloat16)
    for copy in copies[2:]:
        copy.wait()


def pack(qkv, ids, slots):
    heads, count, triple = qkv.shape
    width = triple // 3
    return pl.pallas_call(
        pack_kernel,
        out_shape=pltpu.VMEM((heads, 3 * count + CODE_ROWS, width), qkv.dtype),
        in_specs=[HBM] * 3,
        out_specs=VMEM,
        scratch_shapes=[
            pltpu.VMEM(ids.shape, ids.dtype),
            pltpu.VMEM(slots.shape, slots.dtype),
            pltpu.SemaphoreType.DMA((5,)),
        ],
        compiler_params=pltpu.CompilerParams(vmem_limit_bytes=8 * MIB),
    )(far(qkv), far(ids), far(slots))


def attention_kernel(rows_ref, expert_out, attended_out, framed, attended):
    sources, packed, width = rows_ref.shape
    count = (packed - CODE_ROWS) // 3
    places = count // FRAMES
    piece = 2 * places
    order = frame_order(2 * count, False)
    for c in range(sources // 2):
        for i in range(3):
            rows = rows_ref[2 * c : 2 * c + 2, i * count : (i + 1) * count, :].reshape(2 * count, width)
            rows = jnp.dot(order, rows, preferred_element_type=jnp.float32)
            framed[i, :, c * piece : (c + 1) * piece, :] = rows.astype(jnp.bfloat16).reshape(FRAMES, piece, width)
    scores = lax.dot_general(
        framed[0], framed[1], (((2,), (2,)), ((0,), (0,))), preferred_element_type=jnp.float32
    ) * width ** (-0.5)
    exponent = jnp.exp(scores - jnp.max(scores, axis=-1, keepdims=True))
    weights = (exponent / jnp.sum(exponent, axis=-1, keepdims=True)).astype(jnp.bfloat16)
    result = lax.dot_general(weights, framed[2], (((2,), (1,)), ((0,), (0,))), preferred_element_type=jnp.float32)
    result = result.astype(jnp.bfloat16)
    attended_out[...] = result
    attended[...] = result.astype(jnp.float32)
    codes = rows_ref[:, 3 * count :, :].reshape(sources * CODE_ROWS, count)
    codes = lax.dot_general(
        codes, frame_order(count, False), (((1,), (1,)), ((), ())), preferred_element_type=jnp.float32
    )
    slot = lax.broadcasted_iota(jnp.int32, (EXPERTS * CAP, count), 0).astype(jnp.float32)
    for c in range(sources // 2):
        pair = []
        for s in (2 * c, 2 * c + 1):
            code = codes[s * CODE_ROWS : s * CODE_ROWS + 2]
            hit = (code[0:1] == slot) | (code[1:2] == slot)
            rows = attended[:, s * places : (s + 1) * places, :].reshape(count, width).astype(jnp.bfloat16)
            rows = jnp.dot(
                jnp.where(hit, 1.0, 0.0).astype(jnp.bfloat16), rows, preferred_element_type=jnp.float32
            )
            pair.append(rows.reshape(EXPERTS, CAP, width))
        expert_out[:, 2 * c * CAP : 2 * (c + 1) * CAP, :] = jnp.concatenate(pair, axis=1).astype(jnp.bfloat16)


def attention(rows):
    sources, packed, width = rows.shape
    by_frame = (FRAMES, sources * (packed - CODE_ROWS) // 3 // FRAMES, width)
    return pl.pallas_call(
        attention_kernel,
        out_shape=[
            jax.ShapeDtypeStruct((EXPERTS, sources * CAP, width), jnp.bfloat16),
            jax.ShapeDtypeStruct(by_frame, jnp.bfloat16),
        ],
        in_specs=[VMEM],
        out_specs=[VMEM] * 2,
        scratch_shapes=[pltpu.VMEM((3,) + by_frame, jnp.bfloat16), pltpu.VMEM(by_frame, jnp.float32)],
        compiler_params=pltpu.CompilerParams(vmem_limit_bytes=24 * MIB),
    )(rows)


def restore_kernel(attended_ref, out_ref):
    sources, count, width = out_ref.shape
    piece = 2 * count // FRAMES
    back = frame_order(2 * count, True)
    for c in range(sources // 2):
        rows = attended_ref[:, c * piece : (c + 1) * piece, :].reshape(2 * count, width)
        rows = jnp.dot(back, rows, preferred_element_type=jnp.float32).astype(jnp.bfloat16)
        out_ref[2 * c : 2 * c + 2] = rows.reshape(2, count, width)


def restore(attended, sources):
    frames, length, width = attended.shape
    return pl.pallas_call(
        restore_kernel,
        out_shape=jax.ShapeDtypeStruct((sources, frames * length // sources, width), attended.dtype),
        in_specs=[VMEM],
        out_specs=VMEM,
        compiler_params=pltpu.CompilerParams(vmem_limit_bytes=16 * MIB),
        cost_estimate=pl.CostEstimate(flops=2**35, bytes_accessed=MIB, transcendentals=0),
    )(attended)


def normalize(resid, scales_ref):
    shifted = resid - jnp.mean(resid, axis=-1, keepdims=True)
    spread = jnp.mean(shifted * shifted, axis=-1, keepdims=True)
    normed = shifted * lax.rsqrt(spread + 1e-06) * (1.0 + scales_ref[2:3, :]) + scales_ref[1:2, :]
    return normed.astype(jnp.bfloat16)


def expert_kernel(
    block, arrived_ref, hidden_ref, scales_ref, first_hbm, second_hbm, out_ref,
    rows, total, first, second, first_done, second_done,
):
    blocks = first_hbm.shape[1] // block
    depth = first.shape[0]

    def fetch_first(step):
        place = lax.rem(step, depth)
        start = pl.multiple_of(step * block, block)
        return pltpu.make_async_copy(first_hbm.at[:, pl.ds(start, block)], first.at[place], first_done.at[place])

    def fetch_second(step):
        place = lax.rem(step, depth)
        start = pl.multiple_of(step * block, block)
        return pltpu.make_async_copy(second_hbm.at[pl.ds(start, block)], second.at[place], second_done.at[place])

    for step in range(min(depth, blocks)):
        fetch_first(step).start()
        fetch_second(step).start()
    total[...] = jnp.zeros_like(total)
    heads, count, lanes = arrived_ref.shape
    parts = []
    for h in range(heads):
        columns = slice(h * lanes, (h + 1) * lanes)
        hidden = hidden_ref[:, h * CAP : (h + 1) * CAP, :].astype(jnp.float32)
        mixed = arrived_ref[h].astype(jnp.float32)
        parts.append(hidden.reshape(count, lanes) + scales_ref[0:1, columns] * mixed)
    rows[...] = normalize(jnp.concatenate(parts, axis=1), scales_ref)

    def work(step, _):
        place = lax.rem(step, depth)
        fetch_first(step).wait()
        inner = jnp.dot(rows[...], first[place], preferred_element_type=jnp.float32)
        inner = jax.nn.gelu(inner, approximate=True).astype(jnp.bfloat16)

        @pl.when(step + depth < blocks)
        def _():
            fetch_first(step + depth).start()

        fetch_second(step).wait()
        total[...] += jnp.dot(inner, second[place], preferred_element_type=jnp.float32)

        @pl.when(step + depth < blocks)
        def _():
            fetch_second(step + depth).start()

        return 0

    lax.fori_loop(0, blocks, work, 0)
    out_ref[...] = total[...].astype(jnp.bfloat16)


def expert(arrived, hidden_rows, scales, first, second):
    width, hidden = first.shape
    count = arrived.shape[0] * CAP
    block = math.gcd(hidden, 1024)
    depth = min(hidden // block, 3)
    return pl.pallas_call(
        functools.partial(expert_kernel, block),
        out_shape=jax.ShapeDtypeStruct((count, width), jnp.bfloat16),
        in_specs=[VMEM] * 3 + [HBM, HBM],
        out_specs=VMEM,
        scratch_shapes=[
            pltpu.VMEM((count, width), jnp.bfloat16),
            pltpu.VMEM((count, width), jnp.float32),
            pltpu.VMEM((depth, width, block), jnp.bfloat16),
            pltpu.VMEM((depth, block, width), jnp.bfloat16),
            pltpu.SemaphoreType.DMA((depth,)),
            pltpu.SemaphoreType.DMA((depth,)),
        ],
        compiler_params=pltpu.CompilerParams(vmem_limit_bytes=44 * MIB),
        cost_estimate=pl.CostEstimate(
            flops=64 * count * width * hidden, bytes_accessed=4 * width * hidden, transcendentals=count * hidden
        ),
    )(arrived, hidden_rows, held(scales), far(first), far(second))


def combine_kernel(hidden_ref, mixed_ref, scales_ref, blending_ref, brought_ref, out_ref):
    heads = mixed_ref.shape[0]
    mixed = jnp.concatenate([mixed_ref[h].astype(jnp.float32) for h in range(heads)], axis=1)
    resid = hidden_ref[...].astype(jnp.float32) + scales_ref[0:1, :] * mixed
    count = resid.shape[0]
    mixture = jnp.dot(blending_ref[...], brought_ref[...], preferred_element_type=jnp.float32)
    mixture = mixture[:count] + (mixture[count : 2 * count] + mixture[2 * count :])
    out_ref[...] = (resid + scales_ref[3:4, :] * mixture).astype(jnp.bfloat16)


def combine(hidden, mixed, scales, blending, brought):
    return pl.pallas_call(
        combine_kernel,
        out_shape=jax.ShapeDtypeStruct(hidden.shape, jnp.bfloat16),
        in_specs=[VMEM] * 5,
        out_specs=VMEM,
        compiler_params=pltpu.CompilerParams(vmem_limit_bytes=24 * MIB),
    )(hidden, mixed, held(scales), held(blending), brought)


def partner(array, step):
    devices = lax.axis_size("seq")
    return lax.ppermute(array, "seq", [(i, i ^ step) for i in range(devices)])


def direct_body(hidden_in, qkv, modulation, route_weight, expert_ids, slots, w_in, w_out):
    triple = qkv.shape[3]
    devices = lax.axis_size("seq")
    me = jnp.full((1,), lax.axis_index("seq"), jnp.int32)
    ids, slot_rows = expert_ids[0].T, slots[0].T
    owned = exchange(pack(qkv[0], ids, slot_rows))
    scales, stay, core, chip, blending = prepare(
        me, hidden_in[0], modulation[0], ids, slot_rows, route_weight[0].T, triple // 3
    )
    core = partner(core, 1)
    chip = partner(chip, 2)
    both = partner(core[1], 2)
    layers = regroup(stay, core[0], chip, both)
    *layers, owned = lax.optimization_barrier((*layers, owned))
    layers = [partner(layer, LAYER * (i + 1)) for i, layer in enumerate(layers)]
    to_experts, attended = attention(owned)
    arrived = exchange(to_experts)
    hidden_rows, attended = lax.optimization_barrier((assemble(me, stay, core, chip, both, layers), attended))
    to_places, arrived = lax.optimization_barrier((restore(attended, devices), arrived))
    mixed = exchange(to_places)
    computed = expert(arrived, hidden_rows, scales, w_in, w_out)
    mixed, computed = lax.optimization_barrier((mixed, computed))
    brought = exchange(computed.reshape(devices, CAP, -1))
    return combine(hidden_in[0], mixed, scales, blending, brought.reshape(devices * CAP, -1))[None]


def attend(queries, key_rows, values):
    length, width = queries.shape
    block_rows = math.gcd(length, 512)
    stacked = queries.reshape(length // block_rows, block_rows, width)

    def scores_for(query_block):
        scores = jnp.dot(query_block, key_rows.T, preferred_element_type=jnp.float32) * width ** (-0.5)
        scores = scores - jnp.max(scores, axis=-1, keepdims=True)
        exponent = jnp.exp(scores)
        weights = (exponent / jnp.sum(exponent, axis=-1, keepdims=True)).astype(jnp.bfloat16)
        return jnp.dot(weights, values, preferred_element_type=jnp.float32).astype(jnp.bfloat16)

    return lax.map(scores_for, stacked).reshape(length, width)


def split_body(hidden_in, qkv, modulation, route_weight, expert_ids, slots, w_in, w_out):
    seq_count, head_count, row_count, triple = qkv.shape
    head_width = triple // 3
    width = head_count * head_width
    devices_seq = lax.axis_size("seq")
    frame_parts = devices_seq // (seq_count * head_count)
    local_frames = FRAMES // frame_parts
    places = row_count // FRAMES
    arranged = qkv.reshape(seq_count, head_count, places, frame_parts, local_frames, triple)
    arranged = arranged.transpose(0, 1, 3, 2, 4, 5).reshape(devices_seq, places, local_frames, triple)
    owned = lax.all_to_all(arranged, "seq", split_axis=0, concat_axis=1, tiled=True)[0]
    by_frame = owned.transpose(1, 0, 2)
    attended = lax.map(
        lambda one_frame: attend(
            one_frame[:, :head_width],
            one_frame[:, head_width : 2 * head_width],
            one_frame[:, 2 * head_width :],
        ),
        by_frame,
    )
    outgoing = attended.transpose(1, 0, 2).reshape(devices_seq, places, local_frames, head_width)
    returned = exchange(outgoing)
    mixed = returned.reshape(seq_count, head_count, frame_parts, places, local_frames, head_width)
    mixed = mixed.transpose(0, 3, 2, 4, 1, 5).reshape(seq_count, row_count, width)
    resid = hidden_in.astype(jnp.float32) + modulation[:, 0][:, None, :] * mixed.astype(jnp.float32)
    center = jnp.mean(resid, axis=-1, keepdims=True)
    shifted = resid - center
    spread = jnp.mean(shifted * shifted, axis=-1, keepdims=True)
    normed = shifted * lax.rsqrt(spread + 1e-06)
    normed = (normed * (1.0 + modulation[:, 2][:, None, :]) + modulation[:, 1][:, None, :]).astype(jnp.bfloat16)
    token_rows = normed.reshape(seq_count * row_count, width)
    choice_count = expert_ids.shape[-1]
    code = slot_code(expert_ids, slots).reshape(-1, choice_count)
    weight = route_weight.reshape(-1, choice_count)
    hits = code[:, :, None] == jnp.arange(EXPERTS * CAP, dtype=jnp.int32)
    selected_expert = jnp.sum(hits, axis=1).astype(jnp.bfloat16)
    expert_blending = jnp.sum(jnp.where(hits, weight[:, :, None], 0.0), axis=1)
    gathered = jnp.einsum(
        "tk,td->kd", selected_expert, token_rows, preferred_element_type=jnp.float32
    ).astype(jnp.bfloat16)
    shards = devices_seq // EXPERTS
    spread_rows = jnp.broadcast_to(
        gathered.reshape(EXPERTS, 1, CAP, width), (EXPERTS, shards, CAP, width)
    ).reshape(devices_seq, CAP, width)
    arrived = exchange(spread_rows)
    inner = jax.nn.gelu(
        jnp.dot(arrived.reshape(-1, width), w_in, preferred_element_type=jnp.float32), approximate=True
    ).astype(jnp.bfloat16)
    computed = jnp.dot(inner, w_out, preferred_element_type=jnp.float32).astype(jnp.bfloat16)
    brought = exchange(computed.reshape(arrived.shape))
    combined_outputs = jnp.sum(
        brought.astype(jnp.float32).reshape(EXPERTS, shards, CAP, width), axis=1
    ).reshape(EXPERTS * CAP, width)
    mixture = jnp.dot(
        expert_blending, combined_outputs, precision=lax.Precision.HIGHEST, preferred_element_type=jnp.float32
    )
    final = resid + modulation[:, 3][:, None, :] * mixture.reshape(seq_count, row_count, width)
    return final.astype(jnp.bfloat16)


def body(*arrays):
    seq_count, head_count = arrays[1].shape[:2]
    devices = lax.axis_size("seq")
    if seq_count == 1 and devices == head_count == EXPERTS == 16:
        return direct_body(*arrays)
    return split_body(*arrays)


def solution(mesh):
    in_specs = (
        P("groups", "seq", None),
        P("groups", None, "seq", None),
        P("groups", None, None),
        P("groups", "seq", None),
        P("groups", "seq", None),
        P("groups", "seq", None),
        P(None, "seq"),
        P("seq", None),
    )
    out_specs = P("groups", "seq", None)
    return jax.shard_map(body, mesh=mesh, in_specs=in_specs, out_specs=out_specs, check_vma=False)
```

time: 141 us -> 122 us (0.87)
  matrix products: 32.8 us -> 0 us
  Pallas kernels: 0 us -> 31.7 us
  waiting for transfers between devices: 60.6 us -> 39 us
  starting transfers between devices: 20.5 us -> 29.7 us
  local copies, waits for them, and re-layouts: 5.83 us -> 1.08 us
  blocking collectives: 18.4 us -> 20.3 us
  other arithmetic: 1.64 us -> 0 us
    all_to_all x3, waiting for transfers between devices: 60.6 us -> 21.2 us  [exchange(): return lax.all_to_all(array, 'seq', split_axis=0, concat_axis=0, tiled=True)]
    dot_general x35 -> x0, matrix products: 32.8 us -> none  [the longest x1 24.8 us: body(): jnp.dot(inner, w_out, preferred_element_type=jnp.float32)]
    pallas_call x0 -> x8, Pallas kernels: none -> 31.7 us  [the longest x1 21.4 us: expert(): pl.pallas_call(functools.partial(expert_kernel, block), out_shape=jax.Sha...]
    ppermute x0 -> x6, waiting for transfers between devices: none -> 17.8 us  [partner(): return lax.ppermute(array, 'seq', [(i, i ^ step) for i in range(devices)])]
    ppermute x0 -> x6, starting transfers between devices: none -> 12.4 us  [partner(): return lax.ppermute(array, 'seq', [(i, i ^ step) for i in range(devices)])]
    all_to_all x3, starting transfers between devices: 20.5 us -> 17.3 us  [exchange(): return lax.all_to_all(array, 'seq', split_axis=0, concat_axis=0, tiled=True)]
    another operation x1 -> x0, local copies, waits for them, and re-layouts: 2.95 us -> none  [body(): arranged.transpose(0, 1, 3, 2, 4, 5)]
    all_to_all x1, blocking collectives: 18.4 us -> 20.3 us  [exchange(): return lax.all_to_all(array, 'seq', split_axis=0, concat_axis=0, tiled=True)]
  transfers between devices with their start and end apart: 3 -> 9, of which waited for: 3 -> 5; matrix products, arithmetic and copies ran while one was open for 0% -> 0% of each run, Pallas kernels for 0% -> 23%
where the time goes in v3:
time: 122 us
  waiting for transfers between devices  39 us (32%)
  Pallas kernels  31.7 us (26%)
  starting transfers between devices  29.7 us (24%)
  blocking collectives  20.3 us (17%)
    pallas_call x1, Pallas kernels, expert(): pl.pallas_call(functools.partial(expert_kernel, block), out_shape=jax.Sha...  21.4 us
    all_to_all x3, waiting for transfers between devices, exchange(): return lax.all_to_all(array, 'seq', split_axis=0, concat_axis=0, tiled=True)  21.2 us
    all_to_all x1, blocking collectives, exchange(): return lax.all_to_all(array, 'seq', split_axis=0, concat_axis=0, tiled=True)  20.3 us
    ppermute x6, waiting for transfers between devices, partner(): return lax.ppermute(array, 'seq', [(i, i ^ step) for i in range(devices)])  17.8 us
    all_to_all x3, starting transfers between devices, exchange(): return lax.all_to_all(array, 'seq', split_axis=0, concat_axis=0, tiled=True)  17.3 us
    ppermute x6, starting transfers between devices, partner(): return lax.ppermute(array, 'seq', [(i, i ^ step) for i in range(devices)])  12.4 us
    pallas_call x1, Pallas kernels, attention(): pl.pallas_call(attention_kernel, out_shape=[jax.ShapeDtypeStruct((EXPERTS...  3.02 us
    pallas_call x1, Pallas kernels, pack(): pl.pallas_call(pack_kernel, out_shape=pltpu.VMEM((heads, 3 * count + CODE...  2.6 us
  transfers between devices with their start and end apart: 9, of which 5 were waited for; matrix products, arithmetic and copies ran while one was open for 0% of the time, Pallas kernels for 23%

profile of v3, /device:TPU:0, one launch (start us, length us, event | category | flops | bytes accessed | tf_op | source)
XLA Modules:
  0.0 121.9 jit_solution(8575402228309331437)
XLA Ops:
  0.0 2.6 %shard_map.84 = bf16[16,392,128]{2,1,0:T(8,128)(2,1)} custom-call(bf16[16,128,384]{2,1,0:T(8,128)(2,1)} %bitcast.29, s32[2,128]{1,0:T(2,128)} %bitcast.24, s32[2,128]{1,0:T(2,128)} %bitcast.26), custom_call_target="tpu_custom_call" | custom-call | tf_op jit(solution)/shard_map/pallas_call | solution.py:177
  2.6 0.0 copy-start.2
  2.6 7.5 %all-to-all-start = ((bf16[16,392,128]{2,1,0:T(8,128)(2,1)}), bf16[16,392,128]{2,1,0:T(8,128)(2,1)S(1)}, u32[]{:S(2)}, u32[]{:S(2)}) async-start(bf16[16,392,128]{2,1,0:T(8,128)(2,1)} %shard_map.84), calls=%async_computation | async-start | bytes 3211264 | tf_op jit(solution)/shard_map/all_to_all | solution.py:32
  10.2 1.4 %shard_map.82 = (f32[4,2048]{1,0:T(4,128)S(1)}, bf16[4,128,128]{2,1,0:T(8,128)(2,1)S(1)}, bf16[2,4,128,128]{3,2,1,0:T(8,128)(2,1)S(1)}, bf16[4,128,128]{2,1,0:T(8,128)(2,1)S(1)}, bf16[384,128]{1,0:T(8,128)(2,1)S(1)}) custom-call(s32[1]{0:T(128)} %bitcast.1.me_ref, bf16[128,2048]{1,0:T(8,128)(2,1)} %bitcast.20, f32[4,2048]{1,0:T(4,128)} %bitcast.30, ...), custom_call_target="tpu_custom_call" | custom-call | flops 67108864 | bytes 4194304 | tf_op jit(solution)/shard_map/pallas_call | solution.py:94
  11.6 0.5 collective-permute-start
  12.0 1.7 %collective-permute-start.1 = (bf16[4,128,128]{2,1,0:T(8,128)(2,1)S(1)}, bf16[4,128,128]{2,1,0:T(8,128)(2,1)S(1)}, u32[]{:S(2)}, u32[]{:S(2)}) collective-permute-start(bf16[4,128,128]{2,1,0:T(8,128)(2,1)S(1)} %get-tuple-element.27), channel_id=1, source_target_pairs={{0,2},{1,3},{2,0},{3,1},{4,6},{5,7},{6,4},{7,5},{8,10},{9,11},{10,... | collective-permute-start | bytes 393224 | tf_op jit(solution)/shard_map/ppermute | solution.py:374
  13.7 1.4 %collective-permute-start.2 = (bf16[4,128,128]{2,1,0:T(8,128)(2,1)S(1)}, bf16[4,128,128]{2,1,0:T(8,128)(2,1)S(1)}, u32[]{:S(2)}, u32[]{:S(2)}) collective-permute-start(bf16[4,128,128]{2,1,0:T(8,128)(2,1)S(1)} %get-tuple-element.46), channel_id=1, source_target_pairs={{0,2},{1,3},{2,0},{3,1},{4,6},{5,7},{6,4},{7,5},{8,10},{9,11},{10,... | collective-permute-start | bytes 393224 | tf_op jit(solution)/shard_map/ppermute | solution.py:374
  15.2 12.3 %collective-permute-done.1.refs_2_.chip_ref = bf16[4,128,128]{2,1,0:T(8,128)(2,1)S(1)} collective-permute-done((bf16[4,128,128]{2,1,0:T(8,128)(2,1)S(1)}, bf16[4,128,128]{2,1,0:T(8,128)(2,1)S(1)}, u32[]{:S(2)}, u32[]{:S(2)}) %collective-permute-start.1) | collective-permute-done | bytes 131104 | tf_op jit(solution)/shard_map/ppermute | solution.py:374
  27.4 4.3 %collective-permute-done.2.refs_3_.both_ref = bf16[4,128,128]{2,1,0:T(8,128)(2,1)S(1)} collective-permute-done((bf16[4,128,128]{2,1,0:T(8,128)(2,1)S(1)}, bf16[4,128,128]{2,1,0:T(8,128)(2,1)S(1)}, u32[]{:S(2)}, u32[]{:S(2)}) %collective-permute-start.2) | collective-permute-done | bytes 131104 | tf_op jit(solution)/shard_map/ppermute | solution.py:374
  31.7 0.7 shard_map.83
  32.4 10.3 %all-to-all-done.rows_ref = bf16[16,392,128]{2,1,0:T(8,128)(2,1)S(1)} async-done(((bf16[16,392,128]{2,1,0:T(8,128)(2,1)}), bf16[16,392,128]{2,1,0:T(8,128)(2,1)S(1)}, u32[]{:S(2)}, u32[]{:S(2)}) %all-to-all-start) | async-done | bytes 1605664 | tf_op jit(solution)/shard_map/all_to_all | solution.py:32
  42.7 4.9 %collective-permute-start.3 = (bf16[4,128,128]{2,1,0:T(8,128)(2,1)}, bf16[4,128,128]{2,1,0:T(8,128)(2,1)S(1)}, u32[]{:S(2)}, u32[]{:S(2)}) collective-permute-start(bf16[4,128,128]{2,1,0:T(8,128)(2,1)} %get-tuple-element.31), channel_id=1, source_target_pairs={{0,4},{1,5},{2,6},{3,7},{4,0},{5,1},{6,2},{7,3},{8,12},{9,13},{10,... | collective-permute-start | bytes 393224 | tf_op jit(solution)/shard_map/ppermute | solution.py:374
  47.6 2.5 %collective-permute-start.4 = (bf16[4,128,128]{2,1,0:T(8,128)(2,1)}, bf16[4,128,128]{2,1,0:T(8,128)(2,1)S(1)}, u32[]{:S(2)}, u32[]{:S(2)}) collective-permute-start(bf16[4,128,128]{2,1,0:T(8,128)(2,1)} %get-tuple-element.32), channel_id=1, source_target_pairs={{0,8},{1,9},{2,10},{3,11},{4,12},{5,13},{6,14},{7,15},{8,0},{9,1},... | collective-permute-start | bytes 393224 | tf_op jit(solution)/shard_map/ppermute | solution.py:374
  50.1 1.5 %collective-permute-start.5 = (bf16[4,128,128]{2,1,0:T(8,128)(2,1)S(1)}, bf16[4,128,128]{2,1,0:T(8,128)(2,1)S(1)}, u32[]{:S(2)}, u32[]{:S(2)}) collective-permute-start(bf16[4,128,128]{2,1,0:T(8,128)(2,1)S(1)} %get-tuple-element.33), channel_id=1, source_target_pairs={{0,12},{1,13},{2,14},{3,15},{4,8},{5,9},{6,10},{7,11},{8,4},{9,5},... | collective-permute-start | bytes 393224 | tf_op jit(solution)/shard_map/ppermute | solution.py:374
  51.6 3.0 %shard_map.86 = (bf16[16,128,128]{2,1,0:T(8,128)(2,1)}, bf16[16,128,128]{2,1,0:T(8,128)(2,1)S(1)}) custom-call(bf16[16,392,128]{2,1,0:T(8,128)(2,1)S(1)} %all-to-all-done.rows_ref), custom_call_target="tpu_custom_call" | custom-call | tf_op jit(solution)/shard_map/pallas_call | solution.py:232
  54.6 4.8 %all-to-all-start.1 = ((bf16[16,128,128]{2,1,0:T(8,128)(2,1)}), bf16[16,128,128]{2,1,0:T(8,128)(2,1)S(1)}, u32[]{:S(2)}, u32[]{:S(2)}) async-start(bf16[16,128,128]{2,1,0:T(8,128)(2,1)} %get-tuple-element.37), calls=%async_computation.1 | async-start | bytes 1048576 | tf_op jit(solution)/shard_map/all_to_all | solution.py:32
  59.4 1.3 %collective-permute-done.4.refs_1_ = bf16[4,128,128]{2,1,0:T(8,128)(2,1)S(1)} collective-permute-done((bf16[4,128,128]{2,1,0:T(8,128)(2,1)}, bf16[4,128,128]{2,1,0:T(8,128)(2,1)S(1)}, u32[]{:S(2)}, u32[]{:S(2)}) %collective-permute-start.4) | collective-permute-done | bytes 131104 | tf_op jit(solution)/shard_map/ppermute | solution.py:374
  60.7 1.0 copy-done.5
  61.8 1.2 %shard_map.87 = bf16[16,128,128]{2,1,0:T(8,128)(2,1)} custom-call(bf16[16,128,128]{2,1,0:T(8,128)(2,1)S(1)} %copy-done.5), custom_call_target="tpu_custom_call" | custom-call | flops 34359738368 | bytes 1048576 | tf_op jit(solution)/shard_map/pallas_call | solution.py:257
  63.0 10.9 %all-to-all-done.1.arrived_ref = bf16[16,128,128]{2,1,0:T(8,128)(2,1)S(1)} async-done(((bf16[16,128,128]{2,1,0:T(8,128)(2,1)}), bf16[16,128,128]{2,1,0:T(8,128)(2,1)S(1)}, u32[]{:S(2)}, u32[]{:S(2)}) %all-to-all-start.1) | async-done | bytes 524320 | tf_op jit(solution)/shard_map/all_to_all | solution.py:32
  73.9 5.0 %all-to-all-start.2 = ((bf16[16,128,128]{2,1,0:T(8,128)(2,1)}), bf16[16,128,128]{2,1,0:T(8,128)(2,1)S(1)}, u32[]{:S(2)}, u32[]{:S(2)}) async-start(bf16[16,128,128]{2,1,0:T(8,128)(2,1)} %shard_map.87), calls=%async_computation.2 | async-start | bytes 1048576 | tf_op jit(solution)/shard_map/all_to_all | solution.py:32
  78.8 21.4 %shard_map.88 = bf16[128,2048]{1,0:T(8,128)(2,1)S(1)} custom-call(bf16[16,128,128]{2,1,0:T(8,128)(2,1)S(1)} %all-to-all-done.1.arrived_ref, bf16[16,128,128]{2,1,0:T(8,128)(2,1)S(1)} %shard_map.85.hidden_ref, f32[4,2048]{1,0:T(4,128)S(1)} %get-tuple-element.41.scales_ref, bf16[2048,8192]{1,0:T(8,128)(2,1)} %first_hbm.1, bf16[8192,2048]{1,0:T(8,128)(2,1)} %second_hbm.1), custom_call_target="tpu_custom_call" | custom-call | flops 137438953472 | bytes 67108864 | tf_op jit(solution)/shard_map/pallas_call | solution.py:332
  100.3 20.3 %all_to_all.20 = bf16[16,8,2048]{2,1,0:T(8,128)(2,1)S(1)} all-to-all(bf16[16,8,2048]{2,1,0:T(8,128)(2,1)S(1)} %bitcast.23), channel_id=1, replica_groups=mesh['groups'=2,'seq'=16] {'seq'}, dimensions={0} | all-to-all | bytes 1048576 | tf_op jit(solution)/shard_map/all_to_all | solution.py:32
  120.5 1.4 %shard_map.89 = bf16[128,2048]{1,0:T(8,128)(2,1)} custom-call(bf16[128,2048]{1,0:T(8,128)(2,1)S(1)} %bitcast.21, bf16[16,128,128]{2,1,0:T(8,128)(2,1)S(1)} %all-to-all-done.2.mixed_ref, f32[4,2048]{1,0:T(4,128)S(1)} %get-tuple-element.41.scales_ref, bf16[384,128]{1,0:T(8,128)(2,1)S(1)} %get-tuple-element.43.blending_ref, bf16[128,2048]{1,0:T(8,128)(2,1)S(1)} %bitcast.22), custom_call_target="tpu_custom_call" | custom-call | tf_op jit(solution)/shard_map/pallas_call | solution.py:363
  (16 shorter events, 0.1 us)
Async XLA Ops:
  2.6 7.6 %copy-start.1 = (s32[1,128,2]{1,2,0:T(2,128)S(1)}, s32[1,128,2]{1,2,0:T(2,128)}, u32[]{:S(2)}) copy-start(s32[1,128,2]{1,2,0:T(2,128)} %param.12) | copy-start | bytes 3076
  2.6 7.5 %copy-start.2 = (s32[1,128,2]{1,2,0:T(2,128)S(1)}, s32[1,128,2]{1,2,0:T(2,128)}, u32[]{:S(2)}) copy-start(s32[1,128,2]{1,2,0:T(2,128)} %param.13) | copy-start | bytes 3076
  2.6 7.5 %copy-start.3 = (f32[1,128,2]{1,2,0:T(2,128)S(1)}, f32[1,128,2]{1,2,0:T(2,128)}, u32[]{:S(2)}) copy-start(f32[1,128,2]{1,2,0:T(2,128)} %param.11) | copy-start | bytes 3076
  2.6 40.1 %all-to-all-start = ((bf16[16,392,128]{2,1,0:T(8,128)(2,1)}), bf16[16,392,128]{2,1,0:T(8,128)(2,1)S(1)}, u32[]{:S(2)}, u32[]{:S(2)}) async-start(bf16[16,392,128]{2,1,0:T(8,128)(2,1)} %shard_map.84), calls=%async_computation | async-start | bytes 3211264 | tf_op jit(solution)/shard_map/all_to_all | solution.py:32
  11.6 2.1 %collective-permute-start = (bf16[2,4,128,128]{3,2,1,0:T(8,128)(2,1)S(1)}, bf16[2,4,128,128]{3,2,1,0:T(8,128)(2,1)S(1)}, u32[]{:S(2)}, u32[]{:S(2)}) collective-permute-start(bf16[2,4,128,128]{3,2,1,0:T(8,128)(2,1)S(1)} %get-tuple-element.26), channel_id=1, source_target_pairs={{0,1},{1,0},{2,3},{3,2},{4,5},{5,4},{6,7},{7,6},{8,9},{9,8},{10,11... | collective-permute-start | bytes 786440 | tf_op jit(solution)/shard_map/ppermute | solution.py:374
  12.0 15.4 %collective-permute-start.1 = (bf16[4,128,128]{2,1,0:T(8,128)(2,1)S(1)}, bf16[4,128,128]{2,1,0:T(8,128)(2,1)S(1)}, u32[]{:S(2)}, u32[]{:S(2)}) collective-permute-start(bf16[4,128,128]{2,1,0:T(8,128)(2,1)S(1)} %get-tuple-element.27), channel_id=1, source_target_pairs={{0,2},{1,3},{2,0},{3,1},{4,6},{5,7},{6,4},{7,5},{8,10},{9,11},{10,... | collective-permute-start | bytes 393224 | tf_op jit(solution)/shard_map/ppermute | solution.py:374
  13.7 18.0 %collective-permute-start.2 = (bf16[4,128,128]{2,1,0:T(8,128)(2,1)S(1)}, bf16[4,128,128]{2,1,0:T(8,128)(2,1)S(1)}, u32[]{:S(2)}, u32[]{:S(2)}) collective-permute-start(bf16[4,128,128]{2,1,0:T(8,128)(2,1)S(1)} %get-tuple-element.46), channel_id=1, source_target_pairs={{0,2},{1,3},{2,0},{3,1},{4,6},{5,7},{6,4},{7,5},{8,10},{9,11},{10,... | collective-permute-start | bytes 393224 | tf_op jit(solution)/shard_map/ppermute | solution.py:374
  42.7 16.7 %collective-permute-start.3 = (bf16[4,128,128]{2,1,0:T(8,128)(2,1)}, bf16[4,128,128]{2,1,0:T(8,128)(2,1)S(1)}, u32[]{:S(2)}, u32[]{:S(2)}) collective-permute-start(bf16[4,128,128]{2,1,0:T(8,128)(2,1)} %get-tuple-element.31), channel_id=1, source_target_pairs={{0,4},{1,5},{2,6},{3,7},{4,0},{5,1},{6,2},{7,3},{8,12},{9,13},{10,... | collective-permute-start | bytes 393224 | tf_op jit(solution)/shard_map/ppermute | solution.py:374
  47.6 13.1 %collective-permute-start.4 = (bf16[4,128,128]{2,1,0:T(8,128)(2,1)}, bf16[4,128,128]{2,1,0:T(8,128)(2,1)S(1)}, u32[]{:S(2)}, u32[]{:S(2)}) collective-permute-start(bf16[4,128,128]{2,1,0:T(8,128)(2,1)} %get-tuple-element.32), channel_id=1, source_target_pairs={{0,8},{1,9},{2,10},{3,11},{4,12},{5,13},{6,14},{7,15},{8,0},{9,1},... | collective-permute-start | bytes 393224 | tf_op jit(solution)/shard_map/ppermute | solution.py:374
  50.1 10.6 %collective-permute-start.5 = (bf16[4,128,128]{2,1,0:T(8,128)(2,1)S(1)}, bf16[4,128,128]{2,1,0:T(8,128)(2,1)S(1)}, u32[]{:S(2)}, u32[]{:S(2)}) collective-permute-start(bf16[4,128,128]{2,1,0:T(8,128)(2,1)S(1)} %get-tuple-element.33), channel_id=1, source_target_pairs={{0,12},{1,13},{2,14},{3,15},{4,8},{5,9},{6,10},{7,11},{8,4},{9,5},... | collective-permute-start | bytes 393224 | tf_op jit(solution)/shard_map/ppermute | solution.py:374
  54.6 6.1 %copy-start.4 = (bf16[16,128,128]{2,1,0:T(8,128)(2,1)}, bf16[16,128,128]{2,1,0:T(8,128)(2,1)S(1)}, u32[]{:S(2)}) copy-start(bf16[16,128,128]{2,1,0:T(8,128)(2,1)S(1)} %get-tuple-element.36.attended_ref) | copy-start | bytes 1572868
  54.6 19.3 %all-to-all-start.1 = ((bf16[16,128,128]{2,1,0:T(8,128)(2,1)}), bf16[16,128,128]{2,1,0:T(8,128)(2,1)S(1)}, u32[]{:S(2)}, u32[]{:S(2)}) async-start(bf16[16,128,128]{2,1,0:T(8,128)(2,1)} %get-tuple-element.37), calls=%async_computation.1 | async-start | bytes 1048576 | tf_op jit(solution)/shard_map/all_to_all | solution.py:32
  60.7 1.0 copy-start.5
  73.9 26.4 %all-to-all-start.2 = ((bf16[16,128,128]{2,1,0:T(8,128)(2,1)}), bf16[16,128,128]{2,1,0:T(8,128)(2,1)S(1)}, u32[]{:S(2)}, u32[]{:S(2)}) async-start(bf16[16,128,128]{2,1,0:T(8,128)(2,1)} %shard_map.87), calls=%async_computation.2 | async-start | bytes 1048576 | tf_op jit(solution)/shard_map/all_to_all | solution.py:32
  78.8 41.7 %copy-start = (bf16[1,128,2048]{2,1,0:T(8,128)(2,1)S(1)}, bf16[1,128,2048]{2,1,0:T(8,128)(2,1)}, u32[]{:S(2)}) copy-start(bf16[1,128,2048]{2,1,0:T(8,128)(2,1)} %param.8) | copy-start | bytes 1572868

commit v4 on v3

--- a/solution.py
+++ b/solution.py
@@ -108,117 +108,98 @@
     )(me, far(hidden), far(scales), ids, slots, gate)
 
 
-def regroup_kernel(*refs):
-    sources, outs = refs[:LAYER], refs[LAYER:]
-    for r, source in enumerate(sources):
-        for i, out in enumerate(outs):
-            out[r] = source[i + 1]
-
-
-def regroup(*sources):
-    layers, *block = sources[0].shape
-    return pl.pallas_call(
-        regroup_kernel,
-        out_shape=[jax.ShapeDtypeStruct((LAYER, *block), sources[0].dtype)] * (layers - 1),
+def by_layer_kernel(*refs):
+    for r in range(LAYER):
+        for i in range(1, LAYER):
+            refs[LAYER + i - 1][r] = refs[r][i]
+
+
+def by_layer(*blocks):
+    return pl.pallas_call(
+        by_layer_kernel,
+        out_shape=[jax.ShapeDtypeStruct(blocks[0].shape, blocks[0].dtype)] * (LAYER - 1),
         in_specs=[VMEM] * LAYER,
-        out_specs=[VMEM] * (layers - 1),
+        out_specs=[VMEM] * (LAYER - 1),
         compiler_params=pltpu.CompilerParams(vmem_limit_bytes=8 * MIB),
-    )(*sources)
-
-
-def assemble_kernel(me_ref, stay_ref, core_ref, chip_ref, both_ref, *refs):
-    *layer_refs, out_ref = refs
-    here = [stay_ref[0], core_ref[0, 0], chip_ref[0], both_ref[0]]
+    )(*blocks)
+
+
+def by_place_kernel(*refs):
+    stay_out, core_out, chip_out = refs[LAYER:]
+    for i in range(LAYER):
+        stay_out[i] = refs[i][0]
+        core_out[0, i] = refs[i][1]
+        chip_out[i] = refs[i][2]
+        core_out[1, i] = refs[i][3]
+
+
+def by_place(*blocks):
+    shape = blocks[0].shape
+    return pl.pallas_call(
+        by_place_kernel,
+        out_shape=[jax.ShapeDtypeStruct(shape, blocks[0].dtype) for shape in (shape, (2,) + shape, shape)],
+        in_specs=[VMEM] * LAYER,
+        out_specs=[VMEM] * 3,
+        compiler_params=pltpu.CompilerParams(vmem_limit_bytes=8 * MIB),
+    )(*blocks)
+
+
+def assemble_kernel(me_ref, *refs):
+    *block_refs, out_ref = refs
+    here, away = block_refs[:LAYER], block_refs[LAYER:]
     for r in range(LAYER):
-        out_ref[me_ref[0] ^ r] = here[r]
-        for i, layer_ref in enumerate(layer_refs):
-            out_ref[me_ref[0] ^ (LAYER * (i + 1) + r)] = layer_ref[r]
-
-
-def assemble(me, stay, core, chip, both, layers):
-    count = LAYER * (len(layers) + 1)
+        for i in range(LAYER):
+            out_ref[me_ref[0] ^ (LAYER * i + r)] = away[i - 1][r] if away and i else here[r][i]
+
+
+def assemble(me, here, away=()):
     return pl.pallas_call(
         assemble_kernel,
-        out_shape=jax.ShapeDtypeStruct((count,) + stay.shape[1:], stay.dtype),
-        in_specs=[SMEM] + [VMEM] * (4 + len(layers)),
+        out_shape=jax.ShapeDtypeStruct((LAYER * LAYER,) + here[0].shape[1:], here[0].dtype),
+        in_specs=[SMEM] + [VMEM] * (LAYER + len(away)),
         out_specs=VMEM,
         compiler_params=pltpu.CompilerParams(vmem_limit_bytes=8 * MIB),
-    )(me, stay, core, chip, both, *layers)
-
-
-def pack_kernel(qkv_hbm, ids_hbm, slots_hbm, send_ref, ids, slots, done):
-    heads, count, triple = qkv_hbm.shape
+    )(me, *here, *away)
+
+
+def attention_kernel(me_ref, codes_ref, rows_ref, expert_out, attended_out, framed, attended, codes):
+    sources, count, triple = rows_ref.shape
     width = triple // 3
-    copies = [
-        pltpu.make_async_copy(ids_hbm, ids, done.at[0]),
-        pltpu.make_async_copy(slots_hbm, slots, done.at[1]),
-    ]
-    copies += [
-        pltpu.make_async_copy(
-            qkv_hbm.at[:, :, pl.ds(i * width, width)], send_ref.at[:, pl.ds(i * count, count), :], done.at[2 + i]
-        )
-        for i in range(3)
-    ]
-    for copy in copies:
-        copy.start()
-    for copy in copies[:2]:
-        copy.wait()
-    own = slot_code(ids[...], slots[...]).astype(jnp.float32)
-    own = jnp.concatenate([own, jnp.zeros((CODE_ROWS - own.shape[0], own.shape[1]), jnp.float32)])
-    for h in range(heads):
-        send_ref[h, 3 * count :, :] = own.astype(jnp.bfloat16)
-    for copy in copies[2:]:
-        copy.wait()
-
-
-def pack(qkv, ids, slots):
-    heads, count, triple = qkv.shape
-    width = triple // 3
-    return pl.pallas_call(
-        pack_kernel,
-        out_shape=pltpu.VMEM((heads, 3 * count + CODE_ROWS, width), qkv.dtype),
-        in_specs=[HBM] * 3,
-        out_specs=VMEM,
-        scratch_shapes=[
-            pltpu.VMEM(ids.shape, ids.dtype),
-            pltpu.VMEM(slots.shape, slots.dtype),
-            pltpu.SemaphoreType.DMA((5,)),
-        ],
-        compiler_params=pltpu.CompilerParams(vmem_limit_bytes=8 * MIB),
-    )(far(qkv), far(ids), far(slots))
-
-
-def attention_kernel(rows_ref, expert_out, attended_out, framed, attended):
-    sources, packed, width = rows_ref.shape
-    count = (packed - CODE_ROWS) // 3
     places = count // FRAMES
     piece = 2 * places
     order = frame_order(2 * count, False)
     for c in range(sources // 2):
-        for i in range(3):
-            rows = rows_ref[2 * c : 2 * c + 2, i * count : (i + 1) * count, :].reshape(2 * count, width)
-            rows = jnp.dot(order, rows, preferred_element_type=jnp.float32)
-            framed[i, :, c * piece : (c + 1) * piece, :] = rows.astype(jnp.bfloat16).reshape(FRAMES, piece, width)
+        rows = rows_ref[2 * c : 2 * c + 2].reshape(2 * count, triple)
+        rows = jnp.dot(order, rows, preferred_element_type=jnp.float32)
+        framed[:, c * piece : (c + 1) * piece, :] = rows.astype(jnp.bfloat16).reshape(FRAMES, piece, triple)
+    queries = framed[:, :, :width]
+    keys = framed[:, :, width : 2 * width]
+    values = framed[:, :, 2 * width :]
     scores = lax.dot_general(
-        framed[0], framed[1], (((2,), (2,)), ((0,), (0,))), preferred_element_type=jnp.float32
+        queries, keys, (((2,), (2,)), ((0,), (0,))), preferred_element_type=jnp.float32
     ) * width ** (-0.5)
     exponent = jnp.exp(scores - jnp.max(scores, axis=-1, keepdims=True))
     weights = (exponent / jnp.sum(exponent, axis=-1, keepdims=True)).astype(jnp.bfloat16)
-    result = lax.dot_general(weights, framed[2], (((2,), (1,)), ((0,), (0,))), preferred_element_type=jnp.float32)
-    result = result.astype(jnp.bfloat16)
-    attended_out[...] = result
-    attended[...] = result.astype(jnp.float32)
-    codes = rows_ref[:, 3 * count :, :].reshape(sources * CODE_ROWS, count)
-    codes = lax.dot_general(
-        codes, frame_order(count, False), (((1,), (1,)), ((), ())), preferred_element_type=jnp.float32
+    result = lax.dot_general(weights, values, (((2,), (1,)), ((0,), (0,))), preferred_element_type=jnp.float32)
+    attended[...] = result.astype(jnp.bfloat16).astype(jnp.float32)
+    codes[...] = jnp.zeros_like(codes)
+    for s in range(sources):
+        m = me_ref[0] ^ s
+        codes[s * CODE_ROWS : s * CODE_ROWS + 2, :] = codes_ref[m // LAYER, m % LAYER].astype(jnp.float32)
+    by_frame = lax.dot_general(
+        codes[...].astype(jnp.bfloat16),
+        frame_order(count, False),
+        (((1,), (1,)), ((), ())),
+        preferred_element_type=jnp.float32,
     )
     slot = lax.broadcasted_iota(jnp.int32, (EXPERTS * CAP, count), 0).astype(jnp.float32)
     for c in range(sources // 2):
         pair = []
         for s in (2 * c, 2 * c + 1):
-            code = codes[s * CODE_ROWS : s * CODE_ROWS + 2]
+            code = by_frame[s * CODE_ROWS : s * CODE_ROWS + 2]
             hit = (code[0:1] == slot) | (code[1:2] == slot)
             rows = attended[:, s * places : (s + 1) * places, :].reshape(count, width).astype(jnp.bfloat16)
+            attended_out[s] = rows
             rows = jnp.dot(
                 jnp.where(hit, 1.0, 0.0).astype(jnp.bfloat16), rows, preferred_element_type=jnp.float32
             )
@@ -226,42 +207,45 @@
         expert_out[:, 2 * c * CAP : 2 * (c + 1) * CAP, :] = jnp.concatenate(pair, axis=1).astype(jnp.bfloat16)
 
 
-def attention(rows):
-    sources, packed, width = rows.shape
-    by_frame = (FRAMES, sources * (packed - CODE_ROWS) // 3 // FRAMES, width)
+def attention(me, codes, rows):
+    sources, count, triple = rows.shape
+    width = triple // 3
+    by_frame = (FRAMES, sources * count // FRAMES)
     return pl.pallas_call(
         attention_kernel,
         out_shape=[
             jax.ShapeDtypeStruct((EXPERTS, sources * CAP, width), jnp.bfloat16),
-            jax.ShapeDtypeStruct(by_frame, jnp.bfloat16),
+            jax.ShapeDtypeStruct((sources, count, width), jnp.bfloat16),
         ],
-        in_specs=[VMEM],
+        in_specs=[SMEM, VMEM, VMEM],
         out_specs=[VMEM] * 2,
-        scratch_shapes=[pltpu.VMEM((3,) + by_frame, jnp.bfloat16), pltpu.VMEM(by_frame, jnp.float32)],
+        scratch_shapes=[
+            pltpu.VMEM(by_frame + (triple,), jnp.bfloat16),
+            pltpu.VMEM(by_frame + (width,), jnp.float32),
+            pltpu.VMEM((sources * CODE_ROWS, count), jnp.float32),
+        ],
         compiler_params=pltpu.CompilerParams(vmem_limit_bytes=24 * MIB),
-    )(rows)
-
-
-def restore_kernel(attended_ref, out_ref):
-    sources, count, width = out_ref.shape
-    piece = 2 * count // FRAMES
-    back = frame_order(2 * count, True)
-    for c in range(sources // 2):
-        rows = attended_ref[:, c * piece : (c + 1) * piece, :].reshape(2 * count, width)
-        rows = jnp.dot(back, rows, preferred_element_type=jnp.float32).astype(jnp.bfloat16)
-        out_ref[2 * c : 2 * c + 2] = rows.reshape(2, count, width)
-
-
-def restore(attended, sources):
-    frames, length, width = attended.shape
+    )(me, codes, rows)
+
+
+def restore_kernel(me_ref, attended_ref, *outs):
+    count = attended_ref.shape[1]
+    back = frame_order(count, True)
+    for m in range(LAYER * LAYER):
+        rows = jnp.dot(back, attended_ref[me_ref[0] ^ m], preferred_element_type=jnp.float32)
+        outs[m // LAYER][m % LAYER] = rows.astype(jnp.bfloat16)
+
+
+def restore(me, attended):
+    block = (LAYER,) + attended.shape[1:]
     return pl.pallas_call(
         restore_kernel,
-        out_shape=jax.ShapeDtypeStruct((sources, frames * length // sources, width), attended.dtype),
-        in_specs=[VMEM],
-        out_specs=VMEM,
+        out_shape=[jax.ShapeDtypeStruct(block, attended.dtype)] * LAYER,
+        in_specs=[SMEM, VMEM],
+        out_specs=[VMEM] * LAYER,
         compiler_params=pltpu.CompilerParams(vmem_limit_bytes=16 * MIB),
         cost_estimate=pl.CostEstimate(flops=2**35, bytes_accessed=MIB, transcendentals=0),
-    )(attended)
+    )(me, attended)
 
 
 def normalize(resid, scales_ref):
@@ -374,29 +358,45 @@
     return lax.ppermute(array, "seq", [(i, i ^ step) for i in range(devices)])
 
 
+def within_layer(stay, core, chip):
+    core = partner(core, 1)
+    chip = partner(chip, 2)
+    return stay, core[0], chip, partner(core[1], 2)
+
+
+def across_layers(blocks):
+    return [partner(block, LAYER * (i + 1)) for i, block in enumerate(blocks)]
+
+
+def gather_codes(code):
+    layer = jnp.stack([code] + [partner(code, r) for r in range(1, LAYER)])
+    return jnp.stack([layer] + [partner(layer, LAYER * i) for i in range(1, LAYER)])
+
+
 def direct_body(hidden_in, qkv, modulation, route_weight, expert_ids, slots, w_in, w_out):
     triple = qkv.shape[3]
     devices = lax.axis_size("seq")
     me = jnp.full((1,), lax.axis_index("seq"), jnp.int32)
     ids, slot_rows = expert_ids[0].T, slots[0].T
-    owned = exchange(pack(qkv[0], ids, slot_rows))
+    owned = exchange(qkv[0])
+    codes = gather_codes(slot_code(ids, slot_rows))
     scales, stay, core, chip, blending = prepare(
         me, hidden_in[0], modulation[0], ids, slot_rows, route_weight[0].T, triple // 3
     )
-    core = partner(core, 1)
-    chip = partner(chip, 2)
-    both = partner(core[1], 2)
-    layers = regroup(stay, core[0], chip, both)
-    *layers, owned = lax.optimization_barrier((*layers, owned))
-    layers = [partner(layer, LAYER * (i + 1)) for i, layer in enumerate(layers)]
-    to_experts, attended = attention(owned)
+    here = within_layer(stay, core, chip)
+    near, *away = by_layer(*here)
+    near, *away, owned = lax.optimization_barrier((partner(near, LAYER), *away, owned))
+    away = [near, partner(away[0], 2 * LAYER), partner(away[1], 3 * LAYER)]
+    to_experts, attended = attention(me, codes, owned)
     arrived = exchange(to_experts)
-    hidden_rows, attended = lax.optimization_barrier((assemble(me, stay, core, chip, both, layers), attended))
-    to_places, arrived = lax.optimization_barrier((restore(attended, devices), arrived))
-    mixed = exchange(to_places)
+    hidden_rows, attended = lax.optimization_barrier((assemble(me, here, away), attended))
+    here, *away = restore(me, attended)
+    *away, arrived = lax.optimization_barrier((*away, arrived))
+    away = across_layers(away)
     computed = expert(arrived, hidden_rows, scales, w_in, w_out)
-    mixed, computed = lax.optimization_barrier((mixed, computed))
+    *away, computed = lax.optimization_barrier((*away, computed))
     brought = exchange(computed.reshape(devices, CAP, -1))
+    mixed = assemble(me, within_layer(*by_place(here, *away)))
     return combine(hidden_in[0], mixed, scales, blending, brought.reshape(devices * CAP, -1))[None]
 
 

time: 122 us -> 116 us (0.951)
  blocking collectives: 20.3 us -> 0 us
  starting transfers between devices: 29.7 us -> 43 us
  waiting for transfers between devices: 39 us -> 42.6 us
  Pallas kernels: 31.7 us -> 28.1 us
    all_to_all x1 -> x0, blocking collectives: 20.3 us -> none  [exchange(): return lax.all_to_all(array, 'seq', split_axis=0, concat_axis=0, tiled=True)]
    ppermute x6 -> x18, starting transfers between devices: 12.4 us -> 26.3 us  [partner(): return lax.ppermute(array, 'seq', [(i, i ^ step) for i in range(devices)])]
    ppermute x6 -> x18, waiting for transfers between devices: 17.8 us -> 27.9 us  [partner(): return lax.ppermute(array, 'seq', [(i, i ^ step) for i in range(devices)])]
    all_to_all x3, waiting for transfers between devices: 21.2 us -> 14.6 us  [exchange(): return lax.all_to_all(array, 'seq', split_axis=0, concat_axis=0, tiled=True)]
    pallas_call x4 -> x5, Pallas kernels: 4.59 us -> 0.44 us  [the longest x1 0.3 us: restore(): pl.pallas_call(restore_kernel, out_shape=[jax.ShapeDtypeStruct(block, att...]
  transfers between devices with their start and end apart: 9 -> 21, of which waited for: 5 -> 10; matrix products, arithmetic and copies ran while one was open for 0% -> 0% of each run, Pallas kernels for 23% -> 23%
where the time goes in v4:
time: 116 us
  starting transfers between devices  43 us (37%)
  waiting for transfers between devices  42.6 us (37%)
  Pallas kernels  28.1 us (24%)
  local copies, waits for them, and re-layouts  2.07 us (2%)
    ppermute x18, waiting for transfers between devices, partner(): return lax.ppermute(array, 'seq', [(i, i ^ step) for i in range(devices)])  27.9 us
    ppermute x18, starting transfers between devices, partner(): return lax.ppermute(array, 'seq', [(i, i ^ step) for i in range(devices)])  26.3 us
    pallas_call x1, Pallas kernels, expert(): pl.pallas_call(functools.partial(expert_kernel, block), out_shape=jax.Sha...  22.2 us
    all_to_all x3, starting transfers between devices, exchange(): return lax.all_to_all(array, 'seq', split_axis=0, concat_axis=0, tiled=True)  16.7 us
    all_to_all x3, waiting for transfers between devices, exchange(): return lax.all_to_all(array, 'seq', split_axis=0, concat_axis=0, tiled=True)  14.6 us
    pallas_call x1, Pallas kernels, attention(): pl.pallas_call(attention_kernel, out_shape=[jax.ShapeDtypeStruct((EXPERTS...  2.72 us
  transfers between devices with their start and end apart: 21, of which 10 were waited for; matrix products, arithmetic and copies ran while one was open for 0% of the time, Pallas kernels for 23%

profile of v4, /device:TPU:0, one launch (start us, length us, event | category | flops | bytes accessed | tf_op | source)
XLA Modules:
  0.0 115.9 jit_solution(4631473842986350424)
XLA Ops:
  0.0 7.4 %all-to-all-start = ((bf16[16,128,384]{2,1,0:T(8,128)(2,1)}), bf16[16,128,384]{2,1,0:T(8,128)(2,1)S(1)}, u32[]{:S(2)}, u32[]{:S(2)}) async-start(bf16[16,128,384]{2,1,0:T(8,128)(2,1)} %bitcast.41), calls=%async_computation | async-start | bytes 3145728 | tf_op jit(solution)/shard_map/all_to_all | solution.py:32
  9.4 1.3 %shard_map.82 = (f32[4,2048]{1,0:T(4,128)S(1)}, bf16[4,128,128]{2,1,0:T(8,128)(2,1)S(1)}, bf16[2,4,128,128]{3,2,1,0:T(8,128)(2,1)S(1)}, bf16[4,128,128]{2,1,0:T(8,128)(2,1)S(1)}, bf16[384,128]{1,0:T(8,128)(2,1)S(1)}) custom-call(s32[1]{0:T(128)} %bitcast.1.me_ref, bf16[128,2048]{1,0:T(8,128)(2,1)} %bitcast.35, f32[4,2048]{1,0:T(4,128)} %bitcast.42, ...), custom_call_target="tpu_custom_call" | custom-call | flops 67108864 | bytes 4194304 | tf_op jit(solution)/shard_map/pallas_call | solution.py:94
  11.2 1.7 %collective-permute-start.1 = (bf16[4,128,128]{2,1,0:T(8,128)(2,1)S(1)}, bf16[4,128,128]{2,1,0:T(8,128)(2,1)S(1)}, u32[]{:S(2)}, u32[]{:S(2)}) collective-permute-start(bf16[4,128,128]{2,1,0:T(8,128)(2,1)S(1)} %get-tuple-element.38), channel_id=1, source_target_pairs={{0,2},{1,3},{2,0},{3,1},{4,6},{5,7},{6,4},{7,5},{8,10},{9,11},{10,... | collective-permute-start | bytes 393224 | tf_op jit(solution)/shard_map/ppermute | solution.py:358
  12.9 1.4 %collective-permute-start.2 = (bf16[4,128,128]{2,1,0:T(8,128)(2,1)S(1)}, bf16[4,128,128]{2,1,0:T(8,128)(2,1)S(1)}, u32[]{:S(2)}, u32[]{:S(2)}) collective-permute-start(bf16[4,128,128]{2,1,0:T(8,128)(2,1)S(1)} %get-tuple-element.69), channel_id=1, source_target_pairs={{0,2},{1,3},{2,0},{3,1},{4,6},{5,7},{6,4},{7,5},{8,10},{9,11},{10,... | collective-permute-start | bytes 393224 | tf_op jit(solution)/shard_map/ppermute | solution.py:358
  14.4 10.1 %collective-permute-done.1.refs_2_ = bf16[4,128,128]{2,1,0:T(8,128)(2,1)S(1)} collective-permute-done((bf16[4,128,128]{2,1,0:T(8,128)(2,1)S(1)}, bf16[4,128,128]{2,1,0:T(8,128)(2,1)S(1)}, u32[]{:S(2)}, u32[]{:S(2)}) %collective-permute-start.1) | collective-permute-done | bytes 131104 | tf_op jit(solution)/shard_map/ppermute | solution.py:358
  24.5 4.2 %collective-permute-done.2.refs_3_ = bf16[4,128,128]{2,1,0:T(8,128)(2,1)S(1)} collective-permute-done((bf16[4,128,128]{2,1,0:T(8,128)(2,1)S(1)}, bf16[4,128,128]{2,1,0:T(8,128)(2,1)S(1)}, u32[]{:S(2)}, u32[]{:S(2)}) %collective-permute-start.2) | collective-permute-done | bytes 131104 | tf_op jit(solution)/shard_map/ppermute | solution.py:358
  30.8 1.1 collective-permute-done.8
  32.6 3.7 %collective-permute-start.10 = (s32[4,2,128]{2,1,0:T(2,128)S(1)}, s32[4,2,128]{2,1,0:T(2,128)S(1)}, u32[]{:S(2)}, u32[]{:S(2)}) collective-permute-start(s32[4,2,128]{2,1,0:T(2,128)S(1)} %pad_add_fusion.1), channel_id=1, source_target_pairs={{0,8},{1,9},{2,10},{3,11},{4,12},{5,13},{6,14},{7,15},{8,0},{9,1},... | collective-permute-start | bytes 12296 | tf_op jit(solution)/shard_map/ppermute | solution.py:358
  36.4 1.4 %collective-permute-start.11 = (s32[4,2,128]{2,1,0:T(2,128)S(1)}, s32[4,2,128]{2,1,0:T(2,128)S(1)}, u32[]{:S(2)}, u32[]{:S(2)}) collective-permute-start(s32[4,2,128]{2,1,0:T(2,128)S(1)} %pad_add_fusion.1), channel_id=1, source_target_pairs={{0,12},{1,13},{2,14},{3,15},{4,8},{5,9},{6,10},{7,11},{8,4},{9,5},... | collective-permute-start | bytes 12296 | tf_op jit(solution)/shard_map/ppermute | solution.py:358
  37.8 1.6 %all-to-all-done.rows_ref = bf16[16,128,384]{2,1,0:T(8,128)(2,1)S(1)} async-done(((bf16[16,128,384]{2,1,0:T(8,128)(2,1)}), bf16[16,128,384]{2,1,0:T(8,128)(2,1)S(1)}, u32[]{:S(2)}, u32[]{:S(2)}) %all-to-all-start) | async-done | bytes 1572896 | tf_op jit(solution)/shard_map/all_to_all | solution.py:32
  39.4 7.5 %collective-permute-start.4 = (bf16[4,128,128]{2,1,0:T(8,128)(2,1)S(1)}, bf16[4,128,128]{2,1,0:T(8,128)(2,1)S(1)}, u32[]{:S(2)}, u32[]{:S(2)}) collective-permute-start(bf16[4,128,128]{2,1,0:T(8,128)(2,1)S(1)} %get-tuple-element.43), channel_id=1, source_target_pairs={{0,8},{1,9},{2,10},{3,11},{4,12},{5,13},{6,14},{7,15},{8,0},{9,1},... | collective-permute-start | bytes 393224 | tf_op jit(solution)/shard_map/ppermute | solution.py:358
  47.0 2.7 %shard_map.85 = (bf16[16,128,128]{2,1,0:T(8,128)(2,1)}, bf16[16,128,128]{2,1,0:T(8,128)(2,1)S(1)}) custom-call(s32[1]{0:T(128)} %bitcast.1.me_ref, s32[4,4,2,128]{3,2,1,0:T(2,128)S(1)} %pad_add_fusion.codes_ref, bf16[16,128,384]{2,1,0:T(8,128)(2,1)S(1)} %all-to-all-done.rows_ref), custom_call_target="tpu_custom_call" | custom-call | tf_op jit(solution)/shard_map/pallas_call | solution.py:214
  49.7 5.2 %all-to-all-start.1 = ((bf16[16,128,128]{2,1,0:T(8,128)(2,1)}), bf16[16,128,128]{2,1,0:T(8,128)(2,1)S(1)}, u32[]{:S(2)}, u32[]{:S(2)}) async-start(bf16[16,128,128]{2,1,0:T(8,128)(2,1)} %get-tuple-element.52), calls=%async_computation.1 | async-start | bytes 1048576 | tf_op jit(solution)/shard_map/all_to_all | solution.py:32
  54.9 1.7 %collective-permute-done.4.refs_5_ = bf16[4,128,128]{2,1,0:T(8,128)(2,1)S(1)} collective-permute-done((bf16[4,128,128]{2,1,0:T(8,128)(2,1)S(1)}, bf16[4,128,128]{2,1,0:T(8,128)(2,1)S(1)}, u32[]{:S(2)}, u32[]{:S(2)}) %collective-permute-start.4) | collective-permute-done | bytes 131104 | tf_op jit(solution)/shard_map/ppermute | solution.py:358
  56.9 12.4 %all-to-all-done.1.arrived_ref = bf16[16,128,128]{2,1,0:T(8,128)(2,1)S(1)} async-done(((bf16[16,128,128]{2,1,0:T(8,128)(2,1)}), bf16[16,128,128]{2,1,0:T(8,128)(2,1)S(1)}, u32[]{:S(2)}, u32[]{:S(2)}) %all-to-all-start.1) | async-done | bytes 524320 | tf_op jit(solution)/shard_map/all_to_all | solution.py:32
  70.4 1.2 %collective-permute-start.13 = (bf16[4,128,128]{2,1,0:T(8,128)(2,1)S(1)}, bf16[4,128,128]{2,1,0:T(8,128)(2,1)S(1)}, u32[]{:S(2)}, u32[]{:S(2)}) collective-permute-start(bf16[4,128,128]{2,1,0:T(8,128)(2,1)S(1)} %get-tuple-element.54), channel_id=1, source_target_pairs={{0,8},{1,9},{2,10},{3,11},{4,12},{5,13},{6,14},{7,15},{8,0},{9,1},... | collective-permute-start | bytes 393224 | tf_op jit(solution)/shard_map/ppermute | solution.py:358
  71.6 2.1 %collective-permute-start.14 = (bf16[4,128,128]{2,1,0:T(8,128)(2,1)S(1)}, bf16[4,128,128]{2,1,0:T(8,128)(2,1)S(1)}, u32[]{:S(2)}, u32[]{:S(2)}) collective-permute-start(bf16[4,128,128]{2,1,0:T(8,128)(2,1)S(1)} %get-tuple-element.55), channel_id=1, source_target_pairs={{0,12},{1,13},{2,14},{3,15},{4,8},{5,9},{6,10},{7,11},{8,4},{9,5},... | collective-permute-start | bytes 393224 | tf_op jit(solution)/shard_map/ppermute | solution.py:358
  73.7 22.2 %shard_map.87 = bf16[128,2048]{1,0:T(8,128)(2,1)} custom-call(bf16[16,128,128]{2,1,0:T(8,128)(2,1)S(1)} %all-to-all-done.1.arrived_ref, bf16[16,128,128]{2,1,0:T(8,128)(2,1)S(1)} %shard_map.84.hidden_ref, f32[4,2048]{1,0:T(4,128)S(1)} %get-tuple-element.58.scales_ref, bf16[2048,8192]{1,0:T(8,128)(2,1)} %first_hbm.1, bf16[8192,2048]{1,0:T(8,128)(2,1)} %second_hbm.1), custom_call_target="tpu_custom_call" | custom-call | flops 137438953472 | bytes 67108864 | tf_op jit(solution)/shard_map/pallas_call | solution.py:316
  96.0 4.1 %all-to-all-start.2 = ((bf16[16,8,2048]{2,1,0:T(8,128)(2,1)}), bf16[16,8,2048]{2,1,0:T(8,128)(2,1)S(1)}, u32[]{:S(2)}, u32[]{:S(2)}) async-start(bf16[16,8,2048]{2,1,0:T(8,128)(2,1)} %bitcast.24), calls=%async_computation.2 | async-start | bytes 1048576 | tf_op jit(solution)/shard_map/all_to_all | solution.py:32
  100.6 1.7 %collective-permute-start.16 = (bf16[4,128,128]{2,1,0:T(8,128)(2,1)S(1)}, bf16[4,128,128]{2,1,0:T(8,128)(2,1)S(1)}, u32[]{:S(2)}, u32[]{:S(2)}) collective-permute-start(bf16[4,128,128]{2,1,0:T(8,128)(2,1)S(1)} %get-tuple-element.64), channel_id=1, source_target_pairs={{0,2},{1,3},{2,0},{3,1},{4,6},{5,7},{6,4},{7,5},{8,10},{9,11},{10,... | collective-permute-start | bytes 393224 | tf_op jit(solution)/shard_map/ppermute | solution.py:358
  102.3 1.4 %collective-permute-start.17 = (bf16[4,128,128]{2,1,0:T(8,128)(2,1)S(1)}, bf16[4,128,128]{2,1,0:T(8,128)(2,1)S(1)}, u32[]{:S(2)}, u32[]{:S(2)}) collective-permute-start(bf16[4,128,128]{2,1,0:T(8,128)(2,1)S(1)} %get-tuple-element.67), channel_id=1, source_target_pairs={{0,2},{1,3},{2,0},{3,1},{4,6},{5,7},{6,4},{7,5},{8,10},{9,11},{10,... | collective-permute-start | bytes 393224 | tf_op jit(solution)/shard_map/ppermute | solution.py:358
  103.8 7.0 %collective-permute-done.16.refs_2_ = bf16[4,128,128]{2,1,0:T(8,128)(2,1)S(1)} collective-permute-done((bf16[4,128,128]{2,1,0:T(8,128)(2,1)S(1)}, bf16[4,128,128]{2,1,0:T(8,128)(2,1)S(1)}, u32[]{:S(2)}, u32[]{:S(2)}) %collective-permute-start.16) | collective-permute-done | bytes 131104 | tf_op jit(solution)/shard_map/ppermute | solution.py:358
  110.8 3.1 %collective-permute-done.17.refs_3_ = bf16[4,128,128]{2,1,0:T(8,128)(2,1)S(1)} collective-permute-done((bf16[4,128,128]{2,1,0:T(8,128)(2,1)S(1)}, bf16[4,128,128]{2,1,0:T(8,128)(2,1)S(1)}, u32[]{:S(2)}, u32[]{:S(2)}) %collective-permute-start.17) | collective-permute-done | bytes 131104 | tf_op jit(solution)/shard_map/ppermute | solution.py:358
  114.6 1.4 %shard_map.90 = bf16[128,2048]{1,0:T(8,128)(2,1)} custom-call(bf16[128,2048]{1,0:T(8,128)(2,1)S(1)} %bitcast.36, bf16[16,128,128]{2,1,0:T(8,128)(2,1)S(1)} %shard_map.89.mixed_ref, f32[4,2048]{1,0:T(4,128)S(1)} %get-tuple-element.58.scales_ref, bf16[384,128]{1,0:T(8,128)(2,1)S(1)} %get-tuple-element.65.blending_ref, bf16[128,2048]{1,0:T(8,128)(2,1)S(1)} %bitcast.37), custom_call_target="tpu_custom_call" | custom-call | tf_op jit(solution)/shard_map/pallas_call | solution.py:347
  (41 shorter events, 8.0 us)
Async XLA Ops:
  0.0 39.4 %all-to-all-start = ((bf16[16,128,384]{2,1,0:T(8,128)(2,1)}), bf16[16,128,384]{2,1,0:T(8,128)(2,1)S(1)}, u32[]{:S(2)}, u32[]{:S(2)}) async-start(bf16[16,128,384]{2,1,0:T(8,128)(2,1)} %bitcast.41), calls=%async_computation | async-start | bytes 3145728 | tf_op jit(solution)/shard_map/all_to_all | solution.py:32
  7.4 0.7 copy-start.1
  8.1 0.7 copy-start.2
  10.8 2.2 %collective-permute-start = (bf16[2,4,128,128]{3,2,1,0:T(8,128)(2,1)S(1)}, bf16[2,4,128,128]{3,2,1,0:T(8,128)(2,1)S(1)}, u32[]{:S(2)}, u32[]{:S(2)}) collective-permute-start(bf16[2,4,128,128]{3,2,1,0:T(8,128)(2,1)S(1)} %get-tuple-element.37), channel_id=1, source_target_pairs={{0,1},{1,0},{2,3},{3,2},{4,5},{5,4},{6,7},{7,6},{8,9},{9,8},{10,11... | collective-permute-start | bytes 786440 | tf_op jit(solution)/shard_map/ppermute | solution.py:358
  11.2 13.3 %collective-permute-start.1 = (bf16[4,128,128]{2,1,0:T(8,128)(2,1)S(1)}, bf16[4,128,128]{2,1,0:T(8,128)(2,1)S(1)}, u32[]{:S(2)}, u32[]{:S(2)}) collective-permute-start(bf16[4,128,128]{2,1,0:T(8,128)(2,1)S(1)} %get-tuple-element.38), channel_id=1, source_target_pairs={{0,2},{1,3},{2,0},{3,1},{4,6},{5,7},{6,4},{7,5},{8,10},{9,11},{10,... | collective-permute-start | bytes 393224 | tf_op jit(solution)/shard_map/ppermute | solution.py:358
  12.9 15.8 %collective-permute-start.2 = (bf16[4,128,128]{2,1,0:T(8,128)(2,1)S(1)}, bf16[4,128,128]{2,1,0:T(8,128)(2,1)S(1)}, u32[]{:S(2)}, u32[]{:S(2)}) collective-permute-start(bf16[4,128,128]{2,1,0:T(8,128)(2,1)S(1)} %get-tuple-element.69), channel_id=1, source_target_pairs={{0,2},{1,3},{2,0},{3,1},{4,6},{5,7},{6,4},{7,5},{8,10},{9,11},{10,... | collective-permute-start | bytes 393224 | tf_op jit(solution)/shard_map/ppermute | solution.py:358
  28.7 9.1 %collective-permute-start.3 = (bf16[4,128,128]{2,1,0:T(8,128)(2,1)S(1)}, bf16[4,128,128]{2,1,0:T(8,128)(2,1)S(1)}, u32[]{:S(2)}, u32[]{:S(2)}) collective-permute-start(bf16[4,128,128]{2,1,0:T(8,128)(2,1)S(1)} %get-tuple-element.39), channel_id=1, source_target_pairs={{0,4},{1,5},{2,6},{3,7},{4,0},{5,1},{6,2},{7,3},{8,12},{9,13},{10,... | collective-permute-start | bytes 393224 | tf_op jit(solution)/shard_map/ppermute | solution.py:358
  28.8 3.1 %collective-permute-start.8 = (s32[2,128]{1,0:T(2,128)S(1)}, s32[2,128]{1,0:T(2,128)S(1)}, u32[]{:S(2)}, u32[]{:S(2)}) collective-permute-start(s32[2,128]{1,0:T(2,128)S(1)} %compare_select_fusion), channel_id=1, source_target_pairs={{0,3},{1,2},{2,1},{3,0},{4,7},{5,6},{6,5},{7,4},{8,11},{9,10},{10,... | collective-permute-start | bytes 3080 | tf_op jit(solution)/shard_map/ppermute | solution.py:358
  28.9 3.6 %collective-permute-start.7 = (s32[2,128]{1,0:T(2,128)S(1)}, s32[2,128]{1,0:T(2,128)S(1)}, u32[]{:S(2)}, u32[]{:S(2)}) collective-permute-start(s32[2,128]{1,0:T(2,128)S(1)} %compare_select_fusion), channel_id=1, source_target_pairs={{0,2},{1,3},{2,0},{3,1},{4,6},{5,7},{6,4},{7,5},{8,10},{9,11},{10,... | collective-permute-start | bytes 3080 | tf_op jit(solution)/shard_map/ppermute | solution.py:358
  30.0 2.5 %collective-permute-start.6 = (s32[2,128]{1,0:T(2,128)S(1)}, s32[2,128]{1,0:T(2,128)S(1)}, u32[]{:S(2)}, u32[]{:S(2)}) collective-permute-start(s32[2,128]{1,0:T(2,128)S(1)} %compare_select_fusion), channel_id=1, source_target_pairs={{0,1},{1,0},{2,3},{3,2},{4,5},{5,4},{6,7},{7,6},{8,9},{9,8},{10,11... | collective-permute-start | bytes 3080 | tf_op jit(solution)/shard_map/ppermute | solution.py:358
  32.6 14.4 %collective-permute-start.10 = (s32[4,2,128]{2,1,0:T(2,128)S(1)}, s32[4,2,128]{2,1,0:T(2,128)S(1)}, u32[]{:S(2)}, u32[]{:S(2)}) collective-permute-start(s32[4,2,128]{2,1,0:T(2,128)S(1)} %pad_add_fusion.1), channel_id=1, source_target_pairs={{0,8},{1,9},{2,10},{3,11},{4,12},{5,13},{6,14},{7,15},{8,0},{9,1},... | collective-permute-start | bytes 12296 | tf_op jit(solution)/shard_map/ppermute | solution.py:358
  36.3 10.6 %collective-permute-start.9 = (s32[4,2,128]{2,1,0:T(2,128)S(1)}, s32[4,2,128]{2,1,0:T(2,128)S(1)}, u32[]{:S(2)}, u32[]{:S(2)}) collective-permute-start(s32[4,2,128]{2,1,0:T(2,128)S(1)} %pad_add_fusion.1), channel_id=1, source_target_pairs={{0,4},{1,5},{2,6},{3,7},{4,0},{5,1},{6,2},{7,3},{8,12},{9,13},{10,... | collective-permute-start | bytes 12296 | tf_op jit(solution)/shard_map/ppermute | solution.py:358
  36.4 10.5 %collective-permute-start.11 = (s32[4,2,128]{2,1,0:T(2,128)S(1)}, s32[4,2,128]{2,1,0:T(2,128)S(1)}, u32[]{:S(2)}, u32[]{:S(2)}) collective-permute-start(s32[4,2,128]{2,1,0:T(2,128)S(1)} %pad_add_fusion.1), channel_id=1, source_target_pairs={{0,12},{1,13},{2,14},{3,15},{4,8},{5,9},{6,10},{7,11},{8,4},{9,5},... | collective-permute-start | bytes 12296 | tf_op jit(solution)/shard_map/ppermute | solution.py:358
  39.4 17.2 %collective-permute-start.4 = (bf16[4,128,128]{2,1,0:T(8,128)(2,1)S(1)}, bf16[4,128,128]{2,1,0:T(8,128)(2,1)S(1)}, u32[]{:S(2)}, u32[]{:S(2)}) collective-permute-start(bf16[4,128,128]{2,1,0:T(8,128)(2,1)S(1)} %get-tuple-element.43), channel_id=1, source_target_pairs={{0,8},{1,9},{2,10},{3,11},{4,12},{5,13},{6,14},{7,15},{8,0},{9,1},... | collective-permute-start | bytes 393224 | tf_op jit(solution)/shard_map/ppermute | solution.py:358
  46.9 9.7 %collective-permute-start.5 = (bf16[4,128,128]{2,1,0:T(8,128)(2,1)S(1)}, bf16[4,128,128]{2,1,0:T(8,128)(2,1)S(1)}, u32[]{:S(2)}, u32[]{:S(2)}) collective-permute-start(bf16[4,128,128]{2,1,0:T(8,128)(2,1)S(1)} %get-tuple-element.44), channel_id=1, source_target_pairs={{0,12},{1,13},{2,14},{3,15},{4,8},{5,9},{6,10},{7,11},{8,4},{9,5},... | collective-permute-start | bytes 393224 | tf_op jit(solution)/shard_map/ppermute | solution.py:358
  49.7 19.7 %all-to-all-start.1 = ((bf16[16,128,128]{2,1,0:T(8,128)(2,1)}), bf16[16,128,128]{2,1,0:T(8,128)(2,1)S(1)}, u32[]{:S(2)}, u32[]{:S(2)}) async-start(bf16[16,128,128]{2,1,0:T(8,128)(2,1)} %get-tuple-element.52), calls=%async_computation.1 | async-start | bytes 1048576 | tf_op jit(solution)/shard_map/all_to_all | solution.py:32
  69.3 26.6 %collective-permute-start.12 = (bf16[4,128,128]{2,1,0:T(8,128)(2,1)S(1)}, bf16[4,128,128]{2,1,0:T(8,128)(2,1)S(1)}, u32[]{:S(2)}, u32[]{:S(2)}) collective-permute-start(bf16[4,128,128]{2,1,0:T(8,128)(2,1)S(1)} %get-tuple-element.53), channel_id=1, source_target_pairs={{0,4},{1,5},{2,6},{3,7},{4,0},{5,1},{6,2},{7,3},{8,12},{9,13},{10,... | collective-permute-start | bytes 393224 | tf_op jit(solution)/shard_map/ppermute | solution.py:358
  70.4 25.5 %collective-permute-start.13 = (bf16[4,128,128]{2,1,0:T(8,128)(2,1)S(1)}, bf16[4,128,128]{2,1,0:T(8,128)(2,1)S(1)}, u32[]{:S(2)}, u32[]{:S(2)}) collective-permute-start(bf16[4,128,128]{2,1,0:T(8,128)(2,1)S(1)} %get-tuple-element.54), channel_id=1, source_target_pairs={{0,8},{1,9},{2,10},{3,11},{4,12},{5,13},{6,14},{7,15},{8,0},{9,1},... | collective-permute-start | bytes 393224 | tf_op jit(solution)/shard_map/ppermute | solution.py:358
  71.6 24.4 %collective-permute-start.14 = (bf16[4,128,128]{2,1,0:T(8,128)(2,1)S(1)}, bf16[4,128,128]{2,1,0:T(8,128)(2,1)S(1)}, u32[]{:S(2)}, u32[]{:S(2)}) collective-permute-start(bf16[4,128,128]{2,1,0:T(8,128)(2,1)S(1)} %get-tuple-element.55), channel_id=1, source_target_pairs={{0,12},{1,13},{2,14},{3,15},{4,8},{5,9},{6,10},{7,11},{8,4},{9,5},... | collective-permute-start | bytes 393224 | tf_op jit(solution)/shard_map/ppermute | solution.py:358
  73.7 40.9 %copy-start = (bf16[1,128,2048]{2,1,0:T(8,128)(2,1)S(1)}, bf16[1,128,2048]{2,1,0:T(8,128)(2,1)}, u32[]{:S(2)}) copy-start(bf16[1,128,2048]{2,1,0:T(8,128)(2,1)} %param.8) | copy-start | bytes 1572868
  96.0 18.6 %all-to-all-start.2 = ((bf16[16,8,2048]{2,1,0:T(8,128)(2,1)}), bf16[16,8,2048]{2,1,0:T(8,128)(2,1)S(1)}, u32[]{:S(2)}, u32[]{:S(2)}) async-start(bf16[16,8,2048]{2,1,0:T(8,128)(2,1)} %bitcast.24), calls=%async_computation.2 | async-start | bytes 1048576 | tf_op jit(solution)/shard_map/all_to_all | solution.py:32
  100.2 2.2 %collective-permute-start.15 = (bf16[2,4,128,128]{3,2,1,0:T(8,128)(2,1)S(1)}, bf16[2,4,128,128]{3,2,1,0:T(8,128)(2,1)S(1)}, u32[]{:S(2)}, u32[]{:S(2)}) collective-permute-start(bf16[2,4,128,128]{3,2,1,0:T(8,128)(2,1)S(1)} %get-tuple-element.63), channel_id=1, source_target_pairs={{0,1},{1,0},{2,3},{3,2},{4,5},{5,4},{6,7},{7,6},{8,9},{9,8},{10,11... | collective-permute-start | bytes 786440 | tf_op jit(solution)/shard_map/ppermute | solution.py:358
  100.6 10.2 %collective-permute-start.16 = (bf16[4,128,128]{2,1,0:T(8,128)(2,1)S(1)}, bf16[4,128,128]{2,1,0:T(8,128)(2,1)S(1)}, u32[]{:S(2)}, u32[]{:S(2)}) collective-permute-start(bf16[4,128,128]{2,1,0:T(8,128)(2,1)S(1)} %get-tuple-element.64), channel_id=1, source_target_pairs={{0,2},{1,3},{2,0},{3,1},{4,6},{5,7},{6,4},{7,5},{8,10},{9,11},{10,... | collective-permute-start | bytes 393224 | tf_op jit(solution)/shard_map/ppermute | solution.py:358
  102.3 11.5 %collective-permute-start.17 = (bf16[4,128,128]{2,1,0:T(8,128)(2,1)S(1)}, bf16[4,128,128]{2,1,0:T(8,128)(2,1)S(1)}, u32[]{:S(2)}, u32[]{:S(2)}) collective-permute-start(bf16[4,128,128]{2,1,0:T(8,128)(2,1)S(1)} %get-tuple-element.67), channel_id=1, source_target_pairs={{0,2},{1,3},{2,0},{3,1},{4,6},{5,7},{6,4},{7,5},{8,10},{9,11},{10,... | collective-permute-start | bytes 393224 | tf_op jit(solution)/shard_map/ppermute | solution.py:358
  (1 other events, 0.7 us)

commit v5 on v4

--- a/solution.py
+++ b/solution.py
@@ -54,8 +54,9 @@
 
 def prepare_kernel(
     me_ref, hidden_hbm, scales_hbm, ids_ref, slots_ref, gate_ref,
-    scales_out, stay_out, core_out, chip_out, blending_out, hidden, done,
+    scales_out, blending_out, *refs
 ):
+    *outs, hidden, done = refs
     copies = [
         pltpu.make_async_copy(hidden_hbm, hidden, done.at[0]),
         pltpu.make_async_copy(scales_hbm, scales_out, done.at[1]),
@@ -72,7 +73,7 @@
     chosen = one_hot(code, me=me_ref[0]).astype(jnp.bfloat16)
     for copy in copies:
         copy.wait()
-    layers, packed, lanes = stay_out.shape
+    layers, packed, lanes = outs[0].shape
     rows = jnp.dot(chosen, hidden[...], preferred_element_type=jnp.float32)
     for h in range(0, packed // CAP, 2):
         pair = [
@@ -80,10 +81,8 @@
         ]
         pair = jnp.concatenate(pair, axis=2).astype(jnp.bfloat16)
         part = slice(h * CAP, (h + 2) * CAP)
-        stay_out[:, part, :] = pair[:, 0]
-        core_out[0, :, part, :] = pair[:, 1]
-        chip_out[:, part, :] = pair[:, 2]
-        core_out[1, :, part, :] = pair[:, 3]
+        for r, out in enumerate(outs):
+            out[:, part, :] = pair[:, r]
 
 
 def prepare(me, hidden, scales, ids, slots, gate, lanes):
@@ -95,13 +94,11 @@
         prepare_kernel,
         out_shape=[
             pltpu.VMEM(scales.shape, scales.dtype),
-            jax.ShapeDtypeStruct((layers,) + block, hidden.dtype),
-            jax.ShapeDtypeStruct((2, layers) + block, hidden.dtype),
-            jax.ShapeDtypeStruct((layers,) + block, hidden.dtype),
             pltpu.VMEM((3 * count, slot_count), jnp.bfloat16),
-        ],
+        ]
+        + [jax.ShapeDtypeStruct((layers,) + block, hidden.dtype)] * LAYER,
         in_specs=[SMEM, HBM, HBM, VMEM, VMEM, VMEM],
-        out_specs=[VMEM] * 5,
+        out_specs=[VMEM] * (2 + LAYER),
         scratch_shapes=[pltpu.VMEM(hidden.shape, hidden.dtype), pltpu.SemaphoreType.DMA((2,))],
         compiler_params=pltpu.CompilerParams(vmem_limit_bytes=16 * MIB),
         cost_estimate=pl.CostEstimate(flops=2 * slot_count * count * width, bytes_accessed=4 * MIB, transcendentals=0),
@@ -125,21 +122,17 @@
 
 
 def by_place_kernel(*refs):
-    stay_out, core_out, chip_out = refs[LAYER:]
     for i in range(LAYER):
-        stay_out[i] = refs[i][0]
-        core_out[0, i] = refs[i][1]
-        chip_out[i] = refs[i][2]
-        core_out[1, i] = refs[i][3]
+        for r in range(LAYER):
+            refs[LAYER + r][i] = refs[i][r]
 
 
 def by_place(*blocks):
-    shape = blocks[0].shape
     return pl.pallas_call(
         by_place_kernel,
-        out_shape=[jax.ShapeDtypeStruct(shape, blocks[0].dtype) for shape in (shape, (2,) + shape, shape)],
+        out_shape=[jax.ShapeDtypeStruct(blocks[0].shape, blocks[0].dtype)] * LAYER,
         in_specs=[VMEM] * LAYER,
-        out_specs=[VMEM] * 3,
+        out_specs=[VMEM] * LAYER,
         compiler_params=pltpu.CompilerParams(vmem_limit_bytes=8 * MIB),
     )(*blocks)
 
@@ -333,24 +326,51 @@
     )(arrived, hidden_rows, held(scales), far(first), far(second))
 
 
-def combine_kernel(hidden_ref, mixed_ref, scales_ref, blending_ref, brought_ref, out_ref):
-    heads = mixed_ref.shape[0]
-    mixed = jnp.concatenate([mixed_ref[h].astype(jnp.float32) for h in range(heads)], axis=1)
-    resid = hidden_ref[...].astype(jnp.float32) + scales_ref[0:1, :] * mixed
-    count = resid.shape[0]
-    mixture = jnp.dot(blending_ref[...], brought_ref[...], preferred_element_type=jnp.float32)
-    mixture = mixture[:count] + (mixture[count : 2 * count] + mixture[2 * count :])
-    out_ref[...] = (resid + scales_ref[3:4, :] * mixture).astype(jnp.bfloat16)
-
-
-def combine(hidden, mixed, scales, blending, brought):
+def residual_kernel(me_ref, *refs):
+    *block_refs, hidden_ref, scales_ref, out_ref = refs
+    lanes = block_refs[0].shape[2]
+    for r in range(LAYER):
+        for i in range(LAYER):
+            head = me_ref[0] ^ (LAYER * i + r)
+            columns = pl.ds(pl.multiple_of(head * lanes, lanes), lanes)
+            mixed = block_refs[r][i].astype(jnp.float32)
+            out_ref[:, columns] = hidden_ref[:, columns].astype(jnp.float32) + scales_ref[0:1, columns] * mixed
+
+
+def residual(me, blocks, hidden, scales):
+    return pl.pallas_call(
+        residual_kernel,
+        out_shape=pltpu.VMEM(hidden.shape, jnp.float32),
+        in_specs=[SMEM] + [VMEM] * (LAYER + 2),
+        out_specs=VMEM,
+        compiler_params=pltpu.CompilerParams(vmem_limit_bytes=8 * MIB),
+    )(me, *blocks, hidden, held(scales))
+
+
+def combine_kernel(resid_ref, scales_ref, blending_ref, brought_ref, out_hbm, out, done):
+    count, width = out.shape
+    step = width // done.shape[0]
+    copies = []
+    for c in range(done.shape[0]):
+        columns = slice(c * step, (c + 1) * step)
+        mixture = jnp.dot(blending_ref[...], brought_ref[:, columns], preferred_element_type=jnp.float32)
+        mixture = mixture[:count] + (mixture[count : 2 * count] + mixture[2 * count :])
+        out[:, columns] = (resid_ref[:, columns] + scales_ref[3:4, columns] * mixture).astype(jnp.bfloat16)
+        copies.append(pltpu.make_async_copy(out.at[:, columns], out_hbm.at[:, columns], done.at[c]))
+        copies[-1].start()
+    for copy in copies:
+        copy.wait()
+
+
+def combine(resid, scales, blending, brought):
     return pl.pallas_call(
         combine_kernel,
-        out_shape=jax.ShapeDtypeStruct(hidden.shape, jnp.bfloat16),
-        in_specs=[VMEM] * 5,
-        out_specs=VMEM,
-        compiler_params=pltpu.CompilerParams(vmem_limit_bytes=24 * MIB),
-    )(hidden, mixed, held(scales), held(blending), brought)
+        out_shape=pltpu.HBM(resid.shape, jnp.bfloat16),
+        in_specs=[VMEM] * 4,
+        out_specs=HBM,
+        scratch_shapes=[pltpu.VMEM(resid.shape, jnp.bfloat16), pltpu.SemaphoreType.DMA((4,))],
+        compiler_params=pltpu.CompilerParams(vmem_limit_bytes=16 * MIB),
+    )(held(resid), held(scales), held(blending), brought)
 
 
 def partner(array, step):
@@ -358,19 +378,17 @@
     return lax.ppermute(array, "seq", [(i, i ^ step) for i in range(devices)])
 
 
-def within_layer(stay, core, chip):
-    core = partner(core, 1)
-    chip = partner(chip, 2)
-    return stay, core[0], chip, partner(core[1], 2)
-
-
-def across_layers(blocks):
-    return [partner(block, LAYER * (i + 1)) for i, block in enumerate(blocks)]
+def within_layer(stay, *blocks):
+    return [stay] + [partner(block, r + 1) for r, block in enumerate(blocks)]
+
+
+def across_layers(stay, *blocks):
+    return [stay] + [partner(block, LAYER * (i + 1)) for i, block in enumerate(blocks)]
 
 
 def gather_codes(code):
-    layer = jnp.stack([code] + [partner(code, r) for r in range(1, LAYER)])
-    return jnp.stack([layer] + [partner(layer, LAYER * i) for i in range(1, LAYER)])
+    layer = jnp.stack(within_layer(*[code] * LAYER))
+    return jnp.stack(across_layers(*[layer] * LAYER))
 
 
 def direct_body(hidden_in, qkv, modulation, route_weight, expert_ids, slots, w_in, w_out):
@@ -380,24 +398,24 @@
     ids, slot_rows = expert_ids[0].T, slots[0].T
     owned = exchange(qkv[0])
     codes = gather_codes(slot_code(ids, slot_rows))
-    scales, stay, core, chip, blending = prepare(
+    scales, blending, *here = prepare(
         me, hidden_in[0], modulation[0], ids, slot_rows, route_weight[0].T, triple // 3
     )
-    here = within_layer(stay, core, chip)
+    here = within_layer(*here)
     near, *away = by_layer(*here)
     near, *away, owned = lax.optimization_barrier((partner(near, LAYER), *away, owned))
     away = [near, partner(away[0], 2 * LAYER), partner(away[1], 3 * LAYER)]
     to_experts, attended = attention(me, codes, owned)
     arrived = exchange(to_experts)
     hidden_rows, attended = lax.optimization_barrier((assemble(me, here, away), attended))
-    here, *away = restore(me, attended)
+    stay, *away = restore(me, attended)
     *away, arrived = lax.optimization_barrier((*away, arrived))
-    away = across_layers(away)
+    away = across_layers(stay, *away)
     computed = expert(arrived, hidden_rows, scales, w_in, w_out)
     *away, computed = lax.optimization_barrier((*away, computed))
     brought = exchange(computed.reshape(devices, CAP, -1))
-    mixed = assemble(me, within_layer(*by_place(here, *away)))
-    return combine(hidden_in[0], mixed, scales, blending, brought.reshape(devices * CAP, -1))[None]
+    resid = residual(me, within_layer(*by_place(*away)), hidden_in[0], scales)
+    return combine(resid, scales, blending, brought.reshape(devices * CAP, -1))[None]
 
 
 def attend(queries, key_rows, values):

time: 116 us -> 116 us (level)
  starting transfers between devices: 43 us -> 40.7 us
  waiting for transfers between devices: 42.6 us -> 44.7 us
    ppermute x18, starting transfers between devices: 26.3 us -> 24 us  [partner(): return lax.ppermute(array, 'seq', [(i, i ^ step) for i in range(devices)])]
where the time goes in v5:
time: 116 us
  waiting for transfers between devices  44.7 us (39%)
  starting transfers between devices  40.7 us (35%)
  Pallas kernels  28.2 us (24%)
  local copies, waits for them, and re-layouts  2.03 us (2%)
    ppermute x18, waiting for transfers between devices, partner(): return lax.ppermute(array, 'seq', [(i, i ^ step) for i in range(devices)])  29 us
    ppermute x18, starting transfers between devices, partner(): return lax.ppermute(array, 'seq', [(i, i ^ step) for i in range(devices)])  24 us
    pallas_call x1, Pallas kernels, expert(): pl.pallas_call(functools.partial(expert_kernel, block), out_shape=jax.Sha...  22.2 us
    all_to_all x3, starting transfers between devices, exchange(): return lax.all_to_all(array, 'seq', split_axis=0, concat_axis=0, tiled=True)  16.7 us
    all_to_all x3, waiting for transfers between devices, exchange(): return lax.all_to_all(array, 'seq', split_axis=0, concat_axis=0, tiled=True)  15.7 us
    pallas_call x1, Pallas kernels, attention(): pl.pallas_call(attention_kernel, out_shape=[jax.ShapeDtypeStruct((EXPERTS...  2.72 us
  transfers between devices with their start and end apart: 21, of which 10 were waited for; matrix products, arithmetic and copies ran while one was open for 0% of the time, Pallas kernels for 23%

profile of v5, /device:TPU:0, one launch (start us, length us, event | category | flops | bytes accessed | tf_op | source)
XLA Modules:
  0.0 115.8 jit_solution(10154618069908591506)
XLA Ops:
  0.0 7.4 %all-to-all-start = ((bf16[16,128,384]{2,1,0:T(8,128)(2,1)}), bf16[16,128,384]{2,1,0:T(8,128)(2,1)S(1)}, u32[]{:S(2)}, u32[]{:S(2)}) async-start(bf16[16,128,384]{2,1,0:T(8,128)(2,1)} %bitcast.33), calls=%async_computation | async-start | bytes 3145728 | tf_op jit(solution)/shard_map/all_to_all | solution.py:32
  9.4 1.3 %shard_map.82 = (f32[4,2048]{1,0:T(4,128)S(1)}, bf16[384,128]{1,0:T(8,128)(2,1)S(1)}, bf16[4,128,128]{2,1,0:T(8,128)(2,1)S(1)}, bf16[4,128,128]{2,1,0:T(8,128)(2...) custom-call(s32[1]{0:T(128)} %bitcast.me_ref, bf16[128,2048]{1,0:T(8,128)(2,1)} %bitcast.27, ...), custom_call_target="tpu_custom_call" | custom-call | flops 67108864 | bytes 4194304 | tf_op jit(solution)/shard_map/pallas_call | solution.py:93
  11.2 1.7 %collective-permute-start.1 = (bf16[4,128,128]{2,1,0:T(8,128)(2,1)S(1)}, bf16[4,128,128]{2,1,0:T(8,128)(2,1)S(1)}, u32[]{:S(2)}, u32[]{:S(2)}) collective-permute-start(bf16[4,128,128]{2,1,0:T(8,128)(2,1)S(1)} %get-tuple-element.41), channel_id=1, source_target_pairs={{0,2},{1,3},{2,0},{3,1},{4,6},{5,7},{6,4},{7,5},{8,10},{9,11},{10,... | collective-permute-start | bytes 393224 | tf_op jit(solution)/shard_map/ppermute | solution.py:378
  12.9 11.6 %collective-permute-done.1.refs_2_ = bf16[4,128,128]{2,1,0:T(8,128)(2,1)S(1)} collective-permute-done((bf16[4,128,128]{2,1,0:T(8,128)(2,1)S(1)}, bf16[4,128,128]{2,1,0:T(8,128)(2,1)S(1)}, u32[]{:S(2)}, u32[]{:S(2)}) %collective-permute-start.1) | collective-permute-done | bytes 131104 | tf_op jit(solution)/shard_map/ppermute | solution.py:378
  24.5 3.6 %collective-permute-done.2.refs_3_ = bf16[4,128,128]{2,1,0:T(8,128)(2,1)S(1)} collective-permute-done((bf16[4,128,128]{2,1,0:T(8,128)(2,1)S(1)}, bf16[4,128,128]{2,1,0:T(8,128)(2,1)S(1)}, u32[]{:S(2)}, u32[]{:S(2)}) %collective-permute-start.2) | collective-permute-done | bytes 131104 | tf_op jit(solution)/shard_map/ppermute | solution.py:378
  28.3 2.1 %collective-permute-start.7 = (s32[2,128]{1,0:T(2,128)S(1)}, s32[2,128]{1,0:T(2,128)S(1)}, u32[]{:S(2)}, u32[]{:S(2)}) collective-permute-start(s32[2,128]{1,0:T(2,128)S(1)} %compare_select_fusion), channel_id=1, source_target_pairs={{0,2},{1,3},{2,0},{3,1},{4,6},{5,7},{6,4},{7,5},{8,10},{9,11},{10,... | collective-permute-start | bytes 3080 | tf_op jit(solution)/shard_map/ppermute | solution.py:378
  31.9 4.1 %collective-permute-start.10 = (s32[4,2,128]{2,1,0:T(2,128)S(1)}, s32[4,2,128]{2,1,0:T(2,128)S(1)}, u32[]{:S(2)}, u32[]{:S(2)}) collective-permute-start(s32[4,2,128]{2,1,0:T(2,128)S(1)} %pad_add_fusion.1), channel_id=1, source_target_pairs={{0,8},{1,9},{2,10},{3,11},{4,12},{5,13},{6,14},{7,15},{8,0},{9,1},... | collective-permute-start | bytes 12296 | tf_op jit(solution)/shard_map/ppermute | solution.py:378
  36.4 1.2 %collective-permute-start.11 = (s32[4,2,128]{2,1,0:T(2,128)S(1)}, s32[4,2,128]{2,1,0:T(2,128)S(1)}, u32[]{:S(2)}, u32[]{:S(2)}) collective-permute-start(s32[4,2,128]{2,1,0:T(2,128)S(1)} %pad_add_fusion.1), channel_id=1, source_target_pairs={{0,12},{1,13},{2,14},{3,15},{4,8},{5,9},{6,10},{7,11},{8,4},{9,5},... | collective-permute-start | bytes 12296 | tf_op jit(solution)/shard_map/ppermute | solution.py:378
  37.5 1.9 %all-to-all-done.rows_ref = bf16[16,128,384]{2,1,0:T(8,128)(2,1)S(1)} async-done(((bf16[16,128,384]{2,1,0:T(8,128)(2,1)}), bf16[16,128,384]{2,1,0:T(8,128)(2,1)S(1)}, u32[]{:S(2)}, u32[]{:S(2)}) %all-to-all-start) | async-done | bytes 1572896 | tf_op jit(solution)/shard_map/all_to_all | solution.py:32
  39.4 7.5 %collective-permute-start.4 = (bf16[4,128,128]{2,1,0:T(8,128)(2,1)S(1)}, bf16[4,128,128]{2,1,0:T(8,128)(2,1)S(1)}, u32[]{:S(2)}, u32[]{:S(2)}) collective-permute-start(bf16[4,128,128]{2,1,0:T(8,128)(2,1)S(1)} %get-tuple-element.47), channel_id=1, source_target_pairs={{0,8},{1,9},{2,10},{3,11},{4,12},{5,13},{6,14},{7,15},{8,0},{9,1},... | collective-permute-start | bytes 393224 | tf_op jit(solution)/shard_map/ppermute | solution.py:378
  47.0 2.7 %shard_map.85 = (bf16[16,128,128]{2,1,0:T(8,128)(2,1)}, bf16[16,128,128]{2,1,0:T(8,128)(2,1)S(1)}) custom-call(s32[1]{0:T(128)} %bitcast.me_ref, s32[4,4,2,128]{3,2,1,0:T(2,128)S(1)} %pad_add_fusion.codes_ref, bf16[16,128,384]{2,1,0:T(8,128)(2,1)S(1)} %all-to-all-done.rows_ref), custom_call_target="tpu_custom_call" | custom-call | tf_op jit(solution)/shard_map/pallas_call | solution.py:207
  49.7 5.2 %all-to-all-start.1 = ((bf16[16,128,128]{2,1,0:T(8,128)(2,1)}), bf16[16,128,128]{2,1,0:T(8,128)(2,1)S(1)}, u32[]{:S(2)}, u32[]{:S(2)}) async-start(bf16[16,128,128]{2,1,0:T(8,128)(2,1)} %get-tuple-element.56), calls=%async_computation.1 | async-start | bytes 1048576 | tf_op jit(solution)/shard_map/all_to_all | solution.py:32
  54.9 1.7 %collective-permute-done.4.refs_5_ = bf16[4,128,128]{2,1,0:T(8,128)(2,1)S(1)} collective-permute-done((bf16[4,128,128]{2,1,0:T(8,128)(2,1)S(1)}, bf16[4,128,128]{2,1,0:T(8,128)(2,1)S(1)}, u32[]{:S(2)}, u32[]{:S(2)}) %collective-permute-start.4) | collective-permute-done | bytes 131104 | tf_op jit(solution)/shard_map/ppermute | solution.py:378
  56.9 12.4 %all-to-all-done.1.arrived_ref = bf16[16,128,128]{2,1,0:T(8,128)(2,1)S(1)} async-done(((bf16[16,128,128]{2,1,0:T(8,128)(2,1)}), bf16[16,128,128]{2,1,0:T(8,128)(2,1)S(1)}, u32[]{:S(2)}, u32[]{:S(2)}) %all-to-all-start.1) | async-done | bytes 524320 | tf_op jit(solution)/shard_map/all_to_all | solution.py:32
  69.3 1.1 collective-permute-start.12
  70.4 1.2 %collective-permute-start.13 = (bf16[4,128,128]{2,1,0:T(8,128)(2,1)S(1)}, bf16[4,128,128]{2,1,0:T(8,128)(2,1)S(1)}, u32[]{:S(2)}, u32[]{:S(2)}) collective-permute-start(bf16[4,128,128]{2,1,0:T(8,128)(2,1)S(1)} %get-tuple-element.58), channel_id=1, source_target_pairs={{0,8},{1,9},{2,10},{3,11},{4,12},{5,13},{6,14},{7,15},{8,0},{9,1},... | collective-permute-start | bytes 393224 | tf_op jit(solution)/shard_map/ppermute | solution.py:378
  71.6 2.1 %collective-permute-start.14 = (bf16[4,128,128]{2,1,0:T(8,128)(2,1)S(1)}, bf16[4,128,128]{2,1,0:T(8,128)(2,1)S(1)}, u32[]{:S(2)}, u32[]{:S(2)}) collective-permute-start(bf16[4,128,128]{2,1,0:T(8,128)(2,1)S(1)} %get-tuple-element.59), channel_id=1, source_target_pairs={{0,12},{1,13},{2,14},{3,15},{4,8},{5,9},{6,10},{7,11},{8,4},{9,5},... | collective-permute-start | bytes 393224 | tf_op jit(solution)/shard_map/ppermute | solution.py:378
  73.7 22.2 %shard_map.87 = bf16[128,2048]{1,0:T(8,128)(2,1)} custom-call(bf16[16,128,128]{2,1,0:T(8,128)(2,1)S(1)} %all-to-all-done.1.arrived_ref, bf16[16,128,128]{2,1,0:T(8,128)(2,1)S(1)} %shard_map.84.hidden_ref, f32[4,2048]{1,0:T(4,128)S(1)} %get-tuple-element.62.scales_ref.refs_5_, bf16[2048,8192]{1,0:T(8,128)(2,1)} %first_hbm.1, bf16[8192,2048]{1,0:T(8,128)(2,1)} %second_hbm.1), custom_call_target="tpu_custom_call" | custom-call | flops 137438953472 | bytes 67108864 | tf_op jit(solution)/shard_map/pallas_call | solution.py:309
  96.0 4.1 %all-to-all-start.2 = ((bf16[16,8,2048]{2,1,0:T(8,128)(2,1)}), bf16[16,8,2048]{2,1,0:T(8,128)(2,1)S(1)}, u32[]{:S(2)}, u32[]{:S(2)}) async-start(bf16[16,8,2048]{2,1,0:T(8,128)(2,1)} %bitcast.20), calls=%async_computation.2 | async-start | bytes 1048576 | tf_op jit(solution)/shard_map/all_to_all | solution.py:32
  100.6 1.7 %collective-permute-start.16 = (bf16[4,128,128]{2,1,0:T(8,128)(2,1)S(1)}, bf16[4,128,128]{2,1,0:T(8,128)(2,1)S(1)}, u32[]{:S(2)}, u32[]{:S(2)}) collective-permute-start(bf16[4,128,128]{2,1,0:T(8,128)(2,1)S(1)} %get-tuple-element.69), channel_id=1, source_target_pairs={{0,2},{1,3},{2,0},{3,1},{4,6},{5,7},{6,4},{7,5},{8,10},{9,11},{10,... | collective-permute-start | bytes 393224 | tf_op jit(solution)/shard_map/ppermute | solution.py:378
  102.3 8.5 %collective-permute-done.16.refs_2_ = bf16[4,128,128]{2,1,0:T(8,128)(2,1)S(1)} collective-permute-done((bf16[4,128,128]{2,1,0:T(8,128)(2,1)S(1)}, bf16[4,128,128]{2,1,0:T(8,128)(2,1)S(1)}, u32[]{:S(2)}, u32[]{:S(2)}) %collective-permute-start.16) | collective-permute-done | bytes 131104 | tf_op jit(solution)/shard_map/ppermute | solution.py:378
  110.8 2.1 %collective-permute-done.17.refs_3_ = bf16[4,128,128]{2,1,0:T(8,128)(2,1)S(1)} collective-permute-done((bf16[4,128,128]{2,1,0:T(8,128)(2,1)S(1)}, bf16[4,128,128]{2,1,0:T(8,128)(2,1)S(1)}, u32[]{:S(2)}, u32[]{:S(2)}) %collective-permute-start.17) | collective-permute-done | bytes 131104 | tf_op jit(solution)/shard_map/ppermute | solution.py:378
  113.2 1.4 %all-to-all-done.2 = bf16[16,8,2048]{2,1,0:T(8,128)(2,1)S(1)} async-done(((bf16[16,8,2048]{2,1,0:T(8,128)(2,1)}), bf16[16,8,2048]{2,1,0:T(8,128)(2,1)S(1)}, u32[]{:S(2)}, u32[]{:S(2)}) %all-to-all-start.2) | async-done | bytes 524320 | tf_op jit(solution)/shard_map/all_to_all | solution.py:32
  114.6 1.2 %shard_map.90 = bf16[128,2048]{1,0:T(8,128)(2,1)} custom-call(f32[128,2048]{1,0:T(8,128)S(1)} %shard_map.89.resid_ref, f32[4,2048]{1,0:T(4,128)S(1)} %get-tuple-element.62.scales_ref.refs_5_, bf16[384,128]{1,0:T(8,128)(2,1)S(1)} %get-tuple-element.71.blending_ref, bf16[128,2048]{1,0:T(8,128)(2,1)S(1)} %bitcast.29), custom_call_target="tpu_custom_call" | custom-call | tf_op jit(solution)/shard_map/pallas_call | solution.py:366
  (39 shorter events, 5.8 us)
Async XLA Ops:
  0.0 39.4 %all-to-all-start = ((bf16[16,128,384]{2,1,0:T(8,128)(2,1)}), bf16[16,128,384]{2,1,0:T(8,128)(2,1)S(1)}, u32[]{:S(2)}, u32[]{:S(2)}) async-start(bf16[16,128,384]{2,1,0:T(8,128)(2,1)} %bitcast.33), calls=%async_computation | async-start | bytes 3145728 | tf_op jit(solution)/shard_map/all_to_all | solution.py:32
  7.4 0.7 copy-start.1
  8.1 0.7 copy-start.2
  10.8 2.2 %collective-permute-start = (bf16[4,128,128]{2,1,0:T(8,128)(2,1)S(1)}, bf16[4,128,128]{2,1,0:T(8,128)(2,1)S(1)}, u32[]{:S(2)}, u32[]{:S(2)}) collective-permute-start(bf16[4,128,128]{2,1,0:T(8,128)(2,1)S(1)} %get-tuple-element.40), channel_id=1, source_target_pairs={{0,1},{1,0},{2,3},{3,2},{4,5},{5,4},{6,7},{7,6},{8,9},{9,8},{10,11... | collective-permute-start | bytes 393224 | tf_op jit(solution)/shard_map/ppermute | solution.py:378
  11.2 13.3 %collective-permute-start.1 = (bf16[4,128,128]{2,1,0:T(8,128)(2,1)S(1)}, bf16[4,128,128]{2,1,0:T(8,128)(2,1)S(1)}, u32[]{:S(2)}, u32[]{:S(2)}) collective-permute-start(bf16[4,128,128]{2,1,0:T(8,128)(2,1)S(1)} %get-tuple-element.41), channel_id=1, source_target_pairs={{0,2},{1,3},{2,0},{3,1},{4,6},{5,7},{6,4},{7,5},{8,10},{9,11},{10,... | collective-permute-start | bytes 393224 | tf_op jit(solution)/shard_map/ppermute | solution.py:378
  12.9 15.2 %collective-permute-start.2 = (bf16[4,128,128]{2,1,0:T(8,128)(2,1)S(1)}, bf16[4,128,128]{2,1,0:T(8,128)(2,1)S(1)}, u32[]{:S(2)}, u32[]{:S(2)}) collective-permute-start(bf16[4,128,128]{2,1,0:T(8,128)(2,1)S(1)} %get-tuple-element.42), channel_id=1, source_target_pairs={{0,3},{1,2},{2,1},{3,0},{4,7},{5,6},{6,5},{7,4},{8,11},{9,10},{10,... | collective-permute-start | bytes 393224 | tf_op jit(solution)/shard_map/ppermute | solution.py:378
  28.1 9.4 %collective-permute-start.3 = (bf16[4,128,128]{2,1,0:T(8,128)(2,1)S(1)}, bf16[4,128,128]{2,1,0:T(8,128)(2,1)S(1)}, u32[]{:S(2)}, u32[]{:S(2)}) collective-permute-start(bf16[4,128,128]{2,1,0:T(8,128)(2,1)S(1)} %get-tuple-element.43), channel_id=1, source_target_pairs={{0,4},{1,5},{2,6},{3,7},{4,0},{5,1},{6,2},{7,3},{8,12},{9,13},{10,... | collective-permute-start | bytes 393224 | tf_op jit(solution)/shard_map/ppermute | solution.py:378
  28.2 3.1 %collective-permute-start.8 = (s32[2,128]{1,0:T(2,128)S(1)}, s32[2,128]{1,0:T(2,128)S(1)}, u32[]{:S(2)}, u32[]{:S(2)}) collective-permute-start(s32[2,128]{1,0:T(2,128)S(1)} %compare_select_fusion), channel_id=1, source_target_pairs={{0,3},{1,2},{2,1},{3,0},{4,7},{5,6},{6,5},{7,4},{8,11},{9,10},{10,... | collective-permute-start | bytes 3080 | tf_op jit(solution)/shard_map/ppermute | solution.py:378
  28.3 3.7 %collective-permute-start.7 = (s32[2,128]{1,0:T(2,128)S(1)}, s32[2,128]{1,0:T(2,128)S(1)}, u32[]{:S(2)}, u32[]{:S(2)}) collective-permute-start(s32[2,128]{1,0:T(2,128)S(1)} %compare_select_fusion), channel_id=1, source_target_pairs={{0,2},{1,3},{2,0},{3,1},{4,6},{5,7},{6,4},{7,5},{8,10},{9,11},{10,... | collective-permute-start | bytes 3080 | tf_op jit(solution)/shard_map/ppermute | solution.py:378
  30.4 1.6 %collective-permute-start.6 = (s32[2,128]{1,0:T(2,128)S(1)}, s32[2,128]{1,0:T(2,128)S(1)}, u32[]{:S(2)}, u32[]{:S(2)}) collective-permute-start(s32[2,128]{1,0:T(2,128)S(1)} %compare_select_fusion), channel_id=1, source_target_pairs={{0,1},{1,0},{2,3},{3,2},{4,5},{5,4},{6,7},{7,6},{8,9},{9,8},{10,11... | collective-permute-start | bytes 3080 | tf_op jit(solution)/shard_map/ppermute | solution.py:378
  31.9 15.0 %collective-permute-start.10 = (s32[4,2,128]{2,1,0:T(2,128)S(1)}, s32[4,2,128]{2,1,0:T(2,128)S(1)}, u32[]{:S(2)}, u32[]{:S(2)}) collective-permute-start(s32[4,2,128]{2,1,0:T(2,128)S(1)} %pad_add_fusion.1), channel_id=1, source_target_pairs={{0,8},{1,9},{2,10},{3,11},{4,12},{5,13},{6,14},{7,15},{8,0},{9,1},... | collective-permute-start | bytes 12296 | tf_op jit(solution)/shard_map/ppermute | solution.py:378
  36.0 10.9 %collective-permute-start.9 = (s32[4,2,128]{2,1,0:T(2,128)S(1)}, s32[4,2,128]{2,1,0:T(2,128)S(1)}, u32[]{:S(2)}, u32[]{:S(2)}) collective-permute-start(s32[4,2,128]{2,1,0:T(2,128)S(1)} %pad_add_fusion.1), channel_id=1, source_target_pairs={{0,4},{1,5},{2,6},{3,7},{4,0},{5,1},{6,2},{7,3},{8,12},{9,13},{10,... | collective-permute-start | bytes 12296 | tf_op jit(solution)/shard_map/ppermute | solution.py:378
  36.4 10.6 %collective-permute-start.11 = (s32[4,2,128]{2,1,0:T(2,128)S(1)}, s32[4,2,128]{2,1,0:T(2,128)S(1)}, u32[]{:S(2)}, u32[]{:S(2)}) collective-permute-start(s32[4,2,128]{2,1,0:T(2,128)S(1)} %pad_add_fusion.1), channel_id=1, source_target_pairs={{0,12},{1,13},{2,14},{3,15},{4,8},{5,9},{6,10},{7,11},{8,4},{9,5},... | collective-permute-start | bytes 12296 | tf_op jit(solution)/shard_map/ppermute | solution.py:378
  39.4 17.1 %collective-permute-start.4 = (bf16[4,128,128]{2,1,0:T(8,128)(2,1)S(1)}, bf16[4,128,128]{2,1,0:T(8,128)(2,1)S(1)}, u32[]{:S(2)}, u32[]{:S(2)}) collective-permute-start(bf16[4,128,128]{2,1,0:T(8,128)(2,1)S(1)} %get-tuple-element.47), channel_id=1, source_target_pairs={{0,8},{1,9},{2,10},{3,11},{4,12},{5,13},{6,14},{7,15},{8,0},{9,1},... | collective-permute-start | bytes 393224 | tf_op jit(solution)/shard_map/ppermute | solution.py:378
  46.9 9.7 %collective-permute-start.5 = (bf16[4,128,128]{2,1,0:T(8,128)(2,1)S(1)}, bf16[4,128,128]{2,1,0:T(8,128)(2,1)S(1)}, u32[]{:S(2)}, u32[]{:S(2)}) collective-permute-start(bf16[4,128,128]{2,1,0:T(8,128)(2,1)S(1)} %get-tuple-element.48), channel_id=1, source_target_pairs={{0,12},{1,13},{2,14},{3,15},{4,8},{5,9},{6,10},{7,11},{8,4},{9,5},... | collective-permute-start | bytes 393224 | tf_op jit(solution)/shard_map/ppermute | solution.py:378
  49.7 19.7 %all-to-all-start.1 = ((bf16[16,128,128]{2,1,0:T(8,128)(2,1)}), bf16[16,128,128]{2,1,0:T(8,128)(2,1)S(1)}, u32[]{:S(2)}, u32[]{:S(2)}) async-start(bf16[16,128,128]{2,1,0:T(8,128)(2,1)} %get-tuple-element.56), calls=%async_computation.1 | async-start | bytes 1048576 | tf_op jit(solution)/shard_map/all_to_all | solution.py:32
  69.3 26.6 %collective-permute-start.12 = (bf16[4,128,128]{2,1,0:T(8,128)(2,1)S(1)}, bf16[4,128,128]{2,1,0:T(8,128)(2,1)S(1)}, u32[]{:S(2)}, u32[]{:S(2)}) collective-permute-start(bf16[4,128,128]{2,1,0:T(8,128)(2,1)S(1)} %get-tuple-element.57), channel_id=1, source_target_pairs={{0,4},{1,5},{2,6},{3,7},{4,0},{5,1},{6,2},{7,3},{8,12},{9,13},{10,... | collective-permute-start | bytes 393224 | tf_op jit(solution)/shard_map/ppermute | solution.py:378
  70.4 25.5 %collective-permute-start.13 = (bf16[4,128,128]{2,1,0:T(8,128)(2,1)S(1)}, bf16[4,128,128]{2,1,0:T(8,128)(2,1)S(1)}, u32[]{:S(2)}, u32[]{:S(2)}) collective-permute-start(bf16[4,128,128]{2,1,0:T(8,128)(2,1)S(1)} %get-tuple-element.58), channel_id=1, source_target_pairs={{0,8},{1,9},{2,10},{3,11},{4,12},{5,13},{6,14},{7,15},{8,0},{9,1},... | collective-permute-start | bytes 393224 | tf_op jit(solution)/shard_map/ppermute | solution.py:378
  71.6 24.4 %collective-permute-start.14 = (bf16[4,128,128]{2,1,0:T(8,128)(2,1)S(1)}, bf16[4,128,128]{2,1,0:T(8,128)(2,1)S(1)}, u32[]{:S(2)}, u32[]{:S(2)}) collective-permute-start(bf16[4,128,128]{2,1,0:T(8,128)(2,1)S(1)} %get-tuple-element.59), channel_id=1, source_target_pairs={{0,12},{1,13},{2,14},{3,15},{4,8},{5,9},{6,10},{7,11},{8,4},{9,5},... | collective-permute-start | bytes 393224 | tf_op jit(solution)/shard_map/ppermute | solution.py:378
  73.7 39.1 %copy-start = (bf16[1,128,2048]{2,1,0:T(8,128)(2,1)S(1)}, bf16[1,128,2048]{2,1,0:T(8,128)(2,1)}, u32[]{:S(2)}) copy-start(bf16[1,128,2048]{2,1,0:T(8,128)(2,1)} %param.8) | copy-start | bytes 1572868
  96.0 18.6 %all-to-all-start.2 = ((bf16[16,8,2048]{2,1,0:T(8,128)(2,1)}), bf16[16,8,2048]{2,1,0:T(8,128)(2,1)S(1)}, u32[]{:S(2)}, u32[]{:S(2)}) async-start(bf16[16,8,2048]{2,1,0:T(8,128)(2,1)} %bitcast.20), calls=%async_computation.2 | async-start | bytes 1048576 | tf_op jit(solution)/shard_map/all_to_all | solution.py:32
  100.2 2.2 %collective-permute-start.15 = (bf16[4,128,128]{2,1,0:T(8,128)(2,1)S(1)}, bf16[4,128,128]{2,1,0:T(8,128)(2,1)S(1)}, u32[]{:S(2)}, u32[]{:S(2)}) collective-permute-start(bf16[4,128,128]{2,1,0:T(8,128)(2,1)S(1)} %get-tuple-element.68), channel_id=1, source_target_pairs={{0,1},{1,0},{2,3},{3,2},{4,5},{5,4},{6,7},{7,6},{8,9},{9,8},{10,11... | collective-permute-start | bytes 393224 | tf_op jit(solution)/shard_map/ppermute | solution.py:378
  100.6 10.2 %collective-permute-start.16 = (bf16[4,128,128]{2,1,0:T(8,128)(2,1)S(1)}, bf16[4,128,128]{2,1,0:T(8,128)(2,1)S(1)}, u32[]{:S(2)}, u32[]{:S(2)}) collective-permute-start(bf16[4,128,128]{2,1,0:T(8,128)(2,1)S(1)} %get-tuple-element.69), channel_id=1, source_target_pairs={{0,2},{1,3},{2,0},{3,1},{4,6},{5,7},{6,4},{7,5},{8,10},{9,11},{10,... | collective-permute-start | bytes 393224 | tf_op jit(solution)/shard_map/ppermute | solution.py:378
  102.3 10.6 %collective-permute-start.17 = (bf16[4,128,128]{2,1,0:T(8,128)(2,1)S(1)}, bf16[4,128,128]{2,1,0:T(8,128)(2,1)S(1)}, u32[]{:S(2)}, u32[]{:S(2)}) collective-permute-start(bf16[4,128,128]{2,1,0:T(8,128)(2,1)S(1)} %get-tuple-element.70), channel_id=1, source_target_pairs={{0,3},{1,2},{2,1},{3,0},{4,7},{5,6},{6,5},{7,4},{8,11},{9,10},{10,... | collective-permute-start | bytes 393224 | tf_op jit(solution)/shard_map/ppermute | solution.py:378
  (1 other events, 0.7 us)

commit v6 on v5

--- a/solution.py
+++ b/solution.py
@@ -155,7 +155,9 @@
     )(me, *here, *away)
 
 
-def attention_kernel(me_ref, codes_ref, rows_ref, expert_out, attended_out, framed, attended, codes):
+def attention_kernel(me_ref, codes_ref, rows_ref, *refs):
+    *outs, framed, attended, codes = refs
+    slot_outs, place_outs = outs[:LAYER], outs[LAYER:]
     sources, count, triple = rows_ref.shape
     width = triple // 3
     places = count // FRAMES
@@ -185,60 +187,48 @@
         (((1,), (1,)), ((), ())),
         preferred_element_type=jnp.float32,
     )
-    slot = lax.broadcasted_iota(jnp.int32, (EXPERTS * CAP, count), 0).astype(jnp.float32)
+    slot = lax.broadcasted_iota(jnp.int32, (EXPERTS * CAP, count), 0) ^ me_ref[0] * CAP
+    slot = slot.astype(jnp.float32)
     for c in range(sources // 2):
         pair = []
         for s in (2 * c, 2 * c + 1):
             code = by_frame[s * CODE_ROWS : s * CODE_ROWS + 2]
             hit = (code[0:1] == slot) | (code[1:2] == slot)
             rows = attended[:, s * places : (s + 1) * places, :].reshape(count, width).astype(jnp.bfloat16)
-            attended_out[s] = rows
             rows = jnp.dot(
                 jnp.where(hit, 1.0, 0.0).astype(jnp.bfloat16), rows, preferred_element_type=jnp.float32
             )
-            pair.append(rows.reshape(EXPERTS, CAP, width))
-        expert_out[:, 2 * c * CAP : 2 * (c + 1) * CAP, :] = jnp.concatenate(pair, axis=1).astype(jnp.bfloat16)
+            pair.append(rows.reshape(EXPERTS // LAYER, LAYER, CAP, width))
+        pair = jnp.concatenate(pair, axis=2).astype(jnp.bfloat16)
+        for r, out in enumerate(slot_outs):
+            out[:, 2 * c * CAP : 2 * (c + 1) * CAP, :] = pair[:, r]
+    back = frame_order(count, True)
+    for i, out in enumerate(place_outs):
+        for r in range(LAYER):
+            start = pl.multiple_of((me_ref[0] ^ (LAYER * i + r)) * places, places)
+            rows = attended[:, pl.ds(start, places), :].reshape(count, width).astype(jnp.bfloat16)
+            out[r] = jnp.dot(back, rows, preferred_element_type=jnp.float32).astype(jnp.bfloat16)
 
 
 def attention(me, codes, rows):
     sources, count, triple = rows.shape
     width = triple // 3
     by_frame = (FRAMES, sources * count // FRAMES)
-    return pl.pallas_call(
+    shapes = [(EXPERTS // LAYER, sources * CAP, width)] * LAYER + [(sources // LAYER, count, width)] * LAYER
+    outs = pl.pallas_call(
         attention_kernel,
-        out_shape=[
-            jax.ShapeDtypeStruct((EXPERTS, sources * CAP, width), jnp.bfloat16),
-            jax.ShapeDtypeStruct((sources, count, width), jnp.bfloat16),
-        ],
+        out_shape=[jax.ShapeDtypeStruct(shape, jnp.bfloat16) for shape in shapes],
         in_specs=[SMEM, VMEM, VMEM],
-        out_specs=[VMEM] * 2,
+        out_specs=[VMEM] * len(shapes),
         scratch_shapes=[
             pltpu.VMEM(by_frame + (triple,), jnp.bfloat16),
             pltpu.VMEM(by_frame + (width,), jnp.float32),
             pltpu.VMEM((sources * CODE_ROWS, count), jnp.float32),
         ],
-        compiler_params=pltpu.CompilerParams(vmem_limit_bytes=24 * MIB),
+        compiler_params=pltpu.CompilerParams(vmem_limit_bytes=20 * MIB),
+        cost_estimate=pl.CostEstimate(flops=2**36, bytes_accessed=4 * MIB, transcendentals=0),
     )(me, codes, rows)
-
-
-def restore_kernel(me_ref, attended_ref, *outs):
-    count = attended_ref.shape[1]
-    back = frame_order(count, True)
-    for m in range(LAYER * LAYER):
-        rows = jnp.dot(back, attended_ref[me_ref[0] ^ m], preferred_element_type=jnp.float32)
-        outs[m // LAYER][m % LAYER] = rows.astype(jnp.bfloat16)
-
-
-def restore(me, attended):
-    block = (LAYER,) + attended.shape[1:]
-    return pl.pallas_call(
-        restore_kernel,
-        out_shape=[jax.ShapeDtypeStruct(block, attended.dtype)] * LAYER,
-        in_specs=[SMEM, VMEM],
-        out_specs=[VMEM] * LAYER,
-        compiler_params=pltpu.CompilerParams(vmem_limit_bytes=16 * MIB),
-        cost_estimate=pl.CostEstimate(flops=2**35, bytes_accessed=MIB, transcendentals=0),
-    )(me, attended)
+    return outs[:LAYER], outs[LAYER:]
 
 
 def normalize(resid, scales_ref):
@@ -248,26 +238,36 @@
     return normed.astype(jnp.bfloat16)
 
 
-def expert_kernel(
-    block, arrived_ref, hidden_ref, scales_ref, first_hbm, second_hbm, out_ref,
-    rows, total, first, second, first_done, second_done,
-):
-    blocks = first_hbm.shape[1] // block
-    depth = first.shape[0]
-
-    def fetch_first(step):
+def stage_kernel(first_hbm, after_ref, first_out, done):
+    del after_ref
+    copy = pltpu.make_async_copy(first_hbm.at[:, pl.ds(0, first_out.shape[1])], first_out, done)
+    copy.start()
+    copy.wait()
+
+
+def stage(first, columns, after):
+    return pl.pallas_call(
+        stage_kernel,
+        out_shape=pltpu.VMEM((first.shape[0], columns), first.dtype),
+        in_specs=[HBM, VMEM],
+        out_specs=VMEM,
+        scratch_shapes=[pltpu.SemaphoreType.DMA],
+        compiler_params=pltpu.CompilerParams(vmem_limit_bytes=4 * MIB),
+        cost_estimate=pl.CostEstimate(flops=0, bytes_accessed=4 * first.shape[0] * columns, transcendentals=0),
+    )(far(first), after)
+
+
+def expert_kernel(block, arrived_ref, hidden_ref, scales_ref, first_ref, second_hbm, out_ref, rows, total, ring, done):
+    blocks = first_ref.shape[1] // block
+    depth = ring.shape[0]
+
+    def fetch(step):
         place = lax.rem(step, depth)
-        start = pl.multiple_of(step * block, block)
-        return pltpu.make_async_copy(first_hbm.at[:, pl.ds(start, block)], first.at[place], first_done.at[place])
-
-    def fetch_second(step):
-        place = lax.rem(step, depth)
-        start = pl.multiple_of(step * block, block)
-        return pltpu.make_async_copy(second_hbm.at[pl.ds(start, block)], second.at[place], second_done.at[place])
+        part = pl.ds(pl.multiple_of(step * block, block), block)
+        return pltpu.make_async_copy(second_hbm.at[part], ring.at[place], done.at[place])
 
     for step in range(min(depth, blocks)):
-        fetch_first(step).start()
-        fetch_second(step).start()
+        fetch(step).start()
     total[...] = jnp.zeros_like(total)
     heads, count, lanes = arrived_ref.shape
     parts = []
@@ -279,21 +279,15 @@
     rows[...] = normalize(jnp.concatenate(parts, axis=1), scales_ref)
 
     def work(step, _):
-        place = lax.rem(step, depth)
-        fetch_first(step).wait()
-        inner = jnp.dot(rows[...], first[place], preferred_element_type=jnp.float32)
+        columns = pl.ds(pl.multiple_of(step * block, block), block)
+        inner = jnp.dot(rows[...], first_ref[:, columns], preferred_element_type=jnp.float32)
         inner = jax.nn.gelu(inner, approximate=True).astype(jnp.bfloat16)
+        fetch(step).wait()
+        total[...] += jnp.dot(inner, ring[lax.rem(step, depth)], preferred_element_type=jnp.float32)
 
         @pl.when(step + depth < blocks)
         def _():
-            fetch_first(step + depth).start()
-
-        fetch_second(step).wait()
-        total[...] += jnp.dot(inner, second[place], preferred_element_type=jnp.float32)
-
-        @pl.when(step + depth < blocks)
-        def _():
-            fetch_second(step + depth).start()
+            fetch(step + depth).start()
 
         return 0
 
@@ -309,21 +303,19 @@
     return pl.pallas_call(
         functools.partial(expert_kernel, block),
         out_shape=jax.ShapeDtypeStruct((count, width), jnp.bfloat16),
-        in_specs=[VMEM] * 3 + [HBM, HBM],
+        in_specs=[VMEM] * 4 + [HBM],
         out_specs=VMEM,
         scratch_shapes=[
             pltpu.VMEM((count, width), jnp.bfloat16),
             pltpu.VMEM((count, width), jnp.float32),
-            pltpu.VMEM((depth, width, block), jnp.bfloat16),
             pltpu.VMEM((depth, block, width), jnp.bfloat16),
             pltpu.SemaphoreType.DMA((depth,)),
-            pltpu.SemaphoreType.DMA((depth,)),
         ],
-        compiler_params=pltpu.CompilerParams(vmem_limit_bytes=44 * MIB),
+        compiler_params=pltpu.CompilerParams(vmem_limit_bytes=22 * MIB),
         cost_estimate=pl.CostEstimate(
-            flops=64 * count * width * hidden, bytes_accessed=4 * width * hidden, transcendentals=count * hidden
+            flops=64 * count * width * hidden, bytes_accessed=2 * width * hidden, transcendentals=count * hidden
         ),
-    )(arrived, hidden_rows, held(scales), far(first), far(second))
+    )(held(arrived), held(hidden_rows), held(scales), held(first), far(second))
 
 
 def residual_kernel(me_ref, *refs):
@@ -382,13 +374,13 @@
     return [stay] + [partner(block, r + 1) for r, block in enumerate(blocks)]
 
 
-def across_layers(stay, *blocks):
-    return [stay] + [partner(block, LAYER * (i + 1)) for i, block in enumerate(blocks)]
+def across_layers(*blocks):
+    return [partner(block, LAYER * (i + 1)) for i, block in enumerate(blocks)]
 
 
 def gather_codes(code):
     layer = jnp.stack(within_layer(*[code] * LAYER))
-    return jnp.stack(across_layers(*[layer] * LAYER))
+    return jnp.stack([layer] + across_layers(*[layer] * (LAYER - 1)))
 
 
 def direct_body(hidden_in, qkv, modulation, route_weight, expert_ids, slots, w_in, w_out):
@@ -405,16 +397,19 @@
     near, *away = by_layer(*here)
     near, *away, owned = lax.optimization_barrier((partner(near, LAYER), *away, owned))
     away = [near, partner(away[0], 2 * LAYER), partner(away[1], 3 * LAYER)]
-    to_experts, attended = attention(me, codes, owned)
-    arrived = exchange(to_experts)
-    hidden_rows, attended = lax.optimization_barrier((assemble(me, here, away), attended))
-    stay, *away = restore(me, attended)
-    *away, arrived = lax.optimization_barrier((*away, arrived))
-    away = across_layers(stay, *away)
-    computed = expert(arrived, hidden_rows, scales, w_in, w_out)
-    *away, computed = lax.optimization_barrier((*away, computed))
+    slot_blocks, (stay, *places) = attention(me, codes, owned)
+    slots_here = within_layer(*slot_blocks)
+    slots_away = by_layer(*slots_here)
+    staged = stage(w_in, w_in.shape[1], slots_away[0])
+    slots_away = across_layers(*slots_away)
+    hidden_rows = assemble(me, here, away)
+    arrived = assemble(me, slots_here, slots_away)
+    *places, arrived = lax.optimization_barrier((*places, arrived))
+    places = across_layers(*places)
+    computed = expert(arrived, hidden_rows, scales, staged, w_out)
+    *places, computed = lax.optimization_barrier((*places, computed))
     brought = exchange(computed.reshape(devices, CAP, -1))
-    resid = residual(me, within_layer(*by_place(*away)), hidden_in[0], scales)
+    resid = residual(me, within_layer(*by_place(stay, *places)), hidden_in[0], scales)
     return combine(resid, scales, blending, brought.reshape(devices * CAP, -1))[None]
 
 

time: 116 us -> 114 us (0.983)
  starting transfers between devices: 40.7 us -> 36.8 us
  Pallas kernels: 28.2 us -> 30.7 us
    all_to_all x3 -> x2, waiting for transfers between devices: 15.7 us -> 1.4 us  [exchange(): return lax.all_to_all(array, 'seq', split_axis=0, concat_axis=0, tiled=True)]
    ppermute x18 -> x24, waiting for transfers between devices: 29 us -> 42.5 us  [partner(): return lax.ppermute(array, 'seq', [(i, i ^ step) for i in range(devices)])]
    pallas_call x2, Pallas kernels: 3.01 us -> 12.6 us  [the longest x1 10.6 us: stage(): pl.pallas_call(stage_kernel, out_shape=pltpu.VMEM((first.shape[0], column...]
    pallas_call x1, Pallas kernels: 22.2 us -> 15 us  [expert(): pl.pallas_call(functools.partial(expert_kernel, block), out_shape=jax.Sha...]
    all_to_all x3 -> x2, starting transfers between devices: 16.7 us -> 11.2 us  [exchange(): return lax.all_to_all(array, 'seq', split_axis=0, concat_axis=0, tiled=True)]
    ppermute x18 -> x24, starting transfers between devices: 24 us -> 25.6 us  [partner(): return lax.ppermute(array, 'seq', [(i, i ^ step) for i in range(devices)])]
  transfers between devices with their start and end apart: 21 -> 26, of which waited for: 10 -> 10; matrix products, arithmetic and copies ran while one was open for 0% -> 0% of each run, Pallas kernels for 23% -> 24%
where the time goes in v6:
time: 114 us
  waiting for transfers between devices  43.9 us (39%)
  starting transfers between devices  36.8 us (32%)
  Pallas kernels  30.7 us (27%)
  local copies, waits for them, and re-layouts  2.03 us (2%)
    ppermute x24, waiting for transfers between devices, partner(): return lax.ppermute(array, 'seq', [(i, i ^ step) for i in range(devices)])  42.5 us
    ppermute x24, starting transfers between devices, partner(): return lax.ppermute(array, 'seq', [(i, i ^ step) for i in range(devices)])  25.6 us
    pallas_call x1, Pallas kernels, expert(): pl.pallas_call(functools.partial(expert_kernel, block), out_shape=jax.Sha...  15 us
    all_to_all x2, starting transfers between devices, exchange(): return lax.all_to_all(array, 'seq', split_axis=0, concat_axis=0, tiled=True)  11.2 us
    pallas_call x1, Pallas kernels, stage(): pl.pallas_call(stage_kernel, out_shape=pltpu.VMEM((first.shape[0], column...  10.6 us
  transfers between devices with their start and end apart: 26, of which 10 were waited for; matrix products, arithmetic and copies ran while one was open for 0% of the time, Pallas kernels for 24%

profile of v6, /device:TPU:0, one launch (start us, length us, event | category | flops | bytes accessed | tf_op | source)
XLA Modules:
  0.0 113.6 jit_solution(914963380314124810)
XLA Ops:
  0.0 7.4 %all-to-all-start = ((bf16[16,128,384]{2,1,0:T(8,128)(2,1)}), bf16[16,128,384]{2,1,0:T(8,128)(2,1)S(1)}, u32[]{:S(2)}, u32[]{:S(2)}) async-start(bf16[16,128,384]{2,1,0:T(8,128)(2,1)} %bitcast.33), calls=%async_computation | async-start | bytes 3145728 | tf_op jit(solution)/shard_map/all_to_all | solution.py:32
  11.2 1.7 %collective-permute-start.7 = (bf16[4,128,128]{2,1,0:T(8,128)(2,1)S(1)}, bf16[4,128,128]{2,1,0:T(8,128)(2,1)S(1)}, u32[]{:S(2)}, u32[]{:S(2)}) collective-permute-start(bf16[4,128,128]{2,1,0:T(8,128)(2,1)S(1)} %get-tuple-element.43), channel_id=1, source_target_pairs={{0,2},{1,3},{2,0},{3,1},{4,6},{5,7},{6,4},{7,5},{8,10},{9,11},{10,... | collective-permute-start | bytes 393224 | tf_op jit(solution)/shard_map/ppermute | solution.py:370
  12.9 1.7 %collective-permute-start.2 = (s32[2,128]{1,0:T(2,128)S(1)}, s32[2,128]{1,0:T(2,128)S(1)}, u32[]{:S(2)}, u32[]{:S(2)}) collective-permute-start(s32[2,128]{1,0:T(2,128)S(1)} %compare_select_fusion), channel_id=1, source_target_pairs={{0,3},{1,2},{2,1},{3,0},{4,7},{5,6},{6,5},{7,4},{8,11},{9,10},{10,... | collective-permute-start | bytes 3080 | tf_op jit(solution)/shard_map/ppermute | solution.py:370
  15.0 13.1 %collective-permute-done.2 = s32[2,128]{1,0:T(2,128)S(1)} collective-permute-done((s32[2,128]{1,0:T(2,128)S(1)}, s32[2,128]{1,0:T(2,128)S(1)}, u32[]{:S(2)}, u32[]{:S(2)}) %collective-permute-start.2) | collective-permute-done | bytes 1056 | tf_op jit(solution)/shard_map/ppermute | solution.py:370
  29.4 3.9 %collective-permute-start.3 = (s32[4,2,128]{2,1,0:T(2,128)S(1)}, s32[4,2,128]{2,1,0:T(2,128)S(1)}, u32[]{:S(2)}, u32[]{:S(2)}) collective-permute-start(s32[4,2,128]{2,1,0:T(2,128)S(1)} %pad_add_fusion.1), channel_id=1, source_target_pairs={{0,4},{1,5},{2,6},{3,7},{4,0},{5,1},{6,2},{7,3},{8,12},{9,13},{10,... | collective-permute-start | bytes 12296 | tf_op jit(solution)/shard_map/ppermute | solution.py:370
  34.0 11.5 %collective-permute-done.4 = s32[4,2,128]{2,1,0:T(2,128)S(1)} collective-permute-done((s32[4,2,128]{2,1,0:T(2,128)S(1)}, s32[4,2,128]{2,1,0:T(2,128)S(1)}, u32[]{:S(2)}, u32[]{:S(2)}) %collective-permute-start.4) | collective-permute-done | bytes 4128 | tf_op jit(solution)/shard_map/ppermute | solution.py:370
  45.5 2.1 %shard_map.84 = (bf16[4,128,128]{2,1,0:T(8,128)(2,1)S(1)}, bf16[4,128,128]{2,1,0:T(8,128)(2,1)S(1)}, bf16[4,128,128]{2,1,0:T(8,128)(2,1)S(1)}, bf16[4,128,128]{2...) custom-call(s32[1]{0:T(128)} %bitcast.me_ref, ...), custom_call_target="tpu_custom_call" | custom-call | flops 68719476736 | bytes 4194304 | tf_op jit(solution)/shard_map/pallas_call | solution.py:218
  47.6 1.7 %collective-permute-start.11 = (bf16[4,128,128]{2,1,0:T(8,128)(2,1)S(1)}, bf16[4,128,128]{2,1,0:T(8,128)(2,1)S(1)}, u32[]{:S(2)}, u32[]{:S(2)}) collective-permute-start(bf16[4,128,128]{2,1,0:T(8,128)(2,1)S(1)} %get-tuple-element.55), channel_id=1, source_target_pairs={{0,2},{1,3},{2,0},{3,1},{4,6},{5,7},{6,4},{7,5},{8,10},{9,11},{10,... | collective-permute-start | bytes 393224 | tf_op jit(solution)/shard_map/ppermute | solution.py:370
  49.5 1.4 %collective-permute-start.19 = (bf16[4,128,128]{2,1,0:T(8,128)(2,1)S(1)}, bf16[4,128,128]{2,1,0:T(8,128)(2,1)S(1)}, u32[]{:S(2)}, u32[]{:S(2)}) collective-permute-start(bf16[4,128,128]{2,1,0:T(8,128)(2,1)S(1)} %get-tuple-element.65), channel_id=1, source_target_pairs={{0,8},{1,9},{2,10},{3,11},{4,12},{5,13},{6,14},{7,15},{8,0},{9,1},... | collective-permute-start | bytes 393224 | tf_op jit(solution)/shard_map/ppermute | solution.py:370
  50.9 1.5 %collective-permute-start.20 = (bf16[4,128,128]{2,1,0:T(8,128)(2,1)S(1)}, bf16[4,128,128]{2,1,0:T(8,128)(2,1)S(1)}, u32[]{:S(2)}, u32[]{:S(2)}) collective-permute-start(bf16[4,128,128]{2,1,0:T(8,128)(2,1)S(1)} %get-tuple-element.66), channel_id=1, source_target_pairs={{0,12},{1,13},{2,14},{3,15},{4,8},{5,9},{6,10},{7,11},{8,4},{9,5},... | collective-permute-start | bytes 393224 | tf_op jit(solution)/shard_map/ppermute | solution.py:370
  52.5 1.5 %collective-permute-done.11.refs_2_ = bf16[4,128,128]{2,1,0:T(8,128)(2,1)S(1)} collective-permute-done((bf16[4,128,128]{2,1,0:T(8,128)(2,1)S(1)}, bf16[4,128,128]{2,1,0:T(8,128)(2,1)S(1)}, u32[]{:S(2)}, u32[]{:S(2)}) %collective-permute-start.11) | collective-permute-done | bytes 131104 | tf_op jit(solution)/shard_map/ppermute | solution.py:370
  54.0 1.9 %collective-permute-done.12.refs_3_ = bf16[4,128,128]{2,1,0:T(8,128)(2,1)S(1)} collective-permute-done((bf16[4,128,128]{2,1,0:T(8,128)(2,1)S(1)}, bf16[4,128,128]{2,1,0:T(8,128)(2,1)S(1)}, u32[]{:S(2)}, u32[]{:S(2)}) %collective-permute-start.12) | collective-permute-done | bytes 131104 | tf_op jit(solution)/shard_map/ppermute | solution.py:370
  55.9 1.5 %collective-permute-start.14 = (bf16[4,128,128]{2,1,0:T(8,128)(2,1)S(1)}, bf16[4,128,128]{2,1,0:T(8,128)(2,1)S(1)}, u32[]{:S(2)}, u32[]{:S(2)}) collective-permute-start(bf16[4,128,128]{2,1,0:T(8,128)(2,1)S(1)} %get-tuple-element.58), channel_id=1, source_target_pairs={{0,8},{1,9},{2,10},{3,11},{4,12},{5,13},{6,14},{7,15},{8,0},{9,1},... | collective-permute-start | bytes 393224 | tf_op jit(solution)/shard_map/ppermute | solution.py:370
  57.4 1.5 %collective-permute-start.15 = (bf16[4,128,128]{2,1,0:T(8,128)(2,1)S(1)}, bf16[4,128,128]{2,1,0:T(8,128)(2,1)S(1)}, u32[]{:S(2)}, u32[]{:S(2)}) collective-permute-start(bf16[4,128,128]{2,1,0:T(8,128)(2,1)S(1)} %get-tuple-element.59), channel_id=1, source_target_pairs={{0,12},{1,13},{2,14},{3,15},{4,8},{5,9},{6,10},{7,11},{8,4},{9,5},... | collective-permute-start | bytes 393224 | tf_op jit(solution)/shard_map/ppermute | solution.py:370
  59.5 10.6 %shard_map.88.first_ref = bf16[2048,8192]{1,0:T(8,128)(2,1)S(1)} custom-call(bf16[2048,8192]{1,0:T(8,128)(2,1)} %first_hbm.1, bf16[4,128,128]{2,1,0:T(8,128)(2,1)S(1)} %get-tuple-element.57.after_ref), custom_call_target="tpu_custom_call" | custom-call | bytes 67108864 | tf_op jit(solution)/shard_map/pallas_call | solution.py:249
  70.1 3.0 %collective-permute-done.14.refs_5_ = bf16[4,128,128]{2,1,0:T(8,128)(2,1)S(1)} collective-permute-done((bf16[4,128,128]{2,1,0:T(8,128)(2,1)S(1)}, bf16[4,128,128]{2,1,0:T(8,128)(2,1)S(1)}, u32[]{:S(2)}, u32[]{:S(2)}) %collective-permute-start.14) | collective-permute-done | bytes 131104 | tf_op jit(solution)/shard_map/ppermute | solution.py:370
  73.2 3.3 %collective-permute-start.16 = (bf16[4,128,128]{2,1,0:T(8,128)(2,1)S(1)}, bf16[4,128,128]{2,1,0:T(8,128)(2,1)S(1)}, u32[]{:S(2)}, u32[]{:S(2)}) collective-permute-start(bf16[4,128,128]{2,1,0:T(8,128)(2,1)S(1)} %get-tuple-element.60), channel_id=1, source_target_pairs={{0,4},{1,5},{2,6},{3,7},{4,0},{5,1},{6,2},{7,3},{8,12},{9,13},{10,... | collective-permute-start | bytes 393224 | tf_op jit(solution)/shard_map/ppermute | solution.py:370
  76.7 2.3 %collective-permute-start.18 = (bf16[4,128,128]{2,1,0:T(8,128)(2,1)S(1)}, bf16[4,128,128]{2,1,0:T(8,128)(2,1)S(1)}, u32[]{:S(2)}, u32[]{:S(2)}) collective-permute-start(bf16[4,128,128]{2,1,0:T(8,128)(2,1)S(1)} %get-tuple-element.62), channel_id=1, source_target_pairs={{0,12},{1,13},{2,14},{3,15},{4,8},{5,9},{6,10},{7,11},{8,4},{9,5},... | collective-permute-start | bytes 393224 | tf_op jit(solution)/shard_map/ppermute | solution.py:370
  79.0 15.0 %shard_map.89 = bf16[128,2048]{1,0:T(8,128)(2,1)} custom-call(bf16[16,128,128]{2,1,0:T(8,128)(2,1)S(1)} %shard_map.86.arrived_ref, bf16[16,128,128]{2,1,0:T(8,128)(2,1)S(1)} %shard_map.87.hidden_ref, f32[4,2048]{1,0:T(4,128)S(1)} %get-tuple-element.67.scales_ref.refs_5_, bf16[2048,8192]{1,0:T(8,128)(2,1)S(1)} %shard_map.88.first_ref, ...), custom_call_target="tpu_custom_call" | custom-call | flops 137438953472 | bytes 33554432 | tf_op jit(solution)/shard_map/pallas_call | solution.py:303
  94.0 3.9 %all-to-all-start.1 = ((bf16[16,8,2048]{2,1,0:T(8,128)(2,1)}), bf16[16,8,2048]{2,1,0:T(8,128)(2,1)S(1)}, u32[]{:S(2)}, u32[]{:S(2)}) async-start(bf16[16,8,2048]{2,1,0:T(8,128)(2,1)} %bitcast.34), calls=%async_computation.1 | async-start | bytes 1048576 | tf_op jit(solution)/shard_map/all_to_all | solution.py:32
  98.4 1.7 %collective-permute-start.22 = (bf16[4,128,128]{2,1,0:T(8,128)(2,1)S(1)}, bf16[4,128,128]{2,1,0:T(8,128)(2,1)S(1)}, u32[]{:S(2)}, u32[]{:S(2)}) collective-permute-start(bf16[4,128,128]{2,1,0:T(8,128)(2,1)S(1)} %get-tuple-element.73), channel_id=1, source_target_pairs={{0,2},{1,3},{2,0},{3,1},{4,6},{5,7},{6,4},{7,5},{8,10},{9,11},{10,... | collective-permute-start | bytes 393224 | tf_op jit(solution)/shard_map/ppermute | solution.py:370
  100.1 8.5 %collective-permute-done.22.refs_2_ = bf16[4,128,128]{2,1,0:T(8,128)(2,1)S(1)} collective-permute-done((bf16[4,128,128]{2,1,0:T(8,128)(2,1)S(1)}, bf16[4,128,128]{2,1,0:T(8,128)(2,1)S(1)}, u32[]{:S(2)}, u32[]{:S(2)}) %collective-permute-start.22) | collective-permute-done | bytes 131104 | tf_op jit(solution)/shard_map/ppermute | solution.py:370
  108.5 2.1 %collective-permute-done.23.refs_3_ = bf16[4,128,128]{2,1,0:T(8,128)(2,1)S(1)} collective-permute-done((bf16[4,128,128]{2,1,0:T(8,128)(2,1)S(1)}, bf16[4,128,128]{2,1,0:T(8,128)(2,1)S(1)}, u32[]{:S(2)}, u32[]{:S(2)}) %collective-permute-start.23) | collective-permute-done | bytes 131104 | tf_op jit(solution)/shard_map/ppermute | solution.py:370
  110.9 1.4 %all-to-all-done.1 = bf16[16,8,2048]{2,1,0:T(8,128)(2,1)S(1)} async-done(((bf16[16,8,2048]{2,1,0:T(8,128)(2,1)}), bf16[16,8,2048]{2,1,0:T(8,128)(2,1)S(1)}, u32[]{:S(2)}, u32[]{:S(2)}) %all-to-all-start.1) | async-done | bytes 524320 | tf_op jit(solution)/shard_map/all_to_all | solution.py:32
  (51 shorter events, 9.3 us)
Async XLA Ops:
  0.0 45.5 %all-to-all-start = ((bf16[16,128,384]{2,1,0:T(8,128)(2,1)}), bf16[16,128,384]{2,1,0:T(8,128)(2,1)S(1)}, u32[]{:S(2)}, u32[]{:S(2)}) async-start(bf16[16,128,384]{2,1,0:T(8,128)(2,1)} %bitcast.33), calls=%async_computation | async-start | bytes 3145728 | tf_op jit(solution)/shard_map/all_to_all | solution.py:32
  10.8 22.5 %collective-permute-start.6 = (bf16[4,128,128]{2,1,0:T(8,128)(2,1)S(1)}, bf16[4,128,128]{2,1,0:T(8,128)(2,1)S(1)}, u32[]{:S(2)}, u32[]{:S(2)}) collective-permute-start(bf16[4,128,128]{2,1,0:T(8,128)(2,1)S(1)} %get-tuple-element.42), channel_id=1, source_target_pairs={{0,1},{1,0},{2,3},{3,2},{4,5},{5,4},{6,7},{7,6},{8,9},{9,8},{10,11... | collective-permute-start | bytes 393224 | tf_op jit(solution)/shard_map/ppermute | solution.py:370
  11.2 22.6 %collective-permute-start.7 = (bf16[4,128,128]{2,1,0:T(8,128)(2,1)S(1)}, bf16[4,128,128]{2,1,0:T(8,128)(2,1)S(1)}, u32[]{:S(2)}, u32[]{:S(2)}) collective-permute-start(bf16[4,128,128]{2,1,0:T(8,128)(2,1)S(1)} %get-tuple-element.43), channel_id=1, source_target_pairs={{0,2},{1,3},{2,0},{3,1},{4,6},{5,7},{6,4},{7,5},{8,10},{9,11},{10,... | collective-permute-start | bytes 393224 | tf_op jit(solution)/shard_map/ppermute | solution.py:370
  12.9 20.9 %collective-permute-start.8 = (bf16[4,128,128]{2,1,0:T(8,128)(2,1)S(1)}, bf16[4,128,128]{2,1,0:T(8,128)(2,1)S(1)}, u32[]{:S(2)}, u32[]{:S(2)}) collective-permute-start(bf16[4,128,128]{2,1,0:T(8,128)(2,1)S(1)} %get-tuple-element.44), channel_id=1, source_target_pairs={{0,3},{1,2},{2,1},{3,0},{4,7},{5,6},{6,5},{7,4},{8,11},{9,10},{10,... | collective-permute-start | bytes 393224 | tf_op jit(solution)/shard_map/ppermute | solution.py:370
  12.9 15.2 %collective-permute-start.2 = (s32[2,128]{1,0:T(2,128)S(1)}, s32[2,128]{1,0:T(2,128)S(1)}, u32[]{:S(2)}, u32[]{:S(2)}) collective-permute-start(s32[2,128]{1,0:T(2,128)S(1)} %compare_select_fusion), channel_id=1, source_target_pairs={{0,3},{1,2},{2,1},{3,0},{4,7},{5,6},{6,5},{7,4},{8,11},{9,10},{10,... | collective-permute-start | bytes 3080 | tf_op jit(solution)/shard_map/ppermute | solution.py:370
  14.7 14.1 %collective-permute-start.1 = (s32[2,128]{1,0:T(2,128)S(1)}, s32[2,128]{1,0:T(2,128)S(1)}, u32[]{:S(2)}, u32[]{:S(2)}) collective-permute-start(s32[2,128]{1,0:T(2,128)S(1)} %compare_select_fusion), channel_id=1, source_target_pairs={{0,2},{1,3},{2,0},{3,1},{4,6},{5,7},{6,4},{7,5},{8,10},{9,11},{10,... | collective-permute-start | bytes 3080 | tf_op jit(solution)/shard_map/ppermute | solution.py:370
  29.4 16.0 %collective-permute-start.4 = (s32[4,2,128]{2,1,0:T(2,128)S(1)}, s32[4,2,128]{2,1,0:T(2,128)S(1)}, u32[]{:S(2)}, u32[]{:S(2)}) collective-permute-start(s32[4,2,128]{2,1,0:T(2,128)S(1)} %pad_add_fusion.1), channel_id=1, source_target_pairs={{0,8},{1,9},{2,10},{3,11},{4,12},{5,13},{6,14},{7,15},{8,0},{9,1},... | collective-permute-start | bytes 12296 | tf_op jit(solution)/shard_map/ppermute | solution.py:370
  29.4 16.0 %collective-permute-start.3 = (s32[4,2,128]{2,1,0:T(2,128)S(1)}, s32[4,2,128]{2,1,0:T(2,128)S(1)}, u32[]{:S(2)}, u32[]{:S(2)}) collective-permute-start(s32[4,2,128]{2,1,0:T(2,128)S(1)} %pad_add_fusion.1), channel_id=1, source_target_pairs={{0,4},{1,5},{2,6},{3,7},{4,0},{5,1},{6,2},{7,3},{8,12},{9,13},{10,... | collective-permute-start | bytes 12296 | tf_op jit(solution)/shard_map/ppermute | solution.py:370
  33.3 12.2 %collective-permute-start.5 = (s32[4,2,128]{2,1,0:T(2,128)S(1)}, s32[4,2,128]{2,1,0:T(2,128)S(1)}, u32[]{:S(2)}, u32[]{:S(2)}) collective-permute-start(s32[4,2,128]{2,1,0:T(2,128)S(1)} %pad_add_fusion.1), channel_id=1, source_target_pairs={{0,12},{1,13},{2,14},{3,15},{4,8},{5,9},{6,10},{7,11},{8,4},{9,5},... | collective-permute-start | bytes 12296 | tf_op jit(solution)/shard_map/ppermute | solution.py:370
  33.9 11.6 %collective-permute-start.9 = (bf16[4,128,128]{2,1,0:T(8,128)(2,1)S(1)}, bf16[4,128,128]{2,1,0:T(8,128)(2,1)S(1)}, u32[]{:S(2)}, u32[]{:S(2)}) collective-permute-start(bf16[4,128,128]{2,1,0:T(8,128)(2,1)S(1)} %get-tuple-element.45), channel_id=1, source_target_pairs={{0,4},{1,5},{2,6},{3,7},{4,0},{5,1},{6,2},{7,3},{8,12},{9,13},{10,... | collective-permute-start | bytes 393224 | tf_op jit(solution)/shard_map/ppermute | solution.py:370
  47.6 4.9 %collective-permute-start.10 = (bf16[4,128,128]{2,1,0:T(8,128)(2,1)S(1)}, bf16[4,128,128]{2,1,0:T(8,128)(2,1)S(1)}, u32[]{:S(2)}, u32[]{:S(2)}) collective-permute-start(bf16[4,128,128]{2,1,0:T(8,128)(2,1)S(1)} %get-tuple-element.54), channel_id=1, source_target_pairs={{0,1},{1,0},{2,3},{3,2},{4,5},{5,4},{6,7},{7,6},{8,9},{9,8},{10,11... | collective-permute-start | bytes 393224 | tf_op jit(solution)/shard_map/ppermute | solution.py:370
  47.6 6.4 %collective-permute-start.11 = (bf16[4,128,128]{2,1,0:T(8,128)(2,1)S(1)}, bf16[4,128,128]{2,1,0:T(8,128)(2,1)S(1)}, u32[]{:S(2)}, u32[]{:S(2)}) collective-permute-start(bf16[4,128,128]{2,1,0:T(8,128)(2,1)S(1)} %get-tuple-element.55), channel_id=1, source_target_pairs={{0,2},{1,3},{2,0},{3,1},{4,6},{5,7},{6,4},{7,5},{8,10},{9,11},{10,... | collective-permute-start | bytes 393224 | tf_op jit(solution)/shard_map/ppermute | solution.py:370
  49.3 6.6 %collective-permute-start.12 = (bf16[4,128,128]{2,1,0:T(8,128)(2,1)S(1)}, bf16[4,128,128]{2,1,0:T(8,128)(2,1)S(1)}, u32[]{:S(2)}, u32[]{:S(2)}) collective-permute-start(bf16[4,128,128]{2,1,0:T(8,128)(2,1)S(1)} %get-tuple-element.56), channel_id=1, source_target_pairs={{0,3},{1,2},{2,1},{3,0},{4,7},{5,6},{6,5},{7,4},{8,11},{9,10},{10,... | collective-permute-start | bytes 393224 | tf_op jit(solution)/shard_map/ppermute | solution.py:370
  49.5 20.6 %collective-permute-start.19 = (bf16[4,128,128]{2,1,0:T(8,128)(2,1)S(1)}, bf16[4,128,128]{2,1,0:T(8,128)(2,1)S(1)}, u32[]{:S(2)}, u32[]{:S(2)}) collective-permute-start(bf16[4,128,128]{2,1,0:T(8,128)(2,1)S(1)} %get-tuple-element.65), channel_id=1, source_target_pairs={{0,8},{1,9},{2,10},{3,11},{4,12},{5,13},{6,14},{7,15},{8,0},{9,1},... | collective-permute-start | bytes 393224 | tf_op jit(solution)/shard_map/ppermute | solution.py:370
  50.9 19.1 %collective-permute-start.20 = (bf16[4,128,128]{2,1,0:T(8,128)(2,1)S(1)}, bf16[4,128,128]{2,1,0:T(8,128)(2,1)S(1)}, u32[]{:S(2)}, u32[]{:S(2)}) collective-permute-start(bf16[4,128,128]{2,1,0:T(8,128)(2,1)S(1)} %get-tuple-element.66), channel_id=1, source_target_pairs={{0,12},{1,13},{2,14},{3,15},{4,8},{5,9},{6,10},{7,11},{8,4},{9,5},... | collective-permute-start | bytes 393224 | tf_op jit(solution)/shard_map/ppermute | solution.py:370
  55.9 17.2 %collective-permute-start.14 = (bf16[4,128,128]{2,1,0:T(8,128)(2,1)S(1)}, bf16[4,128,128]{2,1,0:T(8,128)(2,1)S(1)}, u32[]{:S(2)}, u32[]{:S(2)}) collective-permute-start(bf16[4,128,128]{2,1,0:T(8,128)(2,1)S(1)} %get-tuple-element.58), channel_id=1, source_target_pairs={{0,8},{1,9},{2,10},{3,11},{4,12},{5,13},{6,14},{7,15},{8,0},{9,1},... | collective-permute-start | bytes 393224 | tf_op jit(solution)/shard_map/ppermute | solution.py:370
  57.4 15.8 %collective-permute-start.15 = (bf16[4,128,128]{2,1,0:T(8,128)(2,1)S(1)}, bf16[4,128,128]{2,1,0:T(8,128)(2,1)S(1)}, u32[]{:S(2)}, u32[]{:S(2)}) collective-permute-start(bf16[4,128,128]{2,1,0:T(8,128)(2,1)S(1)} %get-tuple-element.59), channel_id=1, source_target_pairs={{0,12},{1,13},{2,14},{3,15},{4,8},{5,9},{6,10},{7,11},{8,4},{9,5},... | collective-permute-start | bytes 393224 | tf_op jit(solution)/shard_map/ppermute | solution.py:370
  59.0 14.2 %collective-permute-start.13 = (bf16[4,128,128]{2,1,0:T(8,128)(2,1)S(1)}, bf16[4,128,128]{2,1,0:T(8,128)(2,1)S(1)}, u32[]{:S(2)}, u32[]{:S(2)}) collective-permute-start(bf16[4,128,128]{2,1,0:T(8,128)(2,1)S(1)} %get-tuple-element.57.after_ref), channel_id=1, source_target_pairs={{0,4},{1,5},{2,6},{3,7},{4,0},{5,1},{6,2},{7,3},{8,12},{9,13},{10,... | collective-permute-start | bytes 393224 | tf_op jit(solution)/shard_map/ppermute | solution.py:370
  73.2 20.7 %collective-permute-start.16 = (bf16[4,128,128]{2,1,0:T(8,128)(2,1)S(1)}, bf16[4,128,128]{2,1,0:T(8,128)(2,1)S(1)}, u32[]{:S(2)}, u32[]{:S(2)}) collective-permute-start(bf16[4,128,128]{2,1,0:T(8,128)(2,1)S(1)} %get-tuple-element.60), channel_id=1, source_target_pairs={{0,4},{1,5},{2,6},{3,7},{4,0},{5,1},{6,2},{7,3},{8,12},{9,13},{10,... | collective-permute-start | bytes 393224 | tf_op jit(solution)/shard_map/ppermute | solution.py:370
  76.5 17.4 %collective-permute-start.17 = (bf16[4,128,128]{2,1,0:T(8,128)(2,1)S(1)}, bf16[4,128,128]{2,1,0:T(8,128)(2,1)S(1)}, u32[]{:S(2)}, u32[]{:S(2)}) collective-permute-start(bf16[4,128,128]{2,1,0:T(8,128)(2,1)S(1)} %get-tuple-element.61), channel_id=1, source_target_pairs={{0,8},{1,9},{2,10},{3,11},{4,12},{5,13},{6,14},{7,15},{8,0},{9,1},... | collective-permute-start | bytes 393224 | tf_op jit(solution)/shard_map/ppermute | solution.py:370
  76.7 17.3 %collective-permute-start.18 = (bf16[4,128,128]{2,1,0:T(8,128)(2,1)S(1)}, bf16[4,128,128]{2,1,0:T(8,128)(2,1)S(1)}, u32[]{:S(2)}, u32[]{:S(2)}) collective-permute-start(bf16[4,128,128]{2,1,0:T(8,128)(2,1)S(1)} %get-tuple-element.62), channel_id=1, source_target_pairs={{0,12},{1,13},{2,14},{3,15},{4,8},{5,9},{6,10},{7,11},{8,4},{9,5},... | collective-permute-start | bytes 393224 | tf_op jit(solution)/shard_map/ppermute | solution.py:370
  94.0 18.3 %all-to-all-start.1 = ((bf16[16,8,2048]{2,1,0:T(8,128)(2,1)}), bf16[16,8,2048]{2,1,0:T(8,128)(2,1)S(1)}, u32[]{:S(2)}, u32[]{:S(2)}) async-start(bf16[16,8,2048]{2,1,0:T(8,128)(2,1)} %bitcast.34), calls=%async_computation.1 | async-start | bytes 1048576 | tf_op jit(solution)/shard_map/all_to_all | solution.py:32
  98.4 10.2 %collective-permute-start.22 = (bf16[4,128,128]{2,1,0:T(8,128)(2,1)S(1)}, bf16[4,128,128]{2,1,0:T(8,128)(2,1)S(1)}, u32[]{:S(2)}, u32[]{:S(2)}) collective-permute-start(bf16[4,128,128]{2,1,0:T(8,128)(2,1)S(1)} %get-tuple-element.73), channel_id=1, source_target_pairs={{0,2},{1,3},{2,0},{3,1},{4,6},{5,7},{6,4},{7,5},{8,10},{9,11},{10,... | collective-permute-start | bytes 393224 | tf_op jit(solution)/shard_map/ppermute | solution.py:370
  100.0 10.6 %collective-permute-start.23 = (bf16[4,128,128]{2,1,0:T(8,128)(2,1)S(1)}, bf16[4,128,128]{2,1,0:T(8,128)(2,1)S(1)}, u32[]{:S(2)}, u32[]{:S(2)}) collective-permute-start(bf16[4,128,128]{2,1,0:T(8,128)(2,1)S(1)} %get-tuple-element.74), channel_id=1, source_target_pairs={{0,3},{1,2},{2,1},{3,0},{4,7},{5,6},{6,5},{7,4},{8,11},{9,10},{10,... | collective-permute-start | bytes 393224 | tf_op jit(solution)/shard_map/ppermute | solution.py:370
  (6 other events, 37.1 us)

commit v7 on v6

--- a/solution.py
+++ b/solution.py
@@ -156,8 +156,7 @@
 
 
 def attention_kernel(me_ref, codes_ref, rows_ref, *refs):
-    *outs, framed, attended, codes = refs
-    slot_outs, place_outs = outs[:LAYER], outs[LAYER:]
+    *slot_outs, attended_out, framed, attended, codes = refs
     sources, count, triple = rows_ref.shape
     width = triple // 3
     places = count // FRAMES
@@ -195,6 +194,7 @@
             code = by_frame[s * CODE_ROWS : s * CODE_ROWS + 2]
             hit = (code[0:1] == slot) | (code[1:2] == slot)
             rows = attended[:, s * places : (s + 1) * places, :].reshape(count, width).astype(jnp.bfloat16)
+            attended_out[s] = rows
             rows = jnp.dot(
                 jnp.where(hit, 1.0, 0.0).astype(jnp.bfloat16), rows, preferred_element_type=jnp.float32
             )
@@ -202,19 +202,13 @@
         pair = jnp.concatenate(pair, axis=2).astype(jnp.bfloat16)
         for r, out in enumerate(slot_outs):
             out[:, 2 * c * CAP : 2 * (c + 1) * CAP, :] = pair[:, r]
-    back = frame_order(count, True)
-    for i, out in enumerate(place_outs):
-        for r in range(LAYER):
-            start = pl.multiple_of((me_ref[0] ^ (LAYER * i + r)) * places, places)
-            rows = attended[:, pl.ds(start, places), :].reshape(count, width).astype(jnp.bfloat16)
-            out[r] = jnp.dot(back, rows, preferred_element_type=jnp.float32).astype(jnp.bfloat16)
 
 
 def attention(me, codes, rows):
     sources, count, triple = rows.shape
     width = triple // 3
     by_frame = (FRAMES, sources * count // FRAMES)
-    shapes = [(EXPERTS // LAYER, sources * CAP, width)] * LAYER + [(sources // LAYER, count, width)] * LAYER
+    shapes = [(EXPERTS // LAYER, sources * CAP, width)] * LAYER + [(sources, count, width)]
     outs = pl.pallas_call(
         attention_kernel,
         out_shape=[jax.ShapeDtypeStruct(shape, jnp.bfloat16) for shape in shapes],
@@ -228,7 +222,27 @@
         compiler_params=pltpu.CompilerParams(vmem_limit_bytes=20 * MIB),
         cost_estimate=pl.CostEstimate(flops=2**36, bytes_accessed=4 * MIB, transcendentals=0),
     )(me, codes, rows)
-    return outs[:LAYER], outs[LAYER:]
+    return outs
+
+
+def restore_kernel(me_ref, attended_ref, *outs):
+    count = attended_ref.shape[1]
+    back = frame_order(count, True)
+    for m in range(LAYER * LAYER):
+        rows = jnp.dot(back, attended_ref[me_ref[0] ^ m], preferred_element_type=jnp.float32)
+        outs[m // LAYER][m % LAYER] = rows.astype(jnp.bfloat16)
+
+
+def restore(me, attended):
+    block = (LAYER,) + attended.shape[1:]
+    return pl.pallas_call(
+        restore_kernel,
+        out_shape=[jax.ShapeDtypeStruct(block, attended.dtype)] * LAYER,
+        in_specs=[SMEM, VMEM],
+        out_specs=[VMEM] * LAYER,
+        compiler_params=pltpu.CompilerParams(vmem_limit_bytes=16 * MIB),
+        cost_estimate=pl.CostEstimate(flops=2**24, bytes_accessed=MIB, transcendentals=0),
+    )(me, attended)
 
 
 def normalize(resid, scales_ref):
@@ -397,7 +411,8 @@
     near, *away = by_layer(*here)
     near, *away, owned = lax.optimization_barrier((partner(near, LAYER), *away, owned))
     away = [near, partner(away[0], 2 * LAYER), partner(away[1], 3 * LAYER)]
-    slot_blocks, (stay, *places) = attention(me, codes, owned)
+    *slot_blocks, attended = attention(me, codes, owned)
+    stay, *places = restore(me, attended)
     slots_here = within_layer(*slot_blocks)
     slots_away = by_layer(*slots_here)
     staged = stage(w_in, w_in.shape[1], slots_away[0])

time: 114 us -> 114 us (level)
  no operation moved by 1% of the time
where the time goes in v7:
time: 114 us; the launch traced here: 113 us
  waiting for transfers between devices  43.6 us (38%)
  starting transfers between devices  36.8 us (32%)
  Pallas kernels  30.8 us (27%)
  local copies, waits for them, and re-layouts  2.03 us (2%)
    ppermute x24, waiting for transfers between devices, partner(): return lax.ppermute(array, 'seq', [(i, i ^ step) for i in range(devices)])  42.2 us
    ppermute x24, starting transfers between devices, partner(): return lax.ppermute(array, 'seq', [(i, i ^ step) for i in range(devices)])  25.6 us
    pallas_call x1, Pallas kernels, expert(): pl.pallas_call(functools.partial(expert_kernel, block), out_shape=jax.Sha...  14.9 us
    all_to_all x2, starting transfers between devices, exchange(): return lax.all_to_all(array, 'seq', split_axis=0, concat_axis=0, tiled=True)  11.2 us
    pallas_call x1, Pallas kernels, stage(): pl.pallas_call(stage_kernel, out_shape=pltpu.VMEM((first.shape[0], column...  10.6 us
  transfers between devices with their start and end apart: 26, of which 10 were waited for; matrix products, arithmetic and copies ran while one was open for 0% of the time, Pallas kernels for 24%

profile of v7, /device:TPU:0, one launch (start us, length us, event | category | flops | bytes accessed | tf_op | source)
XLA Modules:
  0.0 113.4 jit_solution(17459089105107307356)
XLA Ops:
  0.0 7.4 %all-to-all-start = ((bf16[16,128,384]{2,1,0:T(8,128)(2,1)}), bf16[16,128,384]{2,1,0:T(8,128)(2,1)S(1)}, u32[]{:S(2)}, u32[]{:S(2)}) async-start(bf16[16,128,384]{2,1,0:T(8,128)(2,1)} %bitcast.33), calls=%async_computation | async-start | bytes 3145728 | tf_op jit(solution)/shard_map/all_to_all | solution.py:32
  11.2 1.7 %collective-permute-start.7 = (bf16[4,128,128]{2,1,0:T(8,128)(2,1)S(1)}, bf16[4,128,128]{2,1,0:T(8,128)(2,1)S(1)}, u32[]{:S(2)}, u32[]{:S(2)}) collective-permute-start(bf16[4,128,128]{2,1,0:T(8,128)(2,1)S(1)} %get-tuple-element.44), channel_id=1, source_target_pairs={{0,2},{1,3},{2,0},{3,1},{4,6},{5,7},{6,4},{7,5},{8,10},{9,11},{10,... | collective-permute-start | bytes 393224 | tf_op jit(solution)/shard_map/ppermute | solution.py:384
  12.9 1.7 %collective-permute-start.2 = (s32[2,128]{1,0:T(2,128)S(1)}, s32[2,128]{1,0:T(2,128)S(1)}, u32[]{:S(2)}, u32[]{:S(2)}) collective-permute-start(s32[2,128]{1,0:T(2,128)S(1)} %compare_select_fusion), channel_id=1, source_target_pairs={{0,3},{1,2},{2,1},{3,0},{4,7},{5,6},{6,5},{7,4},{8,11},{9,10},{10,... | collective-permute-start | bytes 3080 | tf_op jit(solution)/shard_map/ppermute | solution.py:384
  15.0 13.1 %collective-permute-done.2 = s32[2,128]{1,0:T(2,128)S(1)} collective-permute-done((s32[2,128]{1,0:T(2,128)S(1)}, s32[2,128]{1,0:T(2,128)S(1)}, u32[]{:S(2)}, u32[]{:S(2)}) %collective-permute-start.2) | collective-permute-done | bytes 1056 | tf_op jit(solution)/shard_map/ppermute | solution.py:384
  29.4 3.9 %collective-permute-start.3 = (s32[4,2,128]{2,1,0:T(2,128)S(1)}, s32[4,2,128]{2,1,0:T(2,128)S(1)}, u32[]{:S(2)}, u32[]{:S(2)}) collective-permute-start(s32[4,2,128]{2,1,0:T(2,128)S(1)} %pad_add_fusion.1), channel_id=1, source_target_pairs={{0,4},{1,5},{2,6},{3,7},{4,0},{5,1},{6,2},{7,3},{8,12},{9,13},{10,... | collective-permute-start | bytes 12296 | tf_op jit(solution)/shard_map/ppermute | solution.py:384
  34.0 11.5 %collective-permute-done.4 = s32[4,2,128]{2,1,0:T(2,128)S(1)} collective-permute-done((s32[4,2,128]{2,1,0:T(2,128)S(1)}, s32[4,2,128]{2,1,0:T(2,128)S(1)}, u32[]{:S(2)}, u32[]{:S(2)}) %collective-permute-start.4) | collective-permute-done | bytes 4128 | tf_op jit(solution)/shard_map/ppermute | solution.py:384
  45.5 1.9 %shard_map.84 = (bf16[4,128,128]{2,1,0:T(8,128)(2,1)S(1)}, bf16[4,128,128]{2,1,0:T(8,128)(2,1)S(1)}, bf16[4,128,128]{2,1,0:T(8,128)(2,1)S(1)}, bf16[4,128,128]{2,1,0:T(8,128)(2,1)S(1)}, bf16[16,128,128]{2,1,0:T(8,128)(2,1)S(1)}) custom-call(s32[1]{0:T(128)} %bitcast.me_ref, s32[4,4,2,128]{3,2,1,0:T(2,128)S(1)} %pad_add_fusion.codes_ref, ...), custom_call_target="tpu_custom_call" | custom-call | flops 68719476736 | bytes 4194304 | tf_op jit(solution)/shard_map/pallas_call | solution.py:212
  47.5 1.7 %collective-permute-start.11 = (bf16[4,128,128]{2,1,0:T(8,128)(2,1)S(1)}, bf16[4,128,128]{2,1,0:T(8,128)(2,1)S(1)}, u32[]{:S(2)}, u32[]{:S(2)}) collective-permute-start(bf16[4,128,128]{2,1,0:T(8,128)(2,1)S(1)} %get-tuple-element.57), channel_id=1, source_target_pairs={{0,2},{1,3},{2,0},{3,1},{4,6},{5,7},{6,4},{7,5},{8,10},{9,11},{10,... | collective-permute-start | bytes 393224 | tf_op jit(solution)/shard_map/ppermute | solution.py:384
  49.4 1.4 %collective-permute-start.19 = (bf16[4,128,128]{2,1,0:T(8,128)(2,1)S(1)}, bf16[4,128,128]{2,1,0:T(8,128)(2,1)S(1)}, u32[]{:S(2)}, u32[]{:S(2)}) collective-permute-start(bf16[4,128,128]{2,1,0:T(8,128)(2,1)S(1)} %get-tuple-element.67), channel_id=1, source_target_pairs={{0,8},{1,9},{2,10},{3,11},{4,12},{5,13},{6,14},{7,15},{8,0},{9,1},... | collective-permute-start | bytes 393224 | tf_op jit(solution)/shard_map/ppermute | solution.py:384
  50.8 1.5 %collective-permute-start.20 = (bf16[4,128,128]{2,1,0:T(8,128)(2,1)S(1)}, bf16[4,128,128]{2,1,0:T(8,128)(2,1)S(1)}, u32[]{:S(2)}, u32[]{:S(2)}) collective-permute-start(bf16[4,128,128]{2,1,0:T(8,128)(2,1)S(1)} %get-tuple-element.68), channel_id=1, source_target_pairs={{0,12},{1,13},{2,14},{3,15},{4,8},{5,9},{6,10},{7,11},{8,4},{9,5},... | collective-permute-start | bytes 393224 | tf_op jit(solution)/shard_map/ppermute | solution.py:384
  52.3 1.5 %collective-permute-done.11.refs_2_ = bf16[4,128,128]{2,1,0:T(8,128)(2,1)S(1)} collective-permute-done((bf16[4,128,128]{2,1,0:T(8,128)(2,1)S(1)}, bf16[4,128,128]{2,1,0:T(8,128)(2,1)S(1)}, u32[]{:S(2)}, u32[]{:S(2)}) %collective-permute-start.11) | collective-permute-done | bytes 131104 | tf_op jit(solution)/shard_map/ppermute | solution.py:384
  53.9 1.9 %collective-permute-done.12.refs_3_ = bf16[4,128,128]{2,1,0:T(8,128)(2,1)S(1)} collective-permute-done((bf16[4,128,128]{2,1,0:T(8,128)(2,1)S(1)}, bf16[4,128,128]{2,1,0:T(8,128)(2,1)S(1)}, u32[]{:S(2)}, u32[]{:S(2)}) %collective-permute-start.12) | collective-permute-done | bytes 131104 | tf_op jit(solution)/shard_map/ppermute | solution.py:384
  55.8 1.5 %collective-permute-start.14 = (bf16[4,128,128]{2,1,0:T(8,128)(2,1)S(1)}, bf16[4,128,128]{2,1,0:T(8,128)(2,1)S(1)}, u32[]{:S(2)}, u32[]{:S(2)}) collective-permute-start(bf16[4,128,128]{2,1,0:T(8,128)(2,1)S(1)} %get-tuple-element.60), channel_id=1, source_target_pairs={{0,8},{1,9},{2,10},{3,11},{4,12},{5,13},{6,14},{7,15},{8,0},{9,1},... | collective-permute-start | bytes 393224 | tf_op jit(solution)/shard_map/ppermute | solution.py:384
  57.3 1.5 %collective-permute-start.15 = (bf16[4,128,128]{2,1,0:T(8,128)(2,1)S(1)}, bf16[4,128,128]{2,1,0:T(8,128)(2,1)S(1)}, u32[]{:S(2)}, u32[]{:S(2)}) collective-permute-start(bf16[4,128,128]{2,1,0:T(8,128)(2,1)S(1)} %get-tuple-element.61), channel_id=1, source_target_pairs={{0,12},{1,13},{2,14},{3,15},{4,8},{5,9},{6,10},{7,11},{8,4},{9,5},... | collective-permute-start | bytes 393224 | tf_op jit(solution)/shard_map/ppermute | solution.py:384
  59.6 10.6 %shard_map.89.first_ref = bf16[2048,8192]{1,0:T(8,128)(2,1)S(1)} custom-call(bf16[2048,8192]{1,0:T(8,128)(2,1)} %first_hbm.1, bf16[4,128,128]{2,1,0:T(8,128)(2,1)S(1)} %get-tuple-element.59.after_ref), custom_call_target="tpu_custom_call" | custom-call | bytes 67108864 | tf_op jit(solution)/shard_map/pallas_call | solution.py:263
  70.3 2.7 %collective-permute-done.14.refs_5_ = bf16[4,128,128]{2,1,0:T(8,128)(2,1)S(1)} collective-permute-done((bf16[4,128,128]{2,1,0:T(8,128)(2,1)S(1)}, bf16[4,128,128]{2,1,0:T(8,128)(2,1)S(1)}, u32[]{:S(2)}, u32[]{:S(2)}) %collective-permute-start.14) | collective-permute-done | bytes 131104 | tf_op jit(solution)/shard_map/ppermute | solution.py:384
  73.1 3.3 %collective-permute-start.16 = (bf16[4,128,128]{2,1,0:T(8,128)(2,1)S(1)}, bf16[4,128,128]{2,1,0:T(8,128)(2,1)S(1)}, u32[]{:S(2)}, u32[]{:S(2)}) collective-permute-start(bf16[4,128,128]{2,1,0:T(8,128)(2,1)S(1)} %get-tuple-element.62), channel_id=1, source_target_pairs={{0,4},{1,5},{2,6},{3,7},{4,0},{5,1},{6,2},{7,3},{8,12},{9,13},{10,... | collective-permute-start | bytes 393224 | tf_op jit(solution)/shard_map/ppermute | solution.py:384
  76.6 2.3 %collective-permute-start.18 = (bf16[4,128,128]{2,1,0:T(8,128)(2,1)S(1)}, bf16[4,128,128]{2,1,0:T(8,128)(2,1)S(1)}, u32[]{:S(2)}, u32[]{:S(2)}) collective-permute-start(bf16[4,128,128]{2,1,0:T(8,128)(2,1)S(1)} %get-tuple-element.64), channel_id=1, source_target_pairs={{0,12},{1,13},{2,14},{3,15},{4,8},{5,9},{6,10},{7,11},{8,4},{9,5},... | collective-permute-start | bytes 393224 | tf_op jit(solution)/shard_map/ppermute | solution.py:384
  78.8 14.9 %shard_map.90 = bf16[128,2048]{1,0:T(8,128)(2,1)} custom-call(bf16[16,128,128]{2,1,0:T(8,128)(2,1)S(1)} %shard_map.87.arrived_ref, bf16[16,128,128]{2,1,0:T(8,128)(2,1)S(1)} %shard_map.88.hidden_ref, f32[4,2048]{1,0:T(4,128)S(1)} %get-tuple-element.69.scales_ref.refs_5_, bf16[2048,8192]{1,0:T(8,128)(2,1)S(1)} %shard_map.89.first_ref, ...), custom_call_target="tpu_custom_call" | custom-call | flops 137438953472 | bytes 33554432 | tf_op jit(solution)/shard_map/pallas_call | solution.py:317
  93.8 3.9 %all-to-all-start.1 = ((bf16[16,8,2048]{2,1,0:T(8,128)(2,1)}), bf16[16,8,2048]{2,1,0:T(8,128)(2,1)S(1)}, u32[]{:S(2)}, u32[]{:S(2)}) async-start(bf16[16,8,2048]{2,1,0:T(8,128)(2,1)} %bitcast.34), calls=%async_computation.1 | async-start | bytes 1048576 | tf_op jit(solution)/shard_map/all_to_all | solution.py:32
  98.2 1.7 %collective-permute-start.22 = (bf16[4,128,128]{2,1,0:T(8,128)(2,1)S(1)}, bf16[4,128,128]{2,1,0:T(8,128)(2,1)S(1)}, u32[]{:S(2)}, u32[]{:S(2)}) collective-permute-start(bf16[4,128,128]{2,1,0:T(8,128)(2,1)S(1)} %get-tuple-element.75), channel_id=1, source_target_pairs={{0,2},{1,3},{2,0},{3,1},{4,6},{5,7},{6,4},{7,5},{8,10},{9,11},{10,... | collective-permute-start | bytes 393224 | tf_op jit(solution)/shard_map/ppermute | solution.py:384
  99.9 8.5 %collective-permute-done.22.refs_2_ = bf16[4,128,128]{2,1,0:T(8,128)(2,1)S(1)} collective-permute-done((bf16[4,128,128]{2,1,0:T(8,128)(2,1)S(1)}, bf16[4,128,128]{2,1,0:T(8,128)(2,1)S(1)}, u32[]{:S(2)}, u32[]{:S(2)}) %collective-permute-start.22) | collective-permute-done | bytes 131104 | tf_op jit(solution)/shard_map/ppermute | solution.py:384
  108.4 2.1 %collective-permute-done.23.refs_3_ = bf16[4,128,128]{2,1,0:T(8,128)(2,1)S(1)} collective-permute-done((bf16[4,128,128]{2,1,0:T(8,128)(2,1)S(1)}, bf16[4,128,128]{2,1,0:T(8,128)(2,1)S(1)}, u32[]{:S(2)}, u32[]{:S(2)}) %collective-permute-start.23) | collective-permute-done | bytes 131104 | tf_op jit(solution)/shard_map/ppermute | solution.py:384
  110.8 1.4 %all-to-all-done.1 = bf16[16,8,2048]{2,1,0:T(8,128)(2,1)S(1)} async-done(((bf16[16,8,2048]{2,1,0:T(8,128)(2,1)}), bf16[16,8,2048]{2,1,0:T(8,128)(2,1)S(1)}, u32[]{:S(2)}, u32[]{:S(2)}) %all-to-all-start.1) | async-done | bytes 524320 | tf_op jit(solution)/shard_map/all_to_all | solution.py:32
  (52 shorter events, 9.6 us)
Async XLA Ops:
  0.0 45.5 %all-to-all-start = ((bf16[16,128,384]{2,1,0:T(8,128)(2,1)}), bf16[16,128,384]{2,1,0:T(8,128)(2,1)S(1)}, u32[]{:S(2)}, u32[]{:S(2)}) async-start(bf16[16,128,384]{2,1,0:T(8,128)(2,1)} %bitcast.33), calls=%async_computation | async-start | bytes 3145728 | tf_op jit(solution)/shard_map/all_to_all | solution.py:32
  10.8 22.5 %collective-permute-start.6 = (bf16[4,128,128]{2,1,0:T(8,128)(2,1)S(1)}, bf16[4,128,128]{2,1,0:T(8,128)(2,1)S(1)}, u32[]{:S(2)}, u32[]{:S(2)}) collective-permute-start(bf16[4,128,128]{2,1,0:T(8,128)(2,1)S(1)} %get-tuple-element.43), channel_id=1, source_target_pairs={{0,1},{1,0},{2,3},{3,2},{4,5},{5,4},{6,7},{7,6},{8,9},{9,8},{10,11... | collective-permute-start | bytes 393224 | tf_op jit(solution)/shard_map/ppermute | solution.py:384
  11.2 22.6 %collective-permute-start.7 = (bf16[4,128,128]{2,1,0:T(8,128)(2,1)S(1)}, bf16[4,128,128]{2,1,0:T(8,128)(2,1)S(1)}, u32[]{:S(2)}, u32[]{:S(2)}) collective-permute-start(bf16[4,128,128]{2,1,0:T(8,128)(2,1)S(1)} %get-tuple-element.44), channel_id=1, source_target_pairs={{0,2},{1,3},{2,0},{3,1},{4,6},{5,7},{6,4},{7,5},{8,10},{9,11},{10,... | collective-permute-start | bytes 393224 | tf_op jit(solution)/shard_map/ppermute | solution.py:384
  12.9 20.9 %collective-permute-start.8 = (bf16[4,128,128]{2,1,0:T(8,128)(2,1)S(1)}, bf16[4,128,128]{2,1,0:T(8,128)(2,1)S(1)}, u32[]{:S(2)}, u32[]{:S(2)}) collective-permute-start(bf16[4,128,128]{2,1,0:T(8,128)(2,1)S(1)} %get-tuple-element.45), channel_id=1, source_target_pairs={{0,3},{1,2},{2,1},{3,0},{4,7},{5,6},{6,5},{7,4},{8,11},{9,10},{10,... | collective-permute-start | bytes 393224 | tf_op jit(solution)/shard_map/ppermute | solution.py:384
  12.9 15.2 %collective-permute-start.2 = (s32[2,128]{1,0:T(2,128)S(1)}, s32[2,128]{1,0:T(2,128)S(1)}, u32[]{:S(2)}, u32[]{:S(2)}) collective-permute-start(s32[2,128]{1,0:T(2,128)S(1)} %compare_select_fusion), channel_id=1, source_target_pairs={{0,3},{1,2},{2,1},{3,0},{4,7},{5,6},{6,5},{7,4},{8,11},{9,10},{10,... | collective-permute-start | bytes 3080 | tf_op jit(solution)/shard_map/ppermute | solution.py:384
  14.7 14.1 %collective-permute-start.1 = (s32[2,128]{1,0:T(2,128)S(1)}, s32[2,128]{1,0:T(2,128)S(1)}, u32[]{:S(2)}, u32[]{:S(2)}) collective-permute-start(s32[2,128]{1,0:T(2,128)S(1)} %compare_select_fusion), channel_id=1, source_target_pairs={{0,2},{1,3},{2,0},{3,1},{4,6},{5,7},{6,4},{7,5},{8,10},{9,11},{10,... | collective-permute-start | bytes 3080 | tf_op jit(solution)/shard_map/ppermute | solution.py:384
  29.4 16.0 %collective-permute-start.4 = (s32[4,2,128]{2,1,0:T(2,128)S(1)}, s32[4,2,128]{2,1,0:T(2,128)S(1)}, u32[]{:S(2)}, u32[]{:S(2)}) collective-permute-start(s32[4,2,128]{2,1,0:T(2,128)S(1)} %pad_add_fusion.1), channel_id=1, source_target_pairs={{0,8},{1,9},{2,10},{3,11},{4,12},{5,13},{6,14},{7,15},{8,0},{9,1},... | collective-permute-start | bytes 12296 | tf_op jit(solution)/shard_map/ppermute | solution.py:384
  29.4 16.0 %collective-permute-start.3 = (s32[4,2,128]{2,1,0:T(2,128)S(1)}, s32[4,2,128]{2,1,0:T(2,128)S(1)}, u32[]{:S(2)}, u32[]{:S(2)}) collective-permute-start(s32[4,2,128]{2,1,0:T(2,128)S(1)} %pad_add_fusion.1), channel_id=1, source_target_pairs={{0,4},{1,5},{2,6},{3,7},{4,0},{5,1},{6,2},{7,3},{8,12},{9,13},{10,... | collective-permute-start | bytes 12296 | tf_op jit(solution)/shard_map/ppermute | solution.py:384
  33.3 12.2 %collective-permute-start.5 = (s32[4,2,128]{2,1,0:T(2,128)S(1)}, s32[4,2,128]{2,1,0:T(2,128)S(1)}, u32[]{:S(2)}, u32[]{:S(2)}) collective-permute-start(s32[4,2,128]{2,1,0:T(2,128)S(1)} %pad_add_fusion.1), channel_id=1, source_target_pairs={{0,12},{1,13},{2,14},{3,15},{4,8},{5,9},{6,10},{7,11},{8,4},{9,5},... | collective-permute-start | bytes 12296 | tf_op jit(solution)/shard_map/ppermute | solution.py:384
  33.9 11.6 %collective-permute-start.9 = (bf16[4,128,128]{2,1,0:T(8,128)(2,1)S(1)}, bf16[4,128,128]{2,1,0:T(8,128)(2,1)S(1)}, u32[]{:S(2)}, u32[]{:S(2)}) collective-permute-start(bf16[4,128,128]{2,1,0:T(8,128)(2,1)S(1)} %get-tuple-element.46), channel_id=1, source_target_pairs={{0,4},{1,5},{2,6},{3,7},{4,0},{5,1},{6,2},{7,3},{8,12},{9,13},{10,... | collective-permute-start | bytes 393224 | tf_op jit(solution)/shard_map/ppermute | solution.py:384
  47.4 4.9 %collective-permute-start.10 = (bf16[4,128,128]{2,1,0:T(8,128)(2,1)S(1)}, bf16[4,128,128]{2,1,0:T(8,128)(2,1)S(1)}, u32[]{:S(2)}, u32[]{:S(2)}) collective-permute-start(bf16[4,128,128]{2,1,0:T(8,128)(2,1)S(1)} %get-tuple-element.56), channel_id=1, source_target_pairs={{0,1},{1,0},{2,3},{3,2},{4,5},{5,4},{6,7},{7,6},{8,9},{9,8},{10,11... | collective-permute-start | bytes 393224 | tf_op jit(solution)/shard_map/ppermute | solution.py:384
  47.5 6.4 %collective-permute-start.11 = (bf16[4,128,128]{2,1,0:T(8,128)(2,1)S(1)}, bf16[4,128,128]{2,1,0:T(8,128)(2,1)S(1)}, u32[]{:S(2)}, u32[]{:S(2)}) collective-permute-start(bf16[4,128,128]{2,1,0:T(8,128)(2,1)S(1)} %get-tuple-element.57), channel_id=1, source_target_pairs={{0,2},{1,3},{2,0},{3,1},{4,6},{5,7},{6,4},{7,5},{8,10},{9,11},{10,... | collective-permute-start | bytes 393224 | tf_op jit(solution)/shard_map/ppermute | solution.py:384
  49.2 6.6 %collective-permute-start.12 = (bf16[4,128,128]{2,1,0:T(8,128)(2,1)S(1)}, bf16[4,128,128]{2,1,0:T(8,128)(2,1)S(1)}, u32[]{:S(2)}, u32[]{:S(2)}) collective-permute-start(bf16[4,128,128]{2,1,0:T(8,128)(2,1)S(1)} %get-tuple-element.58), channel_id=1, source_target_pairs={{0,3},{1,2},{2,1},{3,0},{4,7},{5,6},{6,5},{7,4},{8,11},{9,10},{10,... | collective-permute-start | bytes 393224 | tf_op jit(solution)/shard_map/ppermute | solution.py:384
  49.4 20.9 %collective-permute-start.19 = (bf16[4,128,128]{2,1,0:T(8,128)(2,1)S(1)}, bf16[4,128,128]{2,1,0:T(8,128)(2,1)S(1)}, u32[]{:S(2)}, u32[]{:S(2)}) collective-permute-start(bf16[4,128,128]{2,1,0:T(8,128)(2,1)S(1)} %get-tuple-element.67), channel_id=1, source_target_pairs={{0,8},{1,9},{2,10},{3,11},{4,12},{5,13},{6,14},{7,15},{8,0},{9,1},... | collective-permute-start | bytes 393224 | tf_op jit(solution)/shard_map/ppermute | solution.py:384
  50.8 19.4 %collective-permute-start.20 = (bf16[4,128,128]{2,1,0:T(8,128)(2,1)S(1)}, bf16[4,128,128]{2,1,0:T(8,128)(2,1)S(1)}, u32[]{:S(2)}, u32[]{:S(2)}) collective-permute-start(bf16[4,128,128]{2,1,0:T(8,128)(2,1)S(1)} %get-tuple-element.68), channel_id=1, source_target_pairs={{0,12},{1,13},{2,14},{3,15},{4,8},{5,9},{6,10},{7,11},{8,4},{9,5},... | collective-permute-start | bytes 393224 | tf_op jit(solution)/shard_map/ppermute | solution.py:384
  55.8 17.2 %collective-permute-start.14 = (bf16[4,128,128]{2,1,0:T(8,128)(2,1)S(1)}, bf16[4,128,128]{2,1,0:T(8,128)(2,1)S(1)}, u32[]{:S(2)}, u32[]{:S(2)}) collective-permute-start(bf16[4,128,128]{2,1,0:T(8,128)(2,1)S(1)} %get-tuple-element.60), channel_id=1, source_target_pairs={{0,8},{1,9},{2,10},{3,11},{4,12},{5,13},{6,14},{7,15},{8,0},{9,1},... | collective-permute-start | bytes 393224 | tf_op jit(solution)/shard_map/ppermute | solution.py:384
  57.3 15.7 %collective-permute-start.15 = (bf16[4,128,128]{2,1,0:T(8,128)(2,1)S(1)}, bf16[4,128,128]{2,1,0:T(8,128)(2,1)S(1)}, u32[]{:S(2)}, u32[]{:S(2)}) collective-permute-start(bf16[4,128,128]{2,1,0:T(8,128)(2,1)S(1)} %get-tuple-element.61), channel_id=1, source_target_pairs={{0,12},{1,13},{2,14},{3,15},{4,8},{5,9},{6,10},{7,11},{8,4},{9,5},... | collective-permute-start | bytes 393224 | tf_op jit(solution)/shard_map/ppermute | solution.py:384
  58.8 14.2 %collective-permute-start.13 = (bf16[4,128,128]{2,1,0:T(8,128)(2,1)S(1)}, bf16[4,128,128]{2,1,0:T(8,128)(2,1)S(1)}, u32[]{:S(2)}, u32[]{:S(2)}) collective-permute-start(bf16[4,128,128]{2,1,0:T(8,128)(2,1)S(1)} %get-tuple-element.59.after_ref), channel_id=1, source_target_pairs={{0,4},{1,5},{2,6},{3,7},{4,0},{5,1},{6,2},{7,3},{8,12},{9,13},{10,... | collective-permute-start | bytes 393224 | tf_op jit(solution)/shard_map/ppermute | solution.py:384
  73.1 20.7 %collective-permute-start.16 = (bf16[4,128,128]{2,1,0:T(8,128)(2,1)S(1)}, bf16[4,128,128]{2,1,0:T(8,128)(2,1)S(1)}, u32[]{:S(2)}, u32[]{:S(2)}) collective-permute-start(bf16[4,128,128]{2,1,0:T(8,128)(2,1)S(1)} %get-tuple-element.62), channel_id=1, source_target_pairs={{0,4},{1,5},{2,6},{3,7},{4,0},{5,1},{6,2},{7,3},{8,12},{9,13},{10,... | collective-permute-start | bytes 393224 | tf_op jit(solution)/shard_map/ppermute | solution.py:384
  76.4 17.4 %collective-permute-start.17 = (bf16[4,128,128]{2,1,0:T(8,128)(2,1)S(1)}, bf16[4,128,128]{2,1,0:T(8,128)(2,1)S(1)}, u32[]{:S(2)}, u32[]{:S(2)}) collective-permute-start(bf16[4,128,128]{2,1,0:T(8,128)(2,1)S(1)} %get-tuple-element.63), channel_id=1, source_target_pairs={{0,8},{1,9},{2,10},{3,11},{4,12},{5,13},{6,14},{7,15},{8,0},{9,1},... | collective-permute-start | bytes 393224 | tf_op jit(solution)/shard_map/ppermute | solution.py:384
  76.6 17.2 %collective-permute-start.18 = (bf16[4,128,128]{2,1,0:T(8,128)(2,1)S(1)}, bf16[4,128,128]{2,1,0:T(8,128)(2,1)S(1)}, u32[]{:S(2)}, u32[]{:S(2)}) collective-permute-start(bf16[4,128,128]{2,1,0:T(8,128)(2,1)S(1)} %get-tuple-element.64), channel_id=1, source_target_pairs={{0,12},{1,13},{2,14},{3,15},{4,8},{5,9},{6,10},{7,11},{8,4},{9,5},... | collective-permute-start | bytes 393224 | tf_op jit(solution)/shard_map/ppermute | solution.py:384
  93.8 18.3 %all-to-all-start.1 = ((bf16[16,8,2048]{2,1,0:T(8,128)(2,1)}), bf16[16,8,2048]{2,1,0:T(8,128)(2,1)S(1)}, u32[]{:S(2)}, u32[]{:S(2)}) async-start(bf16[16,8,2048]{2,1,0:T(8,128)(2,1)} %bitcast.34), calls=%async_computation.1 | async-start | bytes 1048576 | tf_op jit(solution)/shard_map/all_to_all | solution.py:32
  98.2 10.2 %collective-permute-start.22 = (bf16[4,128,128]{2,1,0:T(8,128)(2,1)S(1)}, bf16[4,128,128]{2,1,0:T(8,128)(2,1)S(1)}, u32[]{:S(2)}, u32[]{:S(2)}) collective-permute-start(bf16[4,128,128]{2,1,0:T(8,128)(2,1)S(1)} %get-tuple-element.75), channel_id=1, source_target_pairs={{0,2},{1,3},{2,0},{3,1},{4,6},{5,7},{6,4},{7,5},{8,10},{9,11},{10,... | collective-permute-start | bytes 393224 | tf_op jit(solution)/shard_map/ppermute | solution.py:384
  99.9 10.6 %collective-permute-start.23 = (bf16[4,128,128]{2,1,0:T(8,128)(2,1)S(1)}, bf16[4,128,128]{2,1,0:T(8,128)(2,1)S(1)}, u32[]{:S(2)}, u32[]{:S(2)}) collective-permute-start(bf16[4,128,128]{2,1,0:T(8,128)(2,1)S(1)} %get-tuple-element.76), channel_id=1, source_target_pairs={{0,3},{1,2},{2,1},{3,0},{4,7},{5,6},{6,5},{7,4},{8,11},{9,10},{10,... | collective-permute-start | bytes 393224 | tf_op jit(solution)/shard_map/ppermute | solution.py:384
  (6 other events, 37.1 us)

commit v8 on v7

--- a/solution.py
+++ b/solution.py
@@ -312,8 +312,8 @@
 def expert(arrived, hidden_rows, scales, first, second):
     width, hidden = first.shape
     count = arrived.shape[0] * CAP
-    block = math.gcd(hidden, 1024)
-    depth = min(hidden // block, 3)
+    block = math.gcd(hidden, 2048)
+    depth = min(hidden // block, 2)
     return pl.pallas_call(
         functools.partial(expert_kernel, block),
         out_shape=jax.ShapeDtypeStruct((count, width), jnp.bfloat16),

time: 114 us -> 113 us (level)
  no operation moved by 1% of the time
where the time goes in v8:
time: 113 us
  waiting for transfers between devices  43.6 us (39%)
  starting transfers between devices  36.8 us (33%)
  Pallas kernels  30 us (27%)
  local copies, waits for them, and re-layouts  2.03 us (2%)
    ppermute x24, waiting for transfers between devices, partner(): return lax.ppermute(array, 'seq', [(i, i ^ step) for i in range(devices)])  42.2 us
    ppermute x24, starting transfers between devices, partner(): return lax.ppermute(array, 'seq', [(i, i ^ step) for i in range(devices)])  25.6 us
    pallas_call x1, Pallas kernels, expert(): pl.pallas_call(functools.partial(expert_kernel, block), out_shape=jax.Sha...  14.2 us
    all_to_all x2, starting transfers between devices, exchange(): return lax.all_to_all(array, 'seq', split_axis=0, concat_axis=0, tiled=True)  11.2 us
    pallas_call x1, Pallas kernels, stage(): pl.pallas_call(stage_kernel, out_shape=pltpu.VMEM((first.shape[0], column...  10.6 us
  transfers between devices with their start and end apart: 26, of which 10 were waited for; matrix products, arithmetic and copies ran while one was open for 0% of the time, Pallas kernels for 24%

profile of v8, /device:TPU:0, one launch (start us, length us, event | category | flops | bytes accessed | tf_op | source)
XLA Modules:
  0.0 112.6 jit_solution(15656168613330259846)
XLA Ops:
  0.0 7.4 %all-to-all-start = ((bf16[16,128,384]{2,1,0:T(8,128)(2,1)}), bf16[16,128,384]{2,1,0:T(8,128)(2,1)S(1)}, u32[]{:S(2)}, u32[]{:S(2)}) async-start(bf16[16,128,384]{2,1,0:T(8,128)(2,1)} %bitcast.33), calls=%async_computation | async-start | bytes 3145728 | tf_op jit(solution)/shard_map/all_to_all | solution.py:32
  11.2 1.7 %collective-permute-start.7 = (bf16[4,128,128]{2,1,0:T(8,128)(2,1)S(1)}, bf16[4,128,128]{2,1,0:T(8,128)(2,1)S(1)}, u32[]{:S(2)}, u32[]{:S(2)}) collective-permute-start(bf16[4,128,128]{2,1,0:T(8,128)(2,1)S(1)} %get-tuple-element.44), channel_id=1, source_target_pairs={{0,2},{1,3},{2,0},{3,1},{4,6},{5,7},{6,4},{7,5},{8,10},{9,11},{10,... | collective-permute-start | bytes 393224 | tf_op jit(solution)/shard_map/ppermute | solution.py:384
  12.9 1.7 %collective-permute-start.2 = (s32[2,128]{1,0:T(2,128)S(1)}, s32[2,128]{1,0:T(2,128)S(1)}, u32[]{:S(2)}, u32[]{:S(2)}) collective-permute-start(s32[2,128]{1,0:T(2,128)S(1)} %compare_select_fusion), channel_id=1, source_target_pairs={{0,3},{1,2},{2,1},{3,0},{4,7},{5,6},{6,5},{7,4},{8,11},{9,10},{10,... | collective-permute-start | bytes 3080 | tf_op jit(solution)/shard_map/ppermute | solution.py:384
  15.0 13.1 %collective-permute-done.2 = s32[2,128]{1,0:T(2,128)S(1)} collective-permute-done((s32[2,128]{1,0:T(2,128)S(1)}, s32[2,128]{1,0:T(2,128)S(1)}, u32[]{:S(2)}, u32[]{:S(2)}) %collective-permute-start.2) | collective-permute-done | bytes 1056 | tf_op jit(solution)/shard_map/ppermute | solution.py:384
  29.4 3.9 %collective-permute-start.3 = (s32[4,2,128]{2,1,0:T(2,128)S(1)}, s32[4,2,128]{2,1,0:T(2,128)S(1)}, u32[]{:S(2)}, u32[]{:S(2)}) collective-permute-start(s32[4,2,128]{2,1,0:T(2,128)S(1)} %pad_add_fusion.1), channel_id=1, source_target_pairs={{0,4},{1,5},{2,6},{3,7},{4,0},{5,1},{6,2},{7,3},{8,12},{9,13},{10,... | collective-permute-start | bytes 12296 | tf_op jit(solution)/shard_map/ppermute | solution.py:384
  34.0 11.5 %collective-permute-done.4 = s32[4,2,128]{2,1,0:T(2,128)S(1)} collective-permute-done((s32[4,2,128]{2,1,0:T(2,128)S(1)}, s32[4,2,128]{2,1,0:T(2,128)S(1)}, u32[]{:S(2)}, u32[]{:S(2)}) %collective-permute-start.4) | collective-permute-done | bytes 4128 | tf_op jit(solution)/shard_map/ppermute | solution.py:384
  45.5 1.9 %shard_map.84 = (bf16[4,128,128]{2,1,0:T(8,128)(2,1)S(1)}, bf16[4,128,128]{2,1,0:T(8,128)(2,1)S(1)}, bf16[4,128,128]{2,1,0:T(8,128)(2,1)S(1)}, bf16[4,128,128]{2,1,0:T(8,128)(2,1)S(1)}, bf16[16,128,128]{2,1,0:T(8,128)(2,1)S(1)}) custom-call(s32[1]{0:T(128)} %bitcast.me_ref, s32[4,4,2,128]{3,2,1,0:T(2,128)S(1)} %pad_add_fusion.codes_ref, ...), custom_call_target="tpu_custom_call" | custom-call | flops 68719476736 | bytes 4194304 | tf_op jit(solution)/shard_map/pallas_call | solution.py:212
  47.5 1.7 %collective-permute-start.11 = (bf16[4,128,128]{2,1,0:T(8,128)(2,1)S(1)}, bf16[4,128,128]{2,1,0:T(8,128)(2,1)S(1)}, u32[]{:S(2)}, u32[]{:S(2)}) collective-permute-start(bf16[4,128,128]{2,1,0:T(8,128)(2,1)S(1)} %get-tuple-element.57), channel_id=1, source_target_pairs={{0,2},{1,3},{2,0},{3,1},{4,6},{5,7},{6,4},{7,5},{8,10},{9,11},{10,... | collective-permute-start | bytes 393224 | tf_op jit(solution)/shard_map/ppermute | solution.py:384
  49.4 1.4 %collective-permute-start.19 = (bf16[4,128,128]{2,1,0:T(8,128)(2,1)S(1)}, bf16[4,128,128]{2,1,0:T(8,128)(2,1)S(1)}, u32[]{:S(2)}, u32[]{:S(2)}) collective-permute-start(bf16[4,128,128]{2,1,0:T(8,128)(2,1)S(1)} %get-tuple-element.67), channel_id=1, source_target_pairs={{0,8},{1,9},{2,10},{3,11},{4,12},{5,13},{6,14},{7,15},{8,0},{9,1},... | collective-permute-start | bytes 393224 | tf_op jit(solution)/shard_map/ppermute | solution.py:384
  50.8 1.5 %collective-permute-start.20 = (bf16[4,128,128]{2,1,0:T(8,128)(2,1)S(1)}, bf16[4,128,128]{2,1,0:T(8,128)(2,1)S(1)}, u32[]{:S(2)}, u32[]{:S(2)}) collective-permute-start(bf16[4,128,128]{2,1,0:T(8,128)(2,1)S(1)} %get-tuple-element.68), channel_id=1, source_target_pairs={{0,12},{1,13},{2,14},{3,15},{4,8},{5,9},{6,10},{7,11},{8,4},{9,5},... | collective-permute-start | bytes 393224 | tf_op jit(solution)/shard_map/ppermute | solution.py:384
  52.3 1.5 %collective-permute-done.11.refs_2_ = bf16[4,128,128]{2,1,0:T(8,128)(2,1)S(1)} collective-permute-done((bf16[4,128,128]{2,1,0:T(8,128)(2,1)S(1)}, bf16[4,128,128]{2,1,0:T(8,128)(2,1)S(1)}, u32[]{:S(2)}, u32[]{:S(2)}) %collective-permute-start.11) | collective-permute-done | bytes 131104 | tf_op jit(solution)/shard_map/ppermute | solution.py:384
  53.9 1.9 %collective-permute-done.12.refs_3_ = bf16[4,128,128]{2,1,0:T(8,128)(2,1)S(1)} collective-permute-done((bf16[4,128,128]{2,1,0:T(8,128)(2,1)S(1)}, bf16[4,128,128]{2,1,0:T(8,128)(2,1)S(1)}, u32[]{:S(2)}, u32[]{:S(2)}) %collective-permute-start.12) | collective-permute-done | bytes 131104 | tf_op jit(solution)/shard_map/ppermute | solution.py:384
  55.8 1.5 %collective-permute-start.14 = (bf16[4,128,128]{2,1,0:T(8,128)(2,1)S(1)}, bf16[4,128,128]{2,1,0:T(8,128)(2,1)S(1)}, u32[]{:S(2)}, u32[]{:S(2)}) collective-permute-start(bf16[4,128,128]{2,1,0:T(8,128)(2,1)S(1)} %get-tuple-element.60), channel_id=1, source_target_pairs={{0,8},{1,9},{2,10},{3,11},{4,12},{5,13},{6,14},{7,15},{8,0},{9,1},... | collective-permute-start | bytes 393224 | tf_op jit(solution)/shard_map/ppermute | solution.py:384
  57.3 1.5 %collective-permute-start.15 = (bf16[4,128,128]{2,1,0:T(8,128)(2,1)S(1)}, bf16[4,128,128]{2,1,0:T(8,128)(2,1)S(1)}, u32[]{:S(2)}, u32[]{:S(2)}) collective-permute-start(bf16[4,128,128]{2,1,0:T(8,128)(2,1)S(1)} %get-tuple-element.61), channel_id=1, source_target_pairs={{0,12},{1,13},{2,14},{3,15},{4,8},{5,9},{6,10},{7,11},{8,4},{9,5},... | collective-permute-start | bytes 393224 | tf_op jit(solution)/shard_map/ppermute | solution.py:384
  59.6 10.6 %shard_map.89.first_ref = bf16[2048,8192]{1,0:T(8,128)(2,1)S(1)} custom-call(bf16[2048,8192]{1,0:T(8,128)(2,1)} %first_hbm.1, bf16[4,128,128]{2,1,0:T(8,128)(2,1)S(1)} %get-tuple-element.59.after_ref), custom_call_target="tpu_custom_call" | custom-call | bytes 67108864 | tf_op jit(solution)/shard_map/pallas_call | solution.py:263
  70.3 2.7 %collective-permute-done.14.refs_5_ = bf16[4,128,128]{2,1,0:T(8,128)(2,1)S(1)} collective-permute-done((bf16[4,128,128]{2,1,0:T(8,128)(2,1)S(1)}, bf16[4,128,128]{2,1,0:T(8,128)(2,1)S(1)}, u32[]{:S(2)}, u32[]{:S(2)}) %collective-permute-start.14) | collective-permute-done | bytes 131104 | tf_op jit(solution)/shard_map/ppermute | solution.py:384
  73.1 3.3 %collective-permute-start.16 = (bf16[4,128,128]{2,1,0:T(8,128)(2,1)S(1)}, bf16[4,128,128]{2,1,0:T(8,128)(2,1)S(1)}, u32[]{:S(2)}, u32[]{:S(2)}) collective-permute-start(bf16[4,128,128]{2,1,0:T(8,128)(2,1)S(1)} %get-tuple-element.62), channel_id=1, source_target_pairs={{0,4},{1,5},{2,6},{3,7},{4,0},{5,1},{6,2},{7,3},{8,12},{9,13},{10,... | collective-permute-start | bytes 393224 | tf_op jit(solution)/shard_map/ppermute | solution.py:384
  76.6 2.3 %collective-permute-start.18 = (bf16[4,128,128]{2,1,0:T(8,128)(2,1)S(1)}, bf16[4,128,128]{2,1,0:T(8,128)(2,1)S(1)}, u32[]{:S(2)}, u32[]{:S(2)}) collective-permute-start(bf16[4,128,128]{2,1,0:T(8,128)(2,1)S(1)} %get-tuple-element.64), channel_id=1, source_target_pairs={{0,12},{1,13},{2,14},{3,15},{4,8},{5,9},{6,10},{7,11},{8,4},{9,5},... | collective-permute-start | bytes 393224 | tf_op jit(solution)/shard_map/ppermute | solution.py:384
  78.8 14.2 %shard_map.90 = bf16[128,2048]{1,0:T(8,128)(2,1)} custom-call(bf16[16,128,128]{2,1,0:T(8,128)(2,1)S(1)} %shard_map.87.arrived_ref, bf16[16,128,128]{2,1,0:T(8,128)(2,1)S(1)} %shard_map.88.hidden_ref, f32[4,2048]{1,0:T(4,128)S(1)} %get-tuple-element.69.scales_ref.refs_5_, bf16[2048,8192]{1,0:T(8,128)(2,1)S(1)} %shard_map.89.first_ref, ...), custom_call_target="tpu_custom_call" | custom-call | flops 137438953472 | bytes 33554432 | tf_op jit(solution)/shard_map/pallas_call | solution.py:317
  93.0 3.9 %all-to-all-start.1 = ((bf16[16,8,2048]{2,1,0:T(8,128)(2,1)}), bf16[16,8,2048]{2,1,0:T(8,128)(2,1)S(1)}, u32[]{:S(2)}, u32[]{:S(2)}) async-start(bf16[16,8,2048]{2,1,0:T(8,128)(2,1)} %bitcast.34), calls=%async_computation.1 | async-start | bytes 1048576 | tf_op jit(solution)/shard_map/all_to_all | solution.py:32
  97.4 1.7 %collective-permute-start.22 = (bf16[4,128,128]{2,1,0:T(8,128)(2,1)S(1)}, bf16[4,128,128]{2,1,0:T(8,128)(2,1)S(1)}, u32[]{:S(2)}, u32[]{:S(2)}) collective-permute-start(bf16[4,128,128]{2,1,0:T(8,128)(2,1)S(1)} %get-tuple-element.75), channel_id=1, source_target_pairs={{0,2},{1,3},{2,0},{3,1},{4,6},{5,7},{6,4},{7,5},{8,10},{9,11},{10,... | collective-permute-start | bytes 393224 | tf_op jit(solution)/shard_map/ppermute | solution.py:384
  99.1 8.5 %collective-permute-done.22.refs_2_ = bf16[4,128,128]{2,1,0:T(8,128)(2,1)S(1)} collective-permute-done((bf16[4,128,128]{2,1,0:T(8,128)(2,1)S(1)}, bf16[4,128,128]{2,1,0:T(8,128)(2,1)S(1)}, u32[]{:S(2)}, u32[]{:S(2)}) %collective-permute-start.22) | collective-permute-done | bytes 131104 | tf_op jit(solution)/shard_map/ppermute | solution.py:384
  107.6 2.1 %collective-permute-done.23.refs_3_ = bf16[4,128,128]{2,1,0:T(8,128)(2,1)S(1)} collective-permute-done((bf16[4,128,128]{2,1,0:T(8,128)(2,1)S(1)}, bf16[4,128,128]{2,1,0:T(8,128)(2,1)S(1)}, u32[]{:S(2)}, u32[]{:S(2)}) %collective-permute-start.23) | collective-permute-done | bytes 131104 | tf_op jit(solution)/shard_map/ppermute | solution.py:384
  110.0 1.4 %all-to-all-done.1 = bf16[16,8,2048]{2,1,0:T(8,128)(2,1)S(1)} async-done(((bf16[16,8,2048]{2,1,0:T(8,128)(2,1)}), bf16[16,8,2048]{2,1,0:T(8,128)(2,1)S(1)}, u32[]{:S(2)}, u32[]{:S(2)}) %all-to-all-start.1) | async-done | bytes 524320 | tf_op jit(solution)/shard_map/all_to_all | solution.py:32
  (52 shorter events, 9.6 us)
Async XLA Ops:
  0.0 45.5 %all-to-all-start = ((bf16[16,128,384]{2,1,0:T(8,128)(2,1)}), bf16[16,128,384]{2,1,0:T(8,128)(2,1)S(1)}, u32[]{:S(2)}, u32[]{:S(2)}) async-start(bf16[16,128,384]{2,1,0:T(8,128)(2,1)} %bitcast.33), calls=%async_computation | async-start | bytes 3145728 | tf_op jit(solution)/shard_map/all_to_all | solution.py:32
  10.8 22.5 %collective-permute-start.6 = (bf16[4,128,128]{2,1,0:T(8,128)(2,1)S(1)}, bf16[4,128,128]{2,1,0:T(8,128)(2,1)S(1)}, u32[]{:S(2)}, u32[]{:S(2)}) collective-permute-start(bf16[4,128,128]{2,1,0:T(8,128)(2,1)S(1)} %get-tuple-element.43), channel_id=1, source_target_pairs={{0,1},{1,0},{2,3},{3,2},{4,5},{5,4},{6,7},{7,6},{8,9},{9,8},{10,11... | collective-permute-start | bytes 393224 | tf_op jit(solution)/shard_map/ppermute | solution.py:384
  11.2 22.6 %collective-permute-start.7 = (bf16[4,128,128]{2,1,0:T(8,128)(2,1)S(1)}, bf16[4,128,128]{2,1,0:T(8,128)(2,1)S(1)}, u32[]{:S(2)}, u32[]{:S(2)}) collective-permute-start(bf16[4,128,128]{2,1,0:T(8,128)(2,1)S(1)} %get-tuple-element.44), channel_id=1, source_target_pairs={{0,2},{1,3},{2,0},{3,1},{4,6},{5,7},{6,4},{7,5},{8,10},{9,11},{10,... | collective-permute-start | bytes 393224 | tf_op jit(solution)/shard_map/ppermute | solution.py:384
  12.9 20.9 %collective-permute-start.8 = (bf16[4,128,128]{2,1,0:T(8,128)(2,1)S(1)}, bf16[4,128,128]{2,1,0:T(8,128)(2,1)S(1)}, u32[]{:S(2)}, u32[]{:S(2)}) collective-permute-start(bf16[4,128,128]{2,1,0:T(8,128)(2,1)S(1)} %get-tuple-element.45), channel_id=1, source_target_pairs={{0,3},{1,2},{2,1},{3,0},{4,7},{5,6},{6,5},{7,4},{8,11},{9,10},{10,... | collective-permute-start | bytes 393224 | tf_op jit(solution)/shard_map/ppermute | solution.py:384
  12.9 15.2 %collective-permute-start.2 = (s32[2,128]{1,0:T(2,128)S(1)}, s32[2,128]{1,0:T(2,128)S(1)}, u32[]{:S(2)}, u32[]{:S(2)}) collective-permute-start(s32[2,128]{1,0:T(2,128)S(1)} %compare_select_fusion), channel_id=1, source_target_pairs={{0,3},{1,2},{2,1},{3,0},{4,7},{5,6},{6,5},{7,4},{8,11},{9,10},{10,... | collective-permute-start | bytes 3080 | tf_op jit(solution)/shard_map/ppermute | solution.py:384
  14.7 14.1 %collective-permute-start.1 = (s32[2,128]{1,0:T(2,128)S(1)}, s32[2,128]{1,0:T(2,128)S(1)}, u32[]{:S(2)}, u32[]{:S(2)}) collective-permute-start(s32[2,128]{1,0:T(2,128)S(1)} %compare_select_fusion), channel_id=1, source_target_pairs={{0,2},{1,3},{2,0},{3,1},{4,6},{5,7},{6,4},{7,5},{8,10},{9,11},{10,... | collective-permute-start | bytes 3080 | tf_op jit(solution)/shard_map/ppermute | solution.py:384
  29.4 16.0 %collective-permute-start.4 = (s32[4,2,128]{2,1,0:T(2,128)S(1)}, s32[4,2,128]{2,1,0:T(2,128)S(1)}, u32[]{:S(2)}, u32[]{:S(2)}) collective-permute-start(s32[4,2,128]{2,1,0:T(2,128)S(1)} %pad_add_fusion.1), channel_id=1, source_target_pairs={{0,8},{1,9},{2,10},{3,11},{4,12},{5,13},{6,14},{7,15},{8,0},{9,1},... | collective-permute-start | bytes 12296 | tf_op jit(solution)/shard_map/ppermute | solution.py:384
  29.4 16.0 %collective-permute-start.3 = (s32[4,2,128]{2,1,0:T(2,128)S(1)}, s32[4,2,128]{2,1,0:T(2,128)S(1)}, u32[]{:S(2)}, u32[]{:S(2)}) collective-permute-start(s32[4,2,128]{2,1,0:T(2,128)S(1)} %pad_add_fusion.1), channel_id=1, source_target_pairs={{0,4},{1,5},{2,6},{3,7},{4,0},{5,1},{6,2},{7,3},{8,12},{9,13},{10,... | collective-permute-start | bytes 12296 | tf_op jit(solution)/shard_map/ppermute | solution.py:384
  33.3 12.2 %collective-permute-start.5 = (s32[4,2,128]{2,1,0:T(2,128)S(1)}, s32[4,2,128]{2,1,0:T(2,128)S(1)}, u32[]{:S(2)}, u32[]{:S(2)}) collective-permute-start(s32[4,2,128]{2,1,0:T(2,128)S(1)} %pad_add_fusion.1), channel_id=1, source_target_pairs={{0,12},{1,13},{2,14},{3,15},{4,8},{5,9},{6,10},{7,11},{8,4},{9,5},... | collective-permute-start | bytes 12296 | tf_op jit(solution)/shard_map/ppermute | solution.py:384
  33.9 11.6 %collective-permute-start.9 = (bf16[4,128,128]{2,1,0:T(8,128)(2,1)S(1)}, bf16[4,128,128]{2,1,0:T(8,128)(2,1)S(1)}, u32[]{:S(2)}, u32[]{:S(2)}) collective-permute-start(bf16[4,128,128]{2,1,0:T(8,128)(2,1)S(1)} %get-tuple-element.46), channel_id=1, source_target_pairs={{0,4},{1,5},{2,6},{3,7},{4,0},{5,1},{6,2},{7,3},{8,12},{9,13},{10,... | collective-permute-start | bytes 393224 | tf_op jit(solution)/shard_map/ppermute | solution.py:384
  47.4 4.9 %collective-permute-start.10 = (bf16[4,128,128]{2,1,0:T(8,128)(2,1)S(1)}, bf16[4,128,128]{2,1,0:T(8,128)(2,1)S(1)}, u32[]{:S(2)}, u32[]{:S(2)}) collective-permute-start(bf16[4,128,128]{2,1,0:T(8,128)(2,1)S(1)} %get-tuple-element.56), channel_id=1, source_target_pairs={{0,1},{1,0},{2,3},{3,2},{4,5},{5,4},{6,7},{7,6},{8,9},{9,8},{10,11... | collective-permute-start | bytes 393224 | tf_op jit(solution)/shard_map/ppermute | solution.py:384
  47.5 6.4 %collective-permute-start.11 = (bf16[4,128,128]{2,1,0:T(8,128)(2,1)S(1)}, bf16[4,128,128]{2,1,0:T(8,128)(2,1)S(1)}, u32[]{:S(2)}, u32[]{:S(2)}) collective-permute-start(bf16[4,128,128]{2,1,0:T(8,128)(2,1)S(1)} %get-tuple-element.57), channel_id=1, source_target_pairs={{0,2},{1,3},{2,0},{3,1},{4,6},{5,7},{6,4},{7,5},{8,10},{9,11},{10,... | collective-permute-start | bytes 393224 | tf_op jit(solution)/shard_map/ppermute | solution.py:384
  49.2 6.6 %collective-permute-start.12 = (bf16[4,128,128]{2,1,0:T(8,128)(2,1)S(1)}, bf16[4,128,128]{2,1,0:T(8,128)(2,1)S(1)}, u32[]{:S(2)}, u32[]{:S(2)}) collective-permute-start(bf16[4,128,128]{2,1,0:T(8,128)(2,1)S(1)} %get-tuple-element.58), channel_id=1, source_target_pairs={{0,3},{1,2},{2,1},{3,0},{4,7},{5,6},{6,5},{7,4},{8,11},{9,10},{10,... | collective-permute-start | bytes 393224 | tf_op jit(solution)/shard_map/ppermute | solution.py:384
  49.4 20.9 %collective-permute-start.19 = (bf16[4,128,128]{2,1,0:T(8,128)(2,1)S(1)}, bf16[4,128,128]{2,1,0:T(8,128)(2,1)S(1)}, u32[]{:S(2)}, u32[]{:S(2)}) collective-permute-start(bf16[4,128,128]{2,1,0:T(8,128)(2,1)S(1)} %get-tuple-element.67), channel_id=1, source_target_pairs={{0,8},{1,9},{2,10},{3,11},{4,12},{5,13},{6,14},{7,15},{8,0},{9,1},... | collective-permute-start | bytes 393224 | tf_op jit(solution)/shard_map/ppermute | solution.py:384
  50.8 19.4 %collective-permute-start.20 = (bf16[4,128,128]{2,1,0:T(8,128)(2,1)S(1)}, bf16[4,128,128]{2,1,0:T(8,128)(2,1)S(1)}, u32[]{:S(2)}, u32[]{:S(2)}) collective-permute-start(bf16[4,128,128]{2,1,0:T(8,128)(2,1)S(1)} %get-tuple-element.68), channel_id=1, source_target_pairs={{0,12},{1,13},{2,14},{3,15},{4,8},{5,9},{6,10},{7,11},{8,4},{9,5},... | collective-permute-start | bytes 393224 | tf_op jit(solution)/shard_map/ppermute | solution.py:384
  55.8 17.2 %collective-permute-start.14 = (bf16[4,128,128]{2,1,0:T(8,128)(2,1)S(1)}, bf16[4,128,128]{2,1,0:T(8,128)(2,1)S(1)}, u32[]{:S(2)}, u32[]{:S(2)}) collective-permute-start(bf16[4,128,128]{2,1,0:T(8,128)(2,1)S(1)} %get-tuple-element.60), channel_id=1, source_target_pairs={{0,8},{1,9},{2,10},{3,11},{4,12},{5,13},{6,14},{7,15},{8,0},{9,1},... | collective-permute-start | bytes 393224 | tf_op jit(solution)/shard_map/ppermute | solution.py:384
  57.3 15.7 %collective-permute-start.15 = (bf16[4,128,128]{2,1,0:T(8,128)(2,1)S(1)}, bf16[4,128,128]{2,1,0:T(8,128)(2,1)S(1)}, u32[]{:S(2)}, u32[]{:S(2)}) collective-permute-start(bf16[4,128,128]{2,1,0:T(8,128)(2,1)S(1)} %get-tuple-element.61), channel_id=1, source_target_pairs={{0,12},{1,13},{2,14},{3,15},{4,8},{5,9},{6,10},{7,11},{8,4},{9,5},... | collective-permute-start | bytes 393224 | tf_op jit(solution)/shard_map/ppermute | solution.py:384
  58.8 14.2 %collective-permute-start.13 = (bf16[4,128,128]{2,1,0:T(8,128)(2,1)S(1)}, bf16[4,128,128]{2,1,0:T(8,128)(2,1)S(1)}, u32[]{:S(2)}, u32[]{:S(2)}) collective-permute-start(bf16[4,128,128]{2,1,0:T(8,128)(2,1)S(1)} %get-tuple-element.59.after_ref), channel_id=1, source_target_pairs={{0,4},{1,5},{2,6},{3,7},{4,0},{5,1},{6,2},{7,3},{8,12},{9,13},{10,... | collective-permute-start | bytes 393224 | tf_op jit(solution)/shard_map/ppermute | solution.py:384
  73.1 19.9 %collective-permute-start.16 = (bf16[4,128,128]{2,1,0:T(8,128)(2,1)S(1)}, bf16[4,128,128]{2,1,0:T(8,128)(2,1)S(1)}, u32[]{:S(2)}, u32[]{:S(2)}) collective-permute-start(bf16[4,128,128]{2,1,0:T(8,128)(2,1)S(1)} %get-tuple-element.62), channel_id=1, source_target_pairs={{0,4},{1,5},{2,6},{3,7},{4,0},{5,1},{6,2},{7,3},{8,12},{9,13},{10,... | collective-permute-start | bytes 393224 | tf_op jit(solution)/shard_map/ppermute | solution.py:384
  76.4 16.6 %collective-permute-start.17 = (bf16[4,128,128]{2,1,0:T(8,128)(2,1)S(1)}, bf16[4,128,128]{2,1,0:T(8,128)(2,1)S(1)}, u32[]{:S(2)}, u32[]{:S(2)}) collective-permute-start(bf16[4,128,128]{2,1,0:T(8,128)(2,1)S(1)} %get-tuple-element.63), channel_id=1, source_target_pairs={{0,8},{1,9},{2,10},{3,11},{4,12},{5,13},{6,14},{7,15},{8,0},{9,1},... | collective-permute-start | bytes 393224 | tf_op jit(solution)/shard_map/ppermute | solution.py:384
  76.6 16.5 %collective-permute-start.18 = (bf16[4,128,128]{2,1,0:T(8,128)(2,1)S(1)}, bf16[4,128,128]{2,1,0:T(8,128)(2,1)S(1)}, u32[]{:S(2)}, u32[]{:S(2)}) collective-permute-start(bf16[4,128,128]{2,1,0:T(8,128)(2,1)S(1)} %get-tuple-element.64), channel_id=1, source_target_pairs={{0,12},{1,13},{2,14},{3,15},{4,8},{5,9},{6,10},{7,11},{8,4},{9,5},... | collective-permute-start | bytes 393224 | tf_op jit(solution)/shard_map/ppermute | solution.py:384
  93.0 18.4 %all-to-all-start.1 = ((bf16[16,8,2048]{2,1,0:T(8,128)(2,1)}), bf16[16,8,2048]{2,1,0:T(8,128)(2,1)S(1)}, u32[]{:S(2)}, u32[]{:S(2)}) async-start(bf16[16,8,2048]{2,1,0:T(8,128)(2,1)} %bitcast.34), calls=%async_computation.1 | async-start | bytes 1048576 | tf_op jit(solution)/shard_map/all_to_all | solution.py:32
  97.4 10.2 %collective-permute-start.22 = (bf16[4,128,128]{2,1,0:T(8,128)(2,1)S(1)}, bf16[4,128,128]{2,1,0:T(8,128)(2,1)S(1)}, u32[]{:S(2)}, u32[]{:S(2)}) collective-permute-start(bf16[4,128,128]{2,1,0:T(8,128)(2,1)S(1)} %get-tuple-element.75), channel_id=1, source_target_pairs={{0,2},{1,3},{2,0},{3,1},{4,6},{5,7},{6,4},{7,5},{8,10},{9,11},{10,... | collective-permute-start | bytes 393224 | tf_op jit(solution)/shard_map/ppermute | solution.py:384
  99.1 10.6 %collective-permute-start.23 = (bf16[4,128,128]{2,1,0:T(8,128)(2,1)S(1)}, bf16[4,128,128]{2,1,0:T(8,128)(2,1)S(1)}, u32[]{:S(2)}, u32[]{:S(2)}) collective-permute-start(bf16[4,128,128]{2,1,0:T(8,128)(2,1)S(1)} %get-tuple-element.76), channel_id=1, source_target_pairs={{0,3},{1,2},{2,1},{3,0},{4,7},{5,6},{6,5},{7,4},{8,11},{9,10},{10,... | collective-permute-start | bytes 393224 | tf_op jit(solution)/shard_map/ppermute | solution.py:384
  (6 other events, 36.4 us)
